TPU v7x, 512 devices: a whole 4x4x16 slice. The times are simulated.
512 devices in a mesh: pipe: 8 (over z_hi, y), expert: 64 (over z_lo, x, core).
Axes of the slice: x: 4, y: 4, z: 16 (z_hi: 2, z_lo: 8; z = z_hi * 8 + z_lo), core: 2. Of those that a mesh axis runs over, the one named last changes fastest.
Arguments:
- forward_state: bfloat16 [8, 4096, 3584], P('pipe', 'expert'), may hold values from -6 to 6
- grad_state: bfloat16 [8, 4096, 3584], P('pipe', 'expert'), may hold values from -6 to 6
- forward_routes: int32 [8, 4096, 1], P('pipe', 'expert'), may hold values from 0 to 7; in each aligned block of 64 rows (0 to 63, 64 to 127, ..., all dimensions but the last counted through in order) at most 8 rows name the same one
- forward_gates: bfloat16 [8, 4096, 1], P('pipe', 'expert'), may hold values from 0.19921875 to 2
- backward_routes: int32 [8, 4096, 1], P('pipe', 'expert'), may hold values from 0 to 7; in each aligned block of 64 rows (0 to 63, 64 to 127, ..., all dimensions but the last counted through in order) at most 8 rows name the same one
- backward_gates: bfloat16 [8, 4096, 1], P('pipe', 'expert'), may hold values from 0.19921875 to 2
- saved_preacts: bfloat16 [8, 2, 64, 8, 8192], P('pipe', None, None, None, 'expert'), may hold values from -6 to 6
- gate_weight: bfloat16 [8, 3584, 8192], P('pipe', None, 'expert'), may hold values from -0.09375 to 0.09375
- up_weight: bfloat16 [8, 3584, 8192], P('pipe', None, 'expert'), may hold values from -0.09375 to 0.09375
- down_weight: bfloat16 [8, 8192, 3584], P('pipe', 'expert'), may hold values from -0.1875 to 0.1875
Outputs:
- forward_next: bfloat16 [8, 4096, 3584], P('pipe', 'expert')
- backward_next: bfloat16 [8, 4096, 3584], P('pipe', 'expert')
Inputs may be any that keep to these rules, and one draw needn't show every extreme that they name: `forward_routes`: in the 64 tokens of one device at one section, every expert is named by exactly 8 (token, choice) pairs; the 1 expert of a token differ. `backward_routes`: in the 64 tokens of one device at one section, every expert is named by exactly 8 (token, choice) pairs; the 1 expert of a token differ.
All inputs are finite; a program needn't handle non-finite values.
Results may differ from a plain program's by a relative error of at most 0.011.
Values may be sent and summed in bfloat16 or wider, within the bound.
No kernel may reach another device: no remote copies, remote signals or barrier semaphores. Data moves between devices by JAX's collectives and lax.ppermute only.
A program may use at most 128 MiB of HBM per device.

v0:
```python
import jax
import jax.numpy as jnp
from jax import lax
from jax.sharding import PartitionSpec as P

WSPLIT = 8


def from_behind(block, axis, distance):
    devices = range(lax.axis_size(axis))
    route = [((i - distance) % len(devices), i) for i in devices]
    return lax.ppermute(block, axis, route)


def slot_tables(routes, gate_values, expert_count, capacity):
    tokens_here, picked = routes.shape
    expert_ids = jnp.arange(expert_count, dtype=jnp.int32)
    chosen = (routes[:, :, None] == expert_ids).astype(jnp.int32)
    flat_hits = chosen.reshape(tokens_here * picked, expert_count)
    earlier = jnp.cumsum(flat_hits, axis=0) - flat_hits
    position = jnp.sum(earlier * flat_hits, axis=1).reshape(tokens_here, picked)
    slot_ids = jnp.arange(capacity, dtype=jnp.int32)
    placed = chosen[:, :, :, None] * (position[:, :, None, None] == slot_ids).astype(jnp.int32)
    table = jnp.transpose(jnp.sum(placed, axis=1), (1, 2, 0)).astype(jnp.float32)
    scaled = placed.astype(jnp.float32) * gate_values.astype(jnp.float32)[:, :, None, None]
    weighted = jnp.transpose(jnp.sum(scaled, axis=1), (1, 2, 0))
    return (table, weighted)


def replicate_blocks(packed):
    expert_count, capacity, width = packed.shape
    spread = jnp.broadcast_to(packed[:, None], (expert_count, WSPLIT, capacity, width))
    return spread.reshape(expert_count * WSPLIT, capacity, width)


def merge_blocks(returned, table, base):
    expert_count, capacity, tokens_here = table.shape
    width = base.shape[1]
    combined = jnp.sum(
        returned.reshape(expert_count, WSPLIT, capacity, width).astype(jnp.float32), axis=1
    )
    return (base.astype(jnp.float32) + jnp.einsum("ect,ecd->td", table, combined)).astype(
        jnp.bfloat16
    )


def expert_forward(slot_rows, gate_weight, up_weight, down_weight):
    pre_gate = jnp.dot(slot_rows, gate_weight, preferred_element_type=jnp.float32)
    pre_up = jnp.dot(slot_rows, up_weight, preferred_element_type=jnp.float32)
    hidden = (jax.nn.silu(pre_gate) * pre_up).astype(jnp.bfloat16)
    return jnp.dot(hidden, down_weight, preferred_element_type=jnp.float32).astype(jnp.bfloat16)


def forward_layer(activations, routes, gate_values, gate_weight, up_weight, down_weight, capacity):
    width = activations.shape[1]
    expert_count = lax.axis_size("expert") // WSPLIT
    table, weighted = slot_tables(routes, gate_values, expert_count, capacity)
    packed = jnp.einsum(
        "ect,td->ecd", table.astype(jnp.bfloat16), activations, preferred_element_type=jnp.float32
    ).astype(jnp.bfloat16)
    outgoing = replicate_blocks(packed)
    received = lax.all_to_all(outgoing, "expert", split_axis=0, concat_axis=0, tiled=True)
    partial_out = expert_forward(received.reshape(-1, width), gate_weight, up_weight, down_weight)
    returned = lax.all_to_all(
        partial_out.reshape(received.shape), "expert", split_axis=0, concat_axis=0, tiled=True
    )
    return merge_blocks(returned, weighted, activations)


def backward_layer(
    cotangent, routes, gate_values, saved, gate_weight, up_weight, down_weight, capacity
):
    width = cotangent.shape[1]
    expert_count = lax.axis_size("expert") // WSPLIT
    table, weighted = slot_tables(routes, gate_values, expert_count, capacity)
    packed = jnp.einsum(
        "ect,td->ecd", weighted.astype(jnp.bfloat16), cotangent, preferred_element_type=jnp.float32
    ).astype(jnp.bfloat16)
    received = lax.all_to_all(
        replicate_blocks(packed), "expert", split_axis=0, concat_axis=0, tiled=True
    )
    slot_rows = received.reshape(-1, width)
    contract = (((1,), (1,)), ((), ()))
    hidden_grad = lax.dot_general(
        slot_rows, down_weight, contract, preferred_element_type=jnp.float32
    )
    units = saved.shape[-1]
    pre_gate = saved[0].reshape(-1, units).astype(jnp.float32)
    pre_up = saved[1].reshape(-1, units).astype(jnp.float32)
    sig = jax.nn.sigmoid(pre_gate)
    grad_gate = (hidden_grad * pre_up * sig * (1.0 + pre_gate * (1.0 - sig))).astype(jnp.bfloat16)
    grad_up = (hidden_grad * pre_gate * sig).astype(jnp.bfloat16)
    partial_out = lax.dot_general(
        grad_gate, gate_weight, contract, preferred_element_type=jnp.float32
    ) + lax.dot_general(grad_up, up_weight, contract, preferred_element_type=jnp.float32)
    partial_out = partial_out.astype(jnp.bfloat16).reshape(received.shape)
    returned = lax.all_to_all(partial_out, "expert", split_axis=0, concat_axis=0, tiled=True)
    return merge_blocks(returned, table, cotangent)


def body(
    forward_state,
    grad_state,
    forward_routes,
    forward_gates,
    backward_routes,
    backward_gates,
    saved_preacts,
    gate_weight,
    up_weight,
    down_weight,
):
    capacity = saved_preacts.shape[3]
    weights = (gate_weight[0], up_weight[0], down_weight[0])
    result = forward_layer(
        forward_state[0],
        forward_routes[0],
        forward_gates[0],
        weights[0],
        weights[1],
        weights[2],
        capacity,
    )
    gradient = backward_layer(
        grad_state[0],
        backward_routes[0],
        backward_gates[0],
        saved_preacts[0],
        weights[0],
        weights[1],
        weights[2],
        capacity,
    )
    forward_next = from_behind(result, "pipe", 1)
    backward_next = from_behind(gradient, "pipe", -1)
    return (forward_next[None], backward_next[None])


def solution(mesh):
    return jax.shard_map(
        body,
        mesh=mesh,
        in_specs=(
            P("pipe", "expert", None),
            P("pipe", "expert", None),
            P("pipe", "expert", None),
            P("pipe", "expert", None),
            P("pipe", "expert", None),
            P("pipe", "expert", None),
            P("pipe", None, None, None, "expert"),
            P("pipe", None, "expert"),
            P("pipe", None, "expert"),
            P("pipe", "expert", None),
        ),
        out_specs=(P("pipe", "expert", None), P("pipe", "expert", None)),
        check_vma=False,
    )
```

profile of v0, /device:TPU:24, one launch (start us, length us, event | category | flops | bytes accessed | tf_op | source)
XLA Modules:
  0.0 791.6 jit_solution(8360392726569551236)
XLA Ops:
  0.6 0.8 fusion.60
  1.5 0.8 select_reduce_fusion
  2.4 0.7 fusion.74
  3.1 0.7 bitcast_convert_fusion
  3.7 1.3 convolution_convert_fusion.1
  5.0 2.0 broadcast_in_dim.10
  7.1 16.4 %all-to-all-start.2 = ((bf16[64,8,3584]{2,1,0:T(8,128)(2,1)}), bf16[64,8,3584]{2,1,0:T(8,128)(2,1)}, u32[]{:S(2)}, u32[]{:S(2)}) async-start(bf16[64,8,3584]{2,1,0:T(8,128)(2,1)} %bitcast.91), calls=%async_computation.2 | async-start | bytes 7340032 | tf_op jit(solution)/shard_map/all_to_all | solution.py:79
  23.5 0.1 reduce_window_sum.17
  23.6 0.2 select_reduce_fusion.1
  23.8 0.3 convolution_convert_fusion.2
  24.1 162.9 %all-to-all-done.2 = bf16[64,8,3584]{2,1,0:T(8,128)(2,1)} async-done(((bf16[64,8,3584]{2,1,0:T(8,128)(2,1)}), bf16[64,8,3584]{2,1,0:T(8,128)(2,1)}, u32[]{:S(2)}, u32[]{:S(2)}) %all-to-all-start.2) | async-done | bytes 3670048 | tf_op jit(solution)/shard_map/all_to_all | solution.py:79
  187.0 2.2 broadcast_in_dim.8
  189.2 8.3 %all-to-all-start = ((bf16[64,8,3584]{2,1,0:T(8,128)(2,1)}), bf16[64,8,3584]{2,1,0:T(8,128)(2,1)}, u32[]{:S(2)}, u32[]{:S(2)}) async-start(bf16[64,8,3584]{2,1,0:T(8,128)(2,1)} %bitcast.92), calls=%async_computation | async-start | bytes 7340032 | tf_op jit(solution)/shard_map/all_to_all | solution.py:62
  197.5 3.2 fusion.6
  200.8 1.1 fusion.22
  201.9 3.0 fusion.1
  204.9 156.1 %all-to-all-done = bf16[64,8,3584]{2,1,0:T(8,128)(2,1)} async-done(((bf16[64,8,3584]{2,1,0:T(8,128)(2,1)}), bf16[64,8,3584]{2,1,0:T(8,128)(2,1)}, u32[]{:S(2)}, u32[]{:S(2)}) %all-to-all-start) | async-done | bytes 3670048 | tf_op jit(solution)/shard_map/all_to_all | solution.py:62
  361.1 8.1 %all-to-all-start.3 = ((bf16[64,8,3584]{2,1,0:T(8,128)(2,1)}), bf16[64,8,3584]{2,1,0:T(8,128)(2,1)}, u32[]{:S(2)}, u32[]{:S(2)}) async-start(bf16[64,8,3584]{2,1,0:T(8,128)(2,1)} %fusion.1), calls=%async_computation.3 | async-start | bytes 7340032 | tf_op jit(solution)/shard_map/all_to_all | solution.py:97
  369.2 3.1 fusion.10
  372.4 7.9 fusion
  380.3 152.6 %all-to-all-done.3 = bf16[64,8,3584]{2,1,0:T(8,128)(2,1)} async-done(((bf16[64,8,3584]{2,1,0:T(8,128)(2,1)}), bf16[64,8,3584]{2,1,0:T(8,128)(2,1)}, u32[]{:S(2)}, u32[]{:S(2)}) %all-to-all-start.3) | async-done | bytes 3670048 | tf_op jit(solution)/shard_map/all_to_all | solution.py:97
  532.8 8.1 %all-to-all-start.1 = ((bf16[64,8,3584]{2,1,0:T(8,128)(2,1)}), bf16[64,8,3584]{2,1,0:T(8,128)(2,1)}, u32[]{:S(2)}, u32[]{:S(2)}) async-start(bf16[64,8,3584]{2,1,0:T(8,128)(2,1)} %fusion), calls=%async_computation.1 | async-start | bytes 7340032 | tf_op jit(solution)/shard_map/all_to_all | solution.py:64
  541.0 2.6 convert_reduce_fusion
  543.6 0.3 fusion.4
  543.9 2.7 collective-permute-start.1
  546.6 158.0 %all-to-all-done.1 = bf16[64,8,3584]{2,1,0:T(8,128)(2,1)} async-done(((bf16[64,8,3584]{2,1,0:T(8,128)(2,1)}), bf16[64,8,3584]{2,1,0:T(8,128)(2,1)}, u32[]{:S(2)}, u32[]{:S(2)}) %all-to-all-start.1) | async-done | bytes 3670048 | tf_op jit(solution)/shard_map/all_to_all | solution.py:64
  704.6 2.5 convert_reduce_fusion.1
  707.1 0.3 fusion.5
  707.4 47.2 %collective-permute-start = (bf16[64,3584]{1,0:T(8,128)(2,1)S(1)}, bf16[64,3584]{1,0:T(8,128)(2,1)S(1)}, u32[]{:S(2)}, u32[]{:S(2)}) collective-permute-start(bf16[64,3584]{1,0:T(8,128)(2,1)S(1)} %fusion.5), channel_id=1, source_target_pairs={{448,0},{0,64},{64,128},{128,192},{192,256},{256,320},{320,384},{3... | collective-permute-start | bytes 1376264 | tf_op jit(solution)/shard_map/ppermute | solution.py:12
  754.6 35.4 %collective-permute-done = bf16[64,3584]{1,0:T(8,128)(2,1)S(1)} collective-permute-done((bf16[64,3584]{1,0:T(8,128)(2,1)S(1)}, bf16[64,3584]{1,0:T(8,128)(2,1)S(1)}, u32[]{:S(2)}, u32[]{:S(2)}) %collective-permute-start) | collective-permute-done | bytes 458784 | tf_op jit(solution)/shard_map/ppermute | solution.py:12
  790.0 0.8 copy.28
  790.8 0.8 copy.29
  (23 shorter events, 0.2 us)
Async XLA Ops:
  0.6 201.3 %copy-start = (bf16[1,3584,128]{2,1,0:T(8,128)(2,1)S(1)}, bf16[1,3584,128]{2,1,0:T(8,128)(2,1)}, u32[]{:S(2)}) copy-start(bf16[1,3584,128]{2,1,0:T(8,128)(2,1)} %param.18) | copy-start | bytes 2752516
  7.1 16.4 %copy-start.6 = (s32[1,64,1]{1,2,0:T(1,128)S(1)}, s32[1,64,1]{1,2,0:T(1,128)}, u32[]{:S(2)}) copy-start(s32[1,64,1]{1,2,0:T(1,128)} %param.12) | copy-start | bytes 772
  7.1 16.8 %copy-start.3 = (bf16[1,64,3584]{2,1,0:T(8,128)(2,1)S(1)}, bf16[1,64,3584]{2,1,0:T(8,128)(2,1)}, u32[]{:S(2)}) copy-start(bf16[1,64,3584]{2,1,0:T(8,128)(2,1)} %param.10) | copy-start | bytes 1376260
  7.1 180.0 %all-to-all-start.2 = ((bf16[64,8,3584]{2,1,0:T(8,128)(2,1)}), bf16[64,8,3584]{2,1,0:T(8,128)(2,1)}, u32[]{:S(2)}, u32[]{:S(2)}) async-start(bf16[64,8,3584]{2,1,0:T(8,128)(2,1)} %bitcast.91), calls=%async_computation.2 | async-start | bytes 7340032 | tf_op jit(solution)/shard_map/all_to_all | solution.py:79
  189.2 8.3 %copy-start.2 = (bf16[1,128,3584]{2,1,0:T(8,128)(2,1)S(1)}, bf16[1,128,3584]{2,1,0:T(8,128)(2,1)}, u32[]{:S(2)}) copy-start(bf16[1,128,3584]{2,1,0:T(8,128)(2,1)} %param.19) | copy-start | bytes 2752516
  189.2 171.9 %all-to-all-start = ((bf16[64,8,3584]{2,1,0:T(8,128)(2,1)}), bf16[64,8,3584]{2,1,0:T(8,128)(2,1)}, u32[]{:S(2)}, u32[]{:S(2)}) async-start(bf16[64,8,3584]{2,1,0:T(8,128)(2,1)} %bitcast.92), calls=%async_computation | async-start | bytes 7340032 | tf_op jit(solution)/shard_map/all_to_all | solution.py:62
  197.5 3.3 copy-start.1
  197.5 3.3 copy-start.5
  361.1 171.7 %all-to-all-start.3 = ((bf16[64,8,3584]{2,1,0:T(8,128)(2,1)}), bf16[64,8,3584]{2,1,0:T(8,128)(2,1)}, u32[]{:S(2)}, u32[]{:S(2)}) async-start(bf16[64,8,3584]{2,1,0:T(8,128)(2,1)} %fusion.1), calls=%async_computation.3 | async-start | bytes 7340032 | tf_op jit(solution)/shard_map/all_to_all | solution.py:97
  380.3 160.7 %copy-start.7 = (bf16[1,64,1]{1,2,0:T(2,128)(2,1)S(1)}, bf16[1,64,1]{1,2,0:T(2,128)(2,1)}, u32[]{:S(2)}) copy-start(bf16[1,64,1]{1,2,0:T(2,128)(2,1)} %param.13) | copy-start | bytes 388
  532.8 171.7 %all-to-all-start.1 = ((bf16[64,8,3584]{2,1,0:T(8,128)(2,1)}), bf16[64,8,3584]{2,1,0:T(8,128)(2,1)}, u32[]{:S(2)}, u32[]{:S(2)}) async-start(bf16[64,8,3584]{2,1,0:T(8,128)(2,1)} %fusion), calls=%async_computation.1 | async-start | bytes 7340032 | tf_op jit(solution)/shard_map/all_to_all | solution.py:64
  541.0 2.6 copy-start.4
  543.9 210.7 %collective-permute-start.1 = (bf16[64,3584]{1,0:T(8,128)(2,1)S(1)}, bf16[64,3584]{1,0:T(8,128)(2,1)S(1)}, u32[]{:S(2)}, u32[]{:S(2)}) collective-permute-start(bf16[64,3584]{1,0:T(8,128)(2,1)S(1)} %fusion.4), channel_id=1, source_target_pairs={{64,0},{128,64},{192,128},{256,192},{320,256},{384,320},{448,384},... | collective-permute-start | bytes 1376264 | tf_op jit(solution)/shard_map/ppermute | solution.py:12
  707.4 82.6 %collective-permute-start = (bf16[64,3584]{1,0:T(8,128)(2,1)S(1)}, bf16[64,3584]{1,0:T(8,128)(2,1)S(1)}, u32[]{:S(2)}, u32[]{:S(2)}) collective-permute-start(bf16[64,3584]{1,0:T(8,128)(2,1)S(1)} %fusion.5), channel_id=1, source_target_pairs={{448,0},{0,64},{64,128},{128,192},{192,256},{256,320},{320,384},{3... | collective-permute-start | bytes 1376264 | tf_op jit(solution)/shard_map/ppermute | solution.py:12
where the time goes:
time: 801 us; the launch traced here: 792 us
  waiting for transfers between devices  665 us (83%)
  starting transfers between devices  90.7 us (11%)
  matrix products  20.6 us (3%)
  other arithmetic  8.55 us (1%)
    all_to_all x1, waiting for transfers between devices, backward_layer(): lax.all_to_all(replicate_blocks(packed), 'expert', split_axis=0, concat_a...  163 us
    all_to_all x1, waiting for transfers between devices, forward_layer(): lax.all_to_all(partial_out.reshape(received.shape), 'expert', split_axis=...  158 us
    all_to_all x1, waiting for transfers between devices, forward_layer(): lax.all_to_all(outgoing, 'expert', split_axis=0, concat_axis=0, tiled=True)  156 us
    all_to_all x1, waiting for transfers between devices, backward_layer(): lax.all_to_all(partial_out, 'expert', split_axis=0, concat_axis=0, tiled=...  153 us
    ppermute x2, starting transfers between devices, from_behind(): return lax.ppermute(block, axis, route)  49.8 us
    ppermute x2, waiting for transfers between devices, from_behind(): return lax.ppermute(block, axis, route)  35.4 us
    all_to_all x1, starting transfers between devices, backward_layer(): lax.all_to_all(replicate_blocks(packed), 'expert', split_axis=0, concat_a...  16.4 us
  transfers between devices with their start and end apart: 6, of which 5 were waited for; matrix products, arithmetic and copies ran while one was open for 3% of the time, Pallas kernels for 0%

commit v1 on v0

v1 whole, which is shorter than its diff:
```python
import jax
import jax.numpy as jnp
from jax import lax
from jax.sharding import Mesh, PartitionSpec as P

BF = jnp.bfloat16
F32 = jnp.float32
ROWS_T = (((1,), (1,)), ((), ()))


def shift(block, axis, distance):
    n = lax.axis_size(axis)
    return lax.ppermute(block, axis, [(i, (i + distance) % n) for i in range(n)])


def exchange(block):
    return lax.all_to_all(block, "z", split_axis=0, concat_axis=0, tiled=True)


def slot_tables(routes, gate_values, expert_count, capacity):
    tokens_here, picked = routes.shape
    expert_ids = jnp.arange(expert_count, dtype=jnp.int32)
    chosen = (routes[:, :, None] == expert_ids).astype(jnp.int32)
    flat_hits = chosen.reshape(tokens_here * picked, expert_count)
    earlier = jnp.cumsum(flat_hits, axis=0) - flat_hits
    position = jnp.sum(earlier * flat_hits, axis=1).reshape(tokens_here, picked)
    slot_ids = jnp.arange(capacity, dtype=jnp.int32)
    placed = chosen[:, :, :, None] * (position[:, :, None, None] == slot_ids).astype(jnp.int32)
    table = jnp.transpose(jnp.sum(placed, axis=1), (1, 2, 0)).astype(BF)
    scaled = placed.astype(BF) * gate_values[:, :, None, None]
    weighted = jnp.transpose(jnp.sum(scaled, axis=1), (1, 2, 0)).astype(BF)
    slots = expert_count * capacity
    return table.reshape(slots, tokens_here), weighted.reshape(slots, tokens_here)


def pack(table, rows):
    return jnp.dot(table, rows, preferred_element_type=F32).astype(BF)


def merge(returned, table, base):
    combined = lax.dot_general(
        table, returned, (((0,), (0,)), ((), ())), preferred_element_type=F32
    )
    return (base.astype(F32) + combined).astype(BF)


def forward_block(rows, gates, ups, downs):
    total = None
    for gate, up, down in zip(gates, ups, downs):
        pre_gate = jnp.dot(rows, gate, preferred_element_type=F32)
        pre_up = jnp.dot(rows, up, preferred_element_type=F32)
        hidden = (jax.nn.silu(pre_gate) * pre_up).astype(BF)
        piece = jnp.dot(hidden, down, preferred_element_type=F32)
        total = piece if total is None else total + piece
    return total


def backward_block(rows, saved, gates, ups, downs):
    total = None
    for kept, gate, up, down in zip(saved, gates, ups, downs):
        hidden_grad = lax.dot_general(rows, down, ROWS_T, preferred_element_type=F32)
        a, b = kept[0].astype(F32), kept[1].astype(F32)
        sig = jax.nn.sigmoid(a)
        grad_gate = (hidden_grad * b * sig * (1.0 + a * (1.0 - sig))).astype(BF)
        grad_up = (hidden_grad * a * sig).astype(BF)
        piece = lax.dot_general(grad_gate, gate, ROWS_T, preferred_element_type=F32)
        piece = piece + lax.dot_general(grad_up, up, ROWS_T, preferred_element_type=F32)
        total = piece if total is None else total + piece
    return total


def spread_and_sum(rows, compute):
    n = lax.axis_size("x")
    total = compute(rows, 0)
    for k in range(1, n):
        visiting = shift(rows, "x", -k)
        total = total + shift(compute(visiting, k).astype(BF), "x", k).astype(F32)
    return total.astype(BF)


def body(
    forward_state, grad_state, forward_routes, forward_gates, backward_routes, backward_gates,
    saved_preacts, gate_weight, up_weight, down_weight,
):
    x, y, saved = forward_state[0], grad_state[0], saved_preacts[0]
    width = x.shape[1]
    capacity, units = saved.shape[2], saved.shape[3]
    nz, nx, nc = lax.axis_size("z"), lax.axis_size("x"), lax.axis_size("c")
    f_table, f_weighted = slot_tables(forward_routes[0], forward_gates[0], nz, capacity)
    b_table, b_weighted = slot_tables(backward_routes[0], backward_gates[0], nz, capacity)
    f_rows = exchange(pack(f_table, x).reshape(nz, capacity, width)).reshape(-1, width)
    b_rows = exchange(pack(b_weighted, y).reshape(nz, capacity, width)).reshape(-1, width)

    gates = (gate_weight[0], shift(gate_weight[0], "c", 1))
    ups = (up_weight[0], shift(up_weight[0], "c", 1))
    downs = (down_weight[0], shift(down_weight[0], "c", 1))
    me_x, me_c = lax.axis_index("x"), lax.axis_index("c")
    by_core = saved.reshape(2, nz, nx, nc, capacity, units)
    mine = lax.dynamic_index_in_dim(by_core, me_c, 3, keepdims=False)
    theirs = shift(lax.dynamic_index_in_dim(by_core, 1 - me_c, 3, keepdims=False), "c", 1)

    def saved_of(k):
        at = lax.rem(me_x + k, nx)
        return tuple(
            lax.dynamic_index_in_dim(kept, at, 2, keepdims=False).reshape(2, nz * capacity, units)
            for kept in (mine, theirs)
        )

    f_out = spread_and_sum(f_rows, lambda rows, k: forward_block(rows, gates, ups, downs))
    b_out = spread_and_sum(
        b_rows, lambda rows, k: backward_block(rows, saved_of(k), gates, ups, downs)
    )
    f_back = exchange(f_out.reshape(nz, capacity, width)).reshape(-1, width)
    b_back = exchange(b_out.reshape(nz, capacity, width)).reshape(-1, width)
    result = merge(f_back, f_weighted, x)
    gradient = merge(b_back, b_table, y)
    ring = lax.axis_size(("h", "y"))
    forward_next = lax.ppermute(result, ("h", "y"), [(i, (i + 1) % ring) for i in range(ring)])
    backward_next = lax.ppermute(gradient, ("h", "y"), [(i, (i - 1) % ring) for i in range(ring)])
    return forward_next[None], backward_next[None]


def solution(mesh):
    pipes = mesh.shape["pipe"]
    fine = Mesh(mesh.devices.reshape(2, pipes // 2, 8, 4, 2), ("h", "y", "z", "x", "c"))
    pipe, expert = ("h", "y"), ("z", "x", "c")
    tokens = P(pipe, expert, None)
    return jax.shard_map(
        body,
        mesh=fine,
        in_specs=(
            tokens, tokens, tokens, tokens, tokens, tokens,
            P(pipe, None, None, None, expert),
            P(pipe, None, expert),
            P(pipe, None, expert),
            P(pipe, expert, None),
        ),
        out_specs=(tokens, tokens),
        check_vma=False,
    )
```

time: 801 us -> 286 us (0.36)
  the two profiles are of different devices: /device:TPU:24 before, /device:TPU:102 now
where the time goes in v1:
time: 286 us; the launch traced here: 284 us
  waiting for transfers between devices  107 us (37%)
  starting transfers between devices  99 us (35%)
  matrix products  71.9 us (25%)
  local copies, waits for them, and re-layouts  4.48 us (2%)
    all_to_all x4, waiting for transfers between devices, exchange(): return lax.all_to_all(block, 'z', split_axis=0, concat_axis=0, tiled=True)  53.8 us
    ppermute x16, starting transfers between devices, shift(): lax.ppermute(block, axis, [(i, (i + distance) % n) for i in range(n)])  45.5 us
    all_to_all x4, starting transfers between devices, exchange(): return lax.all_to_all(block, 'z', split_axis=0, concat_axis=0, tiled=True)  40.9 us
    ppermute x1, waiting for transfers between devices, body(): lax.ppermute(result, ('h', 'y'), [(i, (i + 1) % ring) for i in range(ring)])  39.2 us
    dot_general x8, matrix products, forward_block(): piece = jnp.dot(hidden, down, preferred_element_type=F32)  21.6 us
    dot_general x8, matrix products, backward_block(): piece = lax.dot_general(grad_gate, gate, ROWS_T, preferred_element_type=F32)  13.4 us
    ppermute x16, waiting for transfers between devices, shift(): lax.ppermute(block, axis, [(i, (i + distance) % n) for i in range(n)])  12.3 us
    dot_general x8, matrix products, backward_block(): lax.dot_general(rows, down, ROWS_T, preferred_element_type=F32)  11.5 us
  transfers between devices with their start and end apart: 22, of which 6 were waited for; matrix products, arithmetic and copies ran while one was open for 25% of the time, Pallas kernels for 0%

profile of v1, /device:TPU:102, one launch (start us, length us, event | category | flops | bytes accessed | tf_op | source)
XLA Modules:
  0.0 283.7 jit_solution(7646202767455520634)
XLA Ops:
  2.3 2.0 fusion.24
  4.4 11.8 %all-to-all-start.2 = ((bf16[8,8,3584]{2,1,0:T(8,128)(2,1)}), bf16[8,8,3584]{2,1,0:T(8,128)(2,1)}, u32[]{:S(2)}, u32[]{:S(2)}) async-start(bf16[8,8,3584]{2,1,0:T(8,128)(2,1)} %fusion.24), calls=%async_computation.2 | async-start | bytes 917504 | tf_op jit(solution)/shard_map/all_to_all | solution.py:17
  18.3 19.1 %all-to-all-done.2 = bf16[8,8,3584]{2,1,0:T(8,128)(2,1)} async-done(((bf16[8,8,3584]{2,1,0:T(8,128)(2,1)}), bf16[8,8,3584]{2,1,0:T(8,128)(2,1)}, u32[]{:S(2)}, u32[]{:S(2)}) %all-to-all-start.2) | async-done | bytes 458784 | tf_op jit(solution)/shard_map/all_to_all | solution.py:17
  37.4 9.1 %all-to-all-start = ((bf16[8,8,3584]{2,1,0:T(8,128)(2,1)}), bf16[8,8,3584]{2,1,0:T(8,128)(2,1)S(1)}, u32[]{:S(2)}, u32[]{:S(2)}) async-start(bf16[8,8,3584]{2,1,0:T(8,128)(2,1)} %fusion.23), calls=%async_computation | async-start | bytes 917504 | tf_op jit(solution)/shard_map/all_to_all | solution.py:17
  48.4 2.4 collective-permute-start.1
  53.5 2.4 collective-permute-start
  55.9 2.7 collective-permute-start.11
  61.5 3.0 %collective-permute-start.13 = (bf16[64,3584]{1,0:T(8,128)(2,1)}, bf16[64,3584]{1,0:T(8,128)(2,1)}, u32[]{:S(2)}, u32[]{:S(2)}) collective-permute-start(bf16[64,3584]{1,0:T(8,128)(2,1)} %bitcast.17), channel_id=1, source_target_pairs={{0,4},{2,6},{4,0},{6,2},{1,5},{3,7},{5,1},{7,3},{8,12},{10,14},{12... | collective-permute-start | bytes 1376264 | tf_op jit(solution)/shard_map/ppermute | solution.py:13
  66.0 4.0 %collective-permute-start.15 = (bf16[64,3584]{1,0:T(8,128)(2,1)}, bf16[64,3584]{1,0:T(8,128)(2,1)}, u32[]{:S(2)}, u32[]{:S(2)}) collective-permute-start(bf16[64,3584]{1,0:T(8,128)(2,1)} %bitcast.17), channel_id=1, source_target_pairs={{0,2},{2,4},{4,6},{6,0},{1,3},{3,5},{5,7},{7,1},{8,10},{10,12},{12... | collective-permute-start | bytes 1376264 | tf_op jit(solution)/shard_map/ppermute | solution.py:13
  72.0 2.7 fusion.137
  77.2 5.3 %collective-permute-done.11 = bf16[64,3584]{1,0:T(8,128)(2,1)} collective-permute-done((bf16[64,3584]{1,0:T(8,128)(2,1)}, bf16[64,3584]{1,0:T(8,128)(2,1)}, u32[]{:S(2)}, u32[]{:S(2)}) %collective-permute-start.11) | collective-permute-done | bytes 458784 | tf_op jit(solution)/shard_map/ppermute | solution.py:13
  91.8 2.5 fusion.15
  94.3 6.0 %collective-permute-start.12 = (bf16[64,3584]{1,0:T(8,128)(2,1)}, bf16[64,3584]{1,0:T(8,128)(2,1)}, u32[]{:S(2)}, u32[]{:S(2)}) collective-permute-start(bf16[64,3584]{1,0:T(8,128)(2,1)} %fusion.15), channel_id=1, source_target_pairs={{0,2},{2,4},{4,6},{6,0},{1,3},{3,5},{5,7},{7,1},{8,10},{10,12},{12... | collective-permute-start | bytes 1376264 | tf_op jit(solution)/shard_map/ppermute | solution.py:13
  105.7 2.5 fusion.16
  115.6 2.5 fusion.17
  118.0 2.8 collective-permute-start.16
  121.1 2.8 fusion.116
  125.5 2.9 %fusion.19 = bf16[64,3584]{1,0:T(8,128)(2,1)} fusion(f32[64,3584]{1,0:T(8,128)} %fusion.116, bf16[128,3584]{1,0:T(8,128)(2,1)S(1)} %collective-permute-done.2, f32[64,128]{1,0:T(8,128)S(1)} %fusion.289, bf16[64,3584]{1,0:T(8,128)(2,1)} %copy-done.4, bf16[3584,128]{1,0:T(8,128)(2,1)} %collective-permute-done.1), kind=kOutput, calls=%fused_computation.35 | convolution fusion | flops 117948416 | bytes 3702784 | tf_op jit(solution)/shard_map/dot_general | solution.py:53
  128.5 4.3 %collective-permute-start.4 = (bf16[64,3584]{1,0:T(8,128)(2,1)}, bf16[64,3584]{1,0:T(8,128)(2,1)}, u32[]{:S(2)}, u32[]{:S(2)}) collective-permute-start(bf16[64,3584]{1,0:T(8,128)(2,1)} %fusion.19), channel_id=1, source_target_pairs={{0,2},{2,4},{4,6},{6,0},{1,3},{3,5},{5,7},{7,1},{8,10},{10,12},{12... | collective-permute-start | bytes 1376264 | tf_op jit(solution)/shard_map/ppermute | solution.py:13
  134.1 2.8 fusion.117
  138.5 2.9 %fusion.20 = bf16[64,3584]{1,0:T(8,128)(2,1)} fusion(f32[64,3584]{1,0:T(8,128)} %fusion.117, bf16[128,3584]{1,0:T(8,128)(2,1)S(1)} %collective-permute-done.2, f32[64,128]{1,0:T(8,128)S(1)} %fusion.290, bf16[64,3584]{1,0:T(8,128)(2,1)} %collective-permute-done.5, bf16[3584,128]{1,0:T(8,128)(2,1)} %collective-permute-done.1), kind=kOutput, calls=%fused_computation.36 | convolution fusion | flops 117948416 | bytes 3702784 | tf_op jit(solution)/shard_map/dot_general | solution.py:53
  141.4 4.3 %collective-permute-start.6 = (bf16[64,3584]{1,0:T(8,128)(2,1)}, bf16[64,3584]{1,0:T(8,128)(2,1)}, u32[]{:S(2)}, u32[]{:S(2)}) collective-permute-start(bf16[64,3584]{1,0:T(8,128)(2,1)} %fusion.20), channel_id=1, source_target_pairs={{0,4},{2,6},{4,0},{6,2},{1,5},{3,7},{5,1},{7,3},{8,12},{10,14},{12... | collective-permute-start | bytes 1376264 | tf_op jit(solution)/shard_map/ppermute | solution.py:13
  147.1 3.2 %fusion.22 = bf16[8,8,3584]{2,1,0:T(8,128)(2,1)} fusion(f32[64,3584]{1,0:T(8,128)} %convolution_add_fusion.7, f32[64,3584]{1,0:T(8,128)S(1)} %copy-done.5, bf16[3584,128]{1,0:T(8,128)(2,1)} %collective-permute-done, bf16[64,3584]{1,0:T(8,128)(2,1)} %collective-permute-done.16, bf16[64,3584]{1,0:T(8,128)(2,1)} %collective-permute-done.14, ...), kind=kOutput, calls=%fused_computation.38 | convolution fusion | flops 60882944 | bytes 4653064 | tf_op jit(solution)/shard_map/dot_general | solution.py:66
  150.3 9.9 %all-to-all-start.3 = ((bf16[8,8,3584]{2,1,0:T(8,128)(2,1)}), bf16[8,8,3584]{2,1,0:T(8,128)(2,1)}, u32[]{:S(2)}, u32[]{:S(2)}) async-start(bf16[8,8,3584]{2,1,0:T(8,128)(2,1)} %fusion.22), calls=%async_computation.3 | async-start | bytes 917504 | tf_op jit(solution)/shard_map/all_to_all | solution.py:17
  162.0 2.5 fusion.118
  164.4 2.9 %fusion.21 = bf16[64,3584]{1,0:T(8,128)(2,1)} fusion(f32[64,3584]{1,0:T(8,128)} %fusion.118, bf16[128,3584]{1,0:T(8,128)(2,1)S(1)} %collective-permute-done.2, f32[64,128]{1,0:T(8,128)S(1)} %fusion.291, bf16[64,3584]{1,0:T(8,128)(2,1)} %collective-permute-done.7, bf16[3584,128]{1,0:T(8,128)(2,1)} %collective-permute-done.1), kind=kOutput, calls=%fused_computation.37 | convolution fusion | flops 117948416 | bytes 3702784 | tf_op jit(solution)/shard_map/dot_general | solution.py:53
  172.4 7.0 %collective-permute-done.8 = bf16[64,3584]{1,0:T(8,128)(2,1)} collective-permute-done((bf16[64,3584]{1,0:T(8,128)(2,1)}, bf16[64,3584]{1,0:T(8,128)(2,1)}, u32[]{:S(2)}, u32[]{:S(2)}) %collective-permute-start.8) | collective-permute-done | bytes 458784 | tf_op jit(solution)/shard_map/ppermute | solution.py:13
  179.4 3.3 %fusion.25 = bf16[8,8,3584]{2,1,0:T(8,128)(2,1)} fusion(f32[64,3584]{1,0:T(8,128)} %fusion.27, bf16[128,3584]{1,0:T(8,128)(2,1)S(1)} %collective-permute-done.2, bf16[64,3584]{1,0:T(8,128)(2,1)} %collective-permute-done.8, bf16[64,3584]{1,0:T(8,128)(2,1)} %collective-permute-done.6, bf16[64,3584]{1,0:T(8,128)(2,1)} %collective-permute-done.4, ...), kind=kOutput, calls=%fused_computation.41 | convolution fusion | flops 119324672 | bytes 5079040 | tf_op jit(solution)/shard_map/dot_general | solution.py:53
  182.7 10.0 %all-to-all-start.1 = ((bf16[8,8,3584]{2,1,0:T(8,128)(2,1)}), bf16[8,8,3584]{2,1,0:T(8,128)(2,1)S(1)}, u32[]{:S(2)}, u32[]{:S(2)}) async-start(bf16[8,8,3584]{2,1,0:T(8,128)(2,1)} %fusion.25), calls=%async_computation.1 | async-start | bytes 917504 | tf_op jit(solution)/shard_map/all_to_all | solution.py:17
  194.1 10.7 %collective-permute-start.17 = (bf16[64,3584]{1,0:T(8,128)(2,1)S(1)}, bf16[64,3584]{1,0:T(8,128)(2,1)S(1)}, u32[]{:S(2)}, u32[]{:S(2)}) collective-permute-start(bf16[64,3584]{1,0:T(8,128)(2,1)S(1)} %fusion.12), channel_id=1, source_target_pairs={{0,448},{64,0},{128,64},{192,128},{256,192},{320,256},{384,320},{4... | collective-permute-start | bytes 1376264 | tf_op jit(solution)/shard_map/ppermute | solution.py:119
  204.8 34.7 %all-to-all-done.1 = bf16[8,8,3584]{2,1,0:T(8,128)(2,1)S(1)} async-done(((bf16[8,8,3584]{2,1,0:T(8,128)(2,1)}), bf16[8,8,3584]{2,1,0:T(8,128)(2,1)S(1)}, u32[]{:S(2)}, u32[]{:S(2)}) %all-to-all-start.1) | async-done | bytes 458784 | tf_op jit(solution)/shard_map/all_to_all | solution.py:17
  243.0 39.2 %collective-permute-done.9 = bf16[64,3584]{1,0:T(8,128)(2,1)S(1)} collective-permute-done((bf16[64,3584]{1,0:T(8,128)(2,1)S(1)}, bf16[64,3584]{1,0:T(8,128)(2,1)S(1)}, u32[]{:S(2)}, u32[]{:S(2)}) %collective-permute-start.9) | collective-permute-done | bytes 458784 | tf_op jit(solution)/shard_map/ppermute | solution.py:118
  (99 shorter events, 58.4 us)
Async XLA Ops:
  4.4 12.9 %copy-start.7 = (bf16[1,64,3584]{2,1,0:T(8,128)(2,1)S(1)}, bf16[1,64,3584]{2,1,0:T(8,128)(2,1)}, u32[]{:S(2)}) copy-start(bf16[1,64,3584]{2,1,0:T(8,128)(2,1)} %param.10) | copy-start | bytes 1376260
  4.4 46.5 %copy-start.10 = (bf16[1,2,64,8,128]{4,3,2,1,0:T(8,128)(2,1)S(1)}, bf16[1,2,64,8,128]{4,3,2,1,0:T(8,128)(2,1)}, u32[]{:S(2)}) copy-start(bf16[1,2,64,8,128]{4,3,2,1,0:T(8,128)(2,1)} %param.16) | copy-start | bytes 786436
  4.4 33.1 %all-to-all-start.2 = ((bf16[8,8,3584]{2,1,0:T(8,128)(2,1)}), bf16[8,8,3584]{2,1,0:T(8,128)(2,1)}, u32[]{:S(2)}, u32[]{:S(2)}) async-start(bf16[8,8,3584]{2,1,0:T(8,128)(2,1)} %fusion.24), calls=%async_computation.2 | async-start | bytes 917504 | tf_op jit(solution)/shard_map/all_to_all | solution.py:17
  17.2 29.3 %copy-start.1 = (bf16[1,128,3584]{2,1,0:T(8,128)(2,1)S(1)}, bf16[1,128,3584]{2,1,0:T(8,128)(2,1)}, u32[]{:S(2)}) copy-start(bf16[1,128,3584]{2,1,0:T(8,128)(2,1)} %param.19) | copy-start | bytes 2752516
  17.2 36.2 %copy-start = (bf16[1,3584,128]{2,1,0:T(8,128)(2,1)S(1)}, bf16[1,3584,128]{2,1,0:T(8,128)(2,1)}, u32[]{:S(2)}) copy-start(bf16[1,3584,128]{2,1,0:T(8,128)(2,1)} %param.17) | copy-start | bytes 2752516
  37.4 32.6 %all-to-all-start = ((bf16[8,8,3584]{2,1,0:T(8,128)(2,1)}), bf16[8,8,3584]{2,1,0:T(8,128)(2,1)S(1)}, u32[]{:S(2)}, u32[]{:S(2)}) async-start(bf16[8,8,3584]{2,1,0:T(8,128)(2,1)} %fusion.23), calls=%async_computation | async-start | bytes 917504 | tf_op jit(solution)/shard_map/all_to_all | solution.py:17
  46.5 15.0 %collective-permute-start.2 = (bf16[128,3584]{1,0:T(8,128)(2,1)S(1)}, bf16[128,3584]{1,0:T(8,128)(2,1)S(1)}, u32[]{:S(2)}, u32[]{:S(2)}) collective-permute-start(bf16[128,3584]{1,0:T(8,128)(2,1)S(1)} %bitcast.311), channel_id=1, source_target_pairs={{0,1},{1,0},{2,3},{3,2},{4,5},{5,4},{6,7},{7,6},{8,9},{9,8},{10,11... | collective-permute-start | bytes 2752520 | tf_op jit(solution)/shard_map/ppermute | solution.py:13
  48.4 21.6 %collective-permute-start.1 = (bf16[3584,128]{1,0:T(8,128)(2,1)}, bf16[3584,128]{1,0:T(8,128)(2,1)}, u32[]{:S(2)}, u32[]{:S(2)}) collective-permute-start(bf16[3584,128]{1,0:T(8,128)(2,1)} %bitcast.312), channel_id=1, source_target_pairs={{0,1},{1,0},{2,3},{3,2},{4,5},{5,4},{6,7},{7,6},{8,9},{9,8},{10,11... | collective-permute-start | bytes 2752520 | tf_op jit(solution)/shard_map/ppermute | solution.py:13
  51.5 14.4 %collective-permute-start.10 = (bf16[2,8,4,8,128]{4,3,1,2,0:T(8,128)(2,1)}, bf16[2,8,4,8,128]{4,3,1,2,0:T(8,128)(2,1)}, u32[]{:S(2)}, u32[]{:S(2)}) collective-permute-start(bf16[2,8,4,8,128]{4,3,1,2,0:T(8,128)(2,1)} %copy_bitcast_fusion), channel_id=1, source_target_pairs={{0,1},{1,0},{2,3},{3,2},{4,5},{5,4},{6,7},{7,6},{8,9},{9,8},{10,11... | collective-permute-start | bytes 393224 | tf_op jit(solution)/shard_map/ppermute | solution.py:13
  53.5 36.4 %collective-permute-start = (bf16[3584,128]{1,0:T(8,128)(2,1)S(1)}, bf16[3584,128]{1,0:T(8,128)(2,1)}, u32[]{:S(2)}, u32[]{:S(2)}) collective-permute-start(bf16[3584,128]{1,0:T(8,128)(2,1)S(1)} %bitcast.310), channel_id=1, source_target_pairs={{0,1},{1,0},{2,3},{3,2},{4,5},{5,4},{6,7},{7,6},{8,9},{9,8},{10,11... | collective-permute-start | bytes 2752520 | tf_op jit(solution)/shard_map/ppermute | solution.py:13
  55.9 26.6 %collective-permute-start.11 = (bf16[64,3584]{1,0:T(8,128)(2,1)}, bf16[64,3584]{1,0:T(8,128)(2,1)}, u32[]{:S(2)}, u32[]{:S(2)}) collective-permute-start(bf16[64,3584]{1,0:T(8,128)(2,1)} %bitcast.17), channel_id=1, source_target_pairs={{0,6},{2,0},{4,2},{6,4},{1,7},{3,1},{5,3},{7,5},{8,14},{10,8},{12,... | collective-permute-start | bytes 1376264 | tf_op jit(solution)/shard_map/ppermute | solution.py:13
  61.5 32.8 %collective-permute-start.13 = (bf16[64,3584]{1,0:T(8,128)(2,1)}, bf16[64,3584]{1,0:T(8,128)(2,1)}, u32[]{:S(2)}, u32[]{:S(2)}) collective-permute-start(bf16[64,3584]{1,0:T(8,128)(2,1)} %bitcast.17), channel_id=1, source_target_pairs={{0,4},{2,6},{4,0},{6,2},{1,5},{3,7},{5,1},{7,3},{8,12},{10,14},{12... | collective-permute-start | bytes 1376264 | tf_op jit(solution)/shard_map/ppermute | solution.py:13
  66.0 42.2 %collective-permute-start.15 = (bf16[64,3584]{1,0:T(8,128)(2,1)}, bf16[64,3584]{1,0:T(8,128)(2,1)}, u32[]{:S(2)}, u32[]{:S(2)}) collective-permute-start(bf16[64,3584]{1,0:T(8,128)(2,1)} %bitcast.17), channel_id=1, source_target_pairs={{0,2},{2,4},{4,6},{6,0},{1,3},{3,5},{5,7},{7,1},{8,10},{10,12},{12... | collective-permute-start | bytes 1376264 | tf_op jit(solution)/shard_map/ppermute | solution.py:13
  70.0 48.0 %collective-permute-start.3 = (bf16[64,3584]{1,0:T(8,128)(2,1)S(1)}, bf16[64,3584]{1,0:T(8,128)(2,1)S(1)}, u32[]{:S(2)}, u32[]{:S(2)}) collective-permute-start(bf16[64,3584]{1,0:T(8,128)(2,1)S(1)} %bitcast.313), channel_id=1, source_target_pairs={{0,6},{2,0},{4,2},{6,4},{1,7},{3,1},{5,3},{7,5},{8,14},{10,8},{12,... | collective-permute-start | bytes 1376264 | tf_op jit(solution)/shard_map/ppermute | solution.py:13
  72.0 3.6 %copy-start.6 = (f32[64,3584]{1,0:T(8,128)S(1)}, f32[64,3584]{1,0:T(8,128)}, u32[]{:S(2)}) copy-start(f32[64,3584]{1,0:T(8,128)} %fusion.141) | copy-start | bytes 2752516
  82.6 45.9 %collective-permute-start.5 = (bf16[64,3584]{1,0:T(8,128)(2,1)S(1)}, bf16[64,3584]{1,0:T(8,128)(2,1)}, u32[]{:S(2)}, u32[]{:S(2)}) collective-permute-start(bf16[64,3584]{1,0:T(8,128)(2,1)S(1)} %bitcast.314), channel_id=1, source_target_pairs={{0,4},{2,6},{4,0},{6,2},{1,5},{3,7},{5,1},{7,3},{8,12},{10,14},{12... | collective-permute-start | bytes 1376264 | tf_op jit(solution)/shard_map/ppermute | solution.py:13
  89.9 51.5 %collective-permute-start.7 = (bf16[64,3584]{1,0:T(8,128)(2,1)S(1)}, bf16[64,3584]{1,0:T(8,128)(2,1)}, u32[]{:S(2)}, u32[]{:S(2)}) collective-permute-start(bf16[64,3584]{1,0:T(8,128)(2,1)S(1)} %bitcast.315), channel_id=1, source_target_pairs={{0,2},{2,4},{4,6},{6,0},{1,3},{3,5},{5,7},{7,1},{8,10},{10,12},{12... | collective-permute-start | bytes 1376264 | tf_op jit(solution)/shard_map/ppermute | solution.py:13
  94.3 52.8 %collective-permute-start.12 = (bf16[64,3584]{1,0:T(8,128)(2,1)}, bf16[64,3584]{1,0:T(8,128)(2,1)}, u32[]{:S(2)}, u32[]{:S(2)}) collective-permute-start(bf16[64,3584]{1,0:T(8,128)(2,1)} %fusion.15), channel_id=1, source_target_pairs={{0,2},{2,4},{4,6},{6,0},{1,3},{3,5},{5,7},{7,1},{8,10},{10,12},{12... | collective-permute-start | bytes 1376264 | tf_op jit(solution)/shard_map/ppermute | solution.py:13
  108.2 38.9 %collective-permute-start.14 = (bf16[64,3584]{1,0:T(8,128)(2,1)}, bf16[64,3584]{1,0:T(8,128)(2,1)}, u32[]{:S(2)}, u32[]{:S(2)}) collective-permute-start(bf16[64,3584]{1,0:T(8,128)(2,1)} %fusion.16), channel_id=1, source_target_pairs={{0,4},{2,6},{4,0},{6,2},{1,5},{3,7},{5,1},{7,3},{8,12},{10,14},{12... | collective-permute-start | bytes 1376264 | tf_op jit(solution)/shard_map/ppermute | solution.py:13
  118.0 29.1 %collective-permute-start.16 = (bf16[64,3584]{1,0:T(8,128)(2,1)}, bf16[64,3584]{1,0:T(8,128)(2,1)}, u32[]{:S(2)}, u32[]{:S(2)}) collective-permute-start(bf16[64,3584]{1,0:T(8,128)(2,1)} %fusion.17), channel_id=1, source_target_pairs={{0,6},{2,0},{4,2},{6,4},{1,7},{3,1},{5,3},{7,5},{8,14},{10,8},{12,... | collective-permute-start | bytes 1376264 | tf_op jit(solution)/shard_map/ppermute | solution.py:13
  128.5 44.0 %collective-permute-start.4 = (bf16[64,3584]{1,0:T(8,128)(2,1)}, bf16[64,3584]{1,0:T(8,128)(2,1)}, u32[]{:S(2)}, u32[]{:S(2)}) collective-permute-start(bf16[64,3584]{1,0:T(8,128)(2,1)} %fusion.19), channel_id=1, source_target_pairs={{0,2},{2,4},{4,6},{6,0},{1,3},{3,5},{5,7},{7,1},{8,10},{10,12},{12... | collective-permute-start | bytes 1376264 | tf_op jit(solution)/shard_map/ppermute | solution.py:13
  141.4 5.7 %copy-start.5 = (f32[64,3584]{1,0:T(8,128)S(1)}, f32[64,3584]{1,0:T(8,128)}, u32[]{:S(2)}) copy-start(f32[64,3584]{1,0:T(8,128)} %fusion.137) | copy-start | bytes 2752516
  141.4 31.0 %collective-permute-start.6 = (bf16[64,3584]{1,0:T(8,128)(2,1)}, bf16[64,3584]{1,0:T(8,128)(2,1)}, u32[]{:S(2)}, u32[]{:S(2)}) collective-permute-start(bf16[64,3584]{1,0:T(8,128)(2,1)} %fusion.20), channel_id=1, source_target_pairs={{0,4},{2,6},{4,0},{6,2},{1,5},{3,7},{5,1},{7,3},{8,12},{10,14},{12... | collective-permute-start | bytes 1376264 | tf_op jit(solution)/shard_map/ppermute | solution.py:13
  150.3 32.3 %all-to-all-start.3 = ((bf16[8,8,3584]{2,1,0:T(8,128)(2,1)}), bf16[8,8,3584]{2,1,0:T(8,128)(2,1)}, u32[]{:S(2)}, u32[]{:S(2)}) async-start(bf16[8,8,3584]{2,1,0:T(8,128)(2,1)} %fusion.22), calls=%async_computation.3 | async-start | bytes 917504 | tf_op jit(solution)/shard_map/all_to_all | solution.py:17
  167.3 3.5 %copy-start.11 = (f32[64,128]{1,0:T(8,128)S(1)}, f32[64,128]{1,0:T(8,128)}, u32[]{:S(2)}) copy-start(f32[64,128]{1,0:T(8,128)} %fusion.246) | copy-start | bytes 98308
  167.3 12.0 %collective-permute-start.8 = (bf16[64,3584]{1,0:T(8,128)(2,1)}, bf16[64,3584]{1,0:T(8,128)(2,1)}, u32[]{:S(2)}, u32[]{:S(2)}) collective-permute-start(bf16[64,3584]{1,0:T(8,128)(2,1)} %fusion.21), channel_id=1, source_target_pairs={{0,6},{2,0},{4,2},{6,4},{1,7},{3,1},{5,3},{7,5},{8,14},{10,8},{12,... | collective-permute-start | bytes 1376264 | tf_op jit(solution)/shard_map/ppermute | solution.py:13
  182.7 10.1 %copy-start.9 = (bf16[1,64,3584]{2,1,0:T(8,128)(2,1)S(1)}, bf16[1,64,3584]{2,1,0:T(8,128)(2,1)}, u32[]{:S(2)}) copy-start(bf16[1,64,3584]{2,1,0:T(8,128)(2,1)} %param.11) | copy-start | bytes 1376260
  182.7 56.8 %all-to-all-start.1 = ((bf16[8,8,3584]{2,1,0:T(8,128)(2,1)}), bf16[8,8,3584]{2,1,0:T(8,128)(2,1)S(1)}, u32[]{:S(2)}, u32[]{:S(2)}) async-start(bf16[8,8,3584]{2,1,0:T(8,128)(2,1)} %fusion.25), calls=%async_computation.1 | async-start | bytes 917504 | tf_op jit(solution)/shard_map/all_to_all | solution.py:17
  192.7 46.7 %copy-start.8 = (bf16[1,64,3584]{2,1,0:T(8,128)(2,1)S(1)}, bf16[1,64,3584]{2,1,0:T(8,128)(2,1)}, u32[]{:S(2)}) copy-start(bf16[1,64,3584]{2,1,0:T(8,128)(2,1)} %param.10) | copy-start | bytes 1376260
  194.1 45.3 %copy-start.14 = (bf16[1,64,1]{1,2,0:T(2,128)(2,1)S(1)}, bf16[1,64,1]{1,2,0:T(2,128)(2,1)}, u32[]{:S(2)}) copy-start(bf16[1,64,1]{1,2,0:T(2,128)(2,1)} %param.13) | copy-start | bytes 388
  194.1 48.9 %collective-permute-start.17 = (bf16[64,3584]{1,0:T(8,128)(2,1)S(1)}, bf16[64,3584]{1,0:T(8,128)(2,1)S(1)}, u32[]{:S(2)}, u32[]{:S(2)}) collective-permute-start(bf16[64,3584]{1,0:T(8,128)(2,1)S(1)} %fusion.12), channel_id=1, source_target_pairs={{0,448},{64,0},{128,64},{192,128},{256,192},{320,256},{384,320},{4... | collective-permute-start | bytes 1376264 | tf_op jit(solution)/shard_map/ppermute | solution.py:119
  239.8 42.4 %collective-permute-start.9 = (bf16[64,3584]{1,0:T(8,128)(2,1)S(1)}, bf16[64,3584]{1,0:T(8,128)(2,1)S(1)}, u32[]{:S(2)}, u32[]{:S(2)}) collective-permute-start(bf16[64,3584]{1,0:T(8,128)(2,1)S(1)} %fusion.13), channel_id=1, source_target_pairs={{0,64},{64,128},{128,192},{192,256},{256,320},{320,384},{384,448},... | collective-permute-start | bytes 1376264 | tf_op jit(solution)/shard_map/ppermute | solution.py:118
  (6 other events, 7.6 us)

commit v2 on v1

v2 whole, which is shorter than its diff:
```python
import functools

import jax
import jax.numpy as jnp
from jax import lax
from jax.experimental import pallas as pl
from jax.experimental.pallas import tpu as pltpu
from jax.sharding import Mesh, PartitionSpec as P

BF = jnp.bfloat16
F32 = jnp.float32
ROWS_T = (((1,), (1,)), ((), ()))
COLUMNS = 512


def permute(block, axis, targets):
    return lax.ppermute(block, axis, list(enumerate(targets)))


def swap_core(block):
    return permute(block, "c", (1, 0))


def swap_weights_x(block):
    return permute(block, "x", (1, 0, 3, 2))


def swap_rows_x(block):
    return permute(block, "x", (3, 2, 1, 0))


def exchange(block):
    return lax.all_to_all(block, "z", split_axis=0, concat_axis=0, tiled=True)


def slot_tables(routes, gate_values, expert_count, capacity):
    tokens_here, picked = routes.shape
    expert_ids = jnp.arange(expert_count, dtype=jnp.int32)
    chosen = (routes[:, :, None] == expert_ids).astype(jnp.int32)
    flat_hits = chosen.reshape(tokens_here * picked, expert_count)
    earlier = jnp.cumsum(flat_hits, axis=0) - flat_hits
    position = jnp.sum(earlier * flat_hits, axis=1).reshape(tokens_here, picked)
    slot_ids = jnp.arange(capacity, dtype=jnp.int32)
    placed = chosen[:, :, :, None] * (position[:, :, None, None] == slot_ids).astype(jnp.int32)
    table = jnp.transpose(jnp.sum(placed, axis=1), (1, 2, 0)).astype(BF)
    scaled = placed.astype(BF) * gate_values[:, :, None, None]
    weighted = jnp.transpose(jnp.sum(scaled, axis=1), (1, 2, 0)).astype(BF)
    slots = expert_count * capacity
    return table.reshape(slots, tokens_here), weighted.reshape(slots, tokens_here)


def pack(table, rows):
    return jnp.dot(table, rows, preferred_element_type=F32).astype(BF)


def merge(returned, table, base):
    combined = lax.dot_general(
        table, returned, (((0,), (0,)), ((), ())), preferred_element_type=F32
    )
    return (base.astype(F32) + combined).astype(BF)


def load_weights(refs, gate_up, down, sems):
    units = down.shape[1]
    copies = []
    for u in range(4):
        copies.append(pltpu.make_async_copy(refs[u], gate_up.at[u, :, pl.ds(0, units)], sems.at[u]))
        copies.append(
            pltpu.make_async_copy(refs[4 + u], gate_up.at[u, :, pl.ds(units, units)], sems.at[4 + u])
        )
        copies.append(pltpu.make_async_copy(refs[8 + u], down.at[u], sems.at[8 + u]))
    return copies


def forward_kernel(own, visiting, *refs):
    weights, (out_own, out_visiting, rows, gate_up, down, hidden, sems) = refs[:12], refs[12:]
    copies = load_weights(weights, gate_up, down, sems)
    for copy in copies:
        copy.start()
    half, width = own.shape
    units = down.shape[1]
    rows[pl.ds(0, half), :] = own[...]
    rows[pl.ds(half, half), :] = visiting[...]
    for u in range(4):
        copies[3 * u].wait()
        copies[3 * u + 1].wait()
        pre = jnp.dot(rows[...], gate_up[u], preferred_element_type=F32)
        gate, up = pre[:, :units], pre[:, units:]
        hidden[u] = (gate * jax.nn.sigmoid(gate) * up).astype(BF)
    for u in range(4):
        copies[3 * u + 2].wait()
    for start in range(0, width, COLUMNS):
        at = pl.ds(start, COLUMNS)
        total = jnp.dot(hidden[0], down[0, :, at], preferred_element_type=F32)
        for u in range(1, 4):
            total = total + jnp.dot(hidden[u], down[u, :, at], preferred_element_type=F32)
        out_own[:, at] = total[:half]
        out_visiting[:, at] = total[half:].astype(BF)


def backward_kernel(own, visiting, saved, *refs):
    weights, (out_own, out_visiting, rows, gate_up, down, grads, sems) = refs[:12], refs[12:]
    copies = load_weights(weights, gate_up, down, sems)
    for copy in copies:
        copy.start()
    half, width = own.shape
    units = down.shape[1]
    rows[pl.ds(0, half), :] = own[...]
    rows[pl.ds(half, half), :] = visiting[...]
    for u in range(4):
        copies[3 * u + 2].wait()
        grad = lax.dot_general(rows[...], down[u], ROWS_T, preferred_element_type=F32)
        a, b = saved[u, 0].astype(F32), saved[u, 1].astype(F32)
        sig = jax.nn.sigmoid(a)
        grads[u, :, pl.ds(0, units)] = (grad * b * sig * (1.0 + a * (1.0 - sig))).astype(BF)
        grads[u, :, pl.ds(units, units)] = (grad * a * sig).astype(BF)
    for u in range(4):
        copies[3 * u].wait()
        copies[3 * u + 1].wait()
    for start in range(0, width, COLUMNS):
        at = pl.ds(start, COLUMNS)
        total = lax.dot_general(grads[0], gate_up[0, at, :], ROWS_T, preferred_element_type=F32)
        for u in range(1, 4):
            total = total + lax.dot_general(
                grads[u], gate_up[u, at, :], ROWS_T, preferred_element_type=F32
            )
        out_own[:, at] = total[:half]
        out_visiting[:, at] = total[half:].astype(BF)


def expert_pass(kernel, own, visiting, extra, weights, middle):
    half, width = own.shape
    units = weights[8].shape[0]
    vmem = pl.BlockSpec(memory_space=pltpu.VMEM)
    rows, flops = 2 * half, 2 * 2 * half * width * 4 * units * 3
    return pl.pallas_call(
        kernel,
        out_shape=(
            jax.ShapeDtypeStruct((half, width), F32),
            jax.ShapeDtypeStruct((half, width), BF),
        ),
        in_specs=[vmem] * (2 + len(extra)) + [pl.BlockSpec(memory_space=pl.ANY)] * 12,
        out_specs=(vmem, vmem),
        scratch_shapes=[
            pltpu.VMEM((rows, width), BF),
            pltpu.VMEM((4, width, 2 * units), BF),
            pltpu.VMEM((4, units, width), BF),
            pltpu.VMEM((4, rows, middle), BF),
            pltpu.SemaphoreType.DMA((12,)),
        ],
        compiler_params=pltpu.CompilerParams(vmem_limit_bytes=40 * 1024 * 1024),
        cost_estimate=pl.CostEstimate(
            flops=flops, bytes_accessed=12 * width * units * 2 + 5 * half * width * 2, transcendentals=0
        ),
    )(own, visiting, *extra, *weights)


def body(
    forward_state, grad_state, forward_routes, forward_gates, backward_routes, backward_gates,
    saved_preacts, gate_weight, up_weight, down_weight,
):
    x, y, saved = forward_state[0], grad_state[0], saved_preacts[0]
    width = x.shape[1]
    capacity, units = saved.shape[2], saved.shape[3]
    nz, nx, nc = lax.axis_size("z"), lax.axis_size("x"), lax.axis_size("c")
    f_table, f_weighted = slot_tables(forward_routes[0], forward_gates[0], nz, capacity)
    b_table, b_weighted = slot_tables(backward_routes[0], backward_gates[0], nz, capacity)
    f_rows = exchange(pack(f_table, x).reshape(nz, capacity, width)).reshape(-1, width)
    b_rows = exchange(pack(b_weighted, y).reshape(nz, capacity, width)).reshape(-1, width)

    own_weights = (gate_weight[0], up_weight[0], down_weight[0])
    beside_weights = [swap_weights_x(mine) for mine in own_weights]
    f_visiting = swap_rows_x(f_rows)
    f_visiting, *beside_weights = lax.optimization_barrier((f_visiting, *beside_weights))
    weights = []
    for mine, beside in zip(own_weights, beside_weights):
        weights += [mine, swap_core(mine), beside, swap_core(beside)]

    me_x, me_c = lax.axis_index("x"), lax.axis_index("c")
    by_place = saved.reshape(2, nz, nx, nc, capacity, units)

    def kept_for(at_x):
        rows_of = [
            lax.dynamic_index_in_dim(by_place, at, 2, keepdims=False) for at in (at_x, nx - 1 - at_x)
        ]
        return jnp.stack(rows_of, 1)

    here = jnp.stack([kept_for(me_x), swap_weights_x(kept_for(me_x ^ 1))])
    mine = lax.dynamic_index_in_dim(here, me_c, 4, keepdims=False)
    theirs = swap_core(lax.dynamic_index_in_dim(here, 1 - me_c, 4, keepdims=False))
    kept = jnp.stack([mine, theirs], 1).reshape(4, 2, 2 * nz * capacity, units)

    f_own, f_visited = expert_pass(
        forward_kernel, f_rows, f_visiting, (), weights, units
    )
    b_own, b_visited = expert_pass(
        backward_kernel, b_rows, swap_rows_x(b_rows), (kept,), weights, 2 * units
    )
    f_out = (f_own + swap_rows_x(f_visited).astype(F32)).astype(BF)
    b_out = (b_own + swap_rows_x(b_visited).astype(F32)).astype(BF)
    f_back = exchange(f_out.reshape(nz, capacity, width)).reshape(-1, width)
    b_back = exchange(b_out.reshape(nz, capacity, width)).reshape(-1, width)
    result = merge(f_back, f_weighted, x)
    gradient = merge(b_back, b_table, y)
    ring = lax.axis_size(("h", "y"))
    forward_next = permute(result, ("h", "y"), [(i + 1) % ring for i in range(ring)])
    backward_next = permute(gradient, ("h", "y"), [(i - 1) % ring for i in range(ring)])
    return forward_next[None], backward_next[None]


def solution(mesh):
    pipes = mesh.shape["pipe"]
    fine = Mesh(mesh.devices.reshape(2, pipes // 2, 8, 4, 2), ("h", "y", "z", "x", "c"))
    pipe, expert = ("h", "y"), ("z", "x", "c")
    tokens = P(pipe, expert, None)
    return jax.shard_map(
        body,
        mesh=fine,
        in_specs=(
            tokens, tokens, tokens, tokens, tokens, tokens,
            P(pipe, None, None, None, expert),
            P(pipe, None, expert),
            P(pipe, None, expert),
            P(pipe, expert, None),
        ),
        out_specs=(tokens, tokens),
        check_vma=False,
    )
```

time: 286 us -> 265 us (0.927)
  the two profiles are of different devices: /device:TPU:102 before, /device:TPU:24 now
where the time goes in v2:
time: 265 us; the launch traced here: 264 us
  waiting for transfers between devices  145 us (55%)
  starting transfers between devices  86.4 us (33%)
  Pallas kernels  15.5 us (6%)
  matrix products  6.02 us (2%)
  other arithmetic  5.55 us (2%)
  local copies, waits for them, and re-layouts  4.61 us (2%)
    ppermute x17, waiting for transfers between devices, permute(): return lax.ppermute(block, axis, list(enumerate(targets)))  75.6 us
    all_to_all x4, waiting for transfers between devices, exchange(): return lax.all_to_all(block, 'z', split_axis=0, concat_axis=0, tiled=True)  69.1 us
    ppermute x17, starting transfers between devices, permute(): return lax.ppermute(block, axis, list(enumerate(targets)))  50.4 us
    all_to_all x4, starting transfers between devices, exchange(): return lax.all_to_all(block, 'z', split_axis=0, concat_axis=0, tiled=True)  35.9 us
    pallas_call x2, Pallas kernels, expert_pass(): pl.pallas_call(kernel, out_shape=(jax.ShapeDtypeStruct((half, width), F32...  15.5 us
  transfers between devices with their start and end apart: 21, of which 11 were waited for; matrix products, arithmetic and copies ran while one was open for 3% of the time, Pallas kernels for 6%

profile of v2, /device:TPU:24, one launch (start us, length us, event | category | flops | bytes accessed | tf_op | source)
XLA Modules:
  0.0 263.8 jit_solution(11447408467595491745)
XLA Ops:
  1.7 2.2 fusion.4
  3.9 12.5 %all-to-all-start = ((bf16[8,8,3584]{2,1,0:T(8,128)(2,1)}), bf16[8,8,3584]{2,1,0:T(8,128)(2,1)}, u32[]{:S(2)}, u32[]{:S(2)}) async-start(bf16[8,8,3584]{2,1,0:T(8,128)(2,1)} %fusion.4), calls=%async_computation | async-start | bytes 917504 | tf_op jit(solution)/shard_map/all_to_all | solution.py:33
  16.4 3.4 %collective-permute-start.1 = (bf16[3584,128]{1,0:T(8,128)(2,1)S(1)}, bf16[3584,128]{1,0:T(8,128)(2,1)}, u32[]{:S(2)}, u32[]{:S(2)}) collective-permute-start(bf16[3584,128]{1,0:T(8,128)(2,1)S(1)} %bitcast.67), channel_id=1, source_target_pairs={{0,2},{2,0},{4,6},{6,4},{1,3},{3,1},{5,7},{7,5},{8,10},{10,8},{12,... | collective-permute-start | bytes 2752520 | tf_op jit(solution)/shard_map/ppermute | solution.py:17
  19.8 2.5 collective-permute-start.2
  22.3 3.4 %collective-permute-start.3 = (bf16[128,3584]{1,0:T(8,128)(2,1)}, bf16[128,3584]{1,0:T(8,128)(2,1)}, u32[]{:S(2)}, u32[]{:S(2)}) collective-permute-start(bf16[128,3584]{1,0:T(8,128)(2,1)} %bitcast.75), channel_id=1, source_target_pairs={{0,2},{2,0},{4,6},{6,4},{1,3},{3,1},{5,7},{7,5},{8,10},{10,8},{12,... | collective-permute-start | bytes 2752520 | tf_op jit(solution)/shard_map/ppermute | solution.py:17
  25.7 1.9 collective-permute-start.4
  27.8 14.6 %all-to-all-done = bf16[8,8,3584]{2,1,0:T(8,128)(2,1)} async-done(((bf16[8,8,3584]{2,1,0:T(8,128)(2,1)}), bf16[8,8,3584]{2,1,0:T(8,128)(2,1)}, u32[]{:S(2)}, u32[]{:S(2)}) %all-to-all-start) | async-done | bytes 458784 | tf_op jit(solution)/shard_map/all_to_all | solution.py:33
  42.4 4.7 %collective-permute-start = (bf16[64,3584]{1,0:T(8,128)(2,1)}, bf16[64,3584]{1,0:T(8,128)(2,1)}, u32[]{:S(2)}, u32[]{:S(2)}) collective-permute-start(bf16[64,3584]{1,0:T(8,128)(2,1)} %bitcast.5.own), channel_id=1, source_target_pairs={{0,6},{2,4},{4,2},{6,0},{1,7},{3,5},{5,3},{7,1},{8,14},{10,12},{12... | collective-permute-start | bytes 1376264 | tf_op jit(solution)/shard_map/ppermute | solution.py:17
  47.9 2.1 fusion.5
  50.0 4.3 %all-to-all-start.2 = ((bf16[8,8,3584]{2,1,0:T(8,128)(2,1)}), bf16[8,8,3584]{2,1,0:T(8,128)(2,1)S(1)}, u32[]{:S(2)}, u32[]{:S(2)}) async-start(bf16[8,8,3584]{2,1,0:T(8,128)(2,1)} %fusion.5), calls=%async_computation.2 | async-start | bytes 917504 | tf_op jit(solution)/shard_map/all_to_all | solution.py:33
  54.3 1.9 collective-permute-start.6
  56.2 5.1 %collective-permute-done.2.refs_6_ = bf16[3584,128]{1,0:T(8,128)(2,1)} collective-permute-done((bf16[3584,128]{1,0:T(8,128)(2,1)S(1)}, bf16[3584,128]{1,0:T(8,128)(2,1)}, u32[]{:S(2)}, u32[]{:S(2)}) %collective-permute-start.2) | collective-permute-done | bytes 917536 | tf_op jit(solution)/shard_map/ppermute | solution.py:17
  63.2 16.3 %collective-permute-done.3.refs_10_ = bf16[128,3584]{1,0:T(8,128)(2,1)} collective-permute-done((bf16[128,3584]{1,0:T(8,128)(2,1)}, bf16[128,3584]{1,0:T(8,128)(2,1)}, u32[]{:S(2)}, u32[]{:S(2)}) %collective-permute-start.3) | collective-permute-done | bytes 917536 | tf_op jit(solution)/shard_map/ppermute | solution.py:17
  81.4 2.4 collective-permute-start.7
  83.9 1.9 collective-permute-start.9
  86.3 2.3 collective-permute-done.9.refs_11_
  88.6 7.4 %shard_map.113 = (f32[64,3584]{1,0:T(8,128)S(1)}, bf16[64,3584]{1,0:T(8,128)(2,1)}) custom-call(bf16[64,3584]{1,0:T(8,128)(2,1)} %bitcast.5.own, bf16[64,3584]{1,0:T(8,128)(2,1)} %collective-permute-done.visiting, bf16[3584,128]{1,0:T(8,128)(2,1)S(1)} %bitcast.69, bf16[3584,128]{1,0:T(8,128)(2,1)} %collective-permute-done.4.refs_1_, ...), custom_call_target="tpu_custom_call" | custom-call | flops 1409286144 | bytes 13303808 | tf_op jit(solution)/shard_map/pallas_call | solution.py:136
  97.0 4.7 %collective-permute-start.10 = (bf16[64,3584]{1,0:T(8,128)(2,1)}, bf16[64,3584]{1,0:T(8,128)(2,1)}, u32[]{:S(2)}, u32[]{:S(2)}) collective-permute-start(bf16[64,3584]{1,0:T(8,128)(2,1)} %get-tuple-element.15), channel_id=1, source_target_pairs={{0,6},{2,4},{4,2},{6,0},{1,7},{3,5},{5,3},{7,1},{8,14},{10,12},{12... | collective-permute-start | bytes 1376264 | tf_op jit(solution)/shard_map/ppermute | solution.py:17
  101.8 2.1 collective-permute-start.13
  103.9 5.1 %collective-permute-done.13 = bf16[2,2,8,2,8,128]{5,4,3,2,0,1:T(8,128)(2,1)} collective-permute-done((bf16[2,2,8,2,8,128]{5,4,3,2,0,1:T(8,128)(2,1)S(1)}, bf16[2,2,8,2,8,128]{5,4,3,2,0,1:T(8,128)(2,1)}, u32[]{:S(2)}, u32[]{:S(2)}) %collective-permute-start.13) | collective-permute-done | bytes 131104 | tf_op jit(solution)/shard_map/ppermute | solution.py:17
  110.0 1.9 collective-permute-start.14
  111.9 2.4 collective-permute-start.12
  114.3 2.1 fusion.6
  116.5 9.6 %all-to-all-start.1 = ((bf16[8,8,3584]{2,1,0:T(8,128)(2,1)}), bf16[8,8,3584]{2,1,0:T(8,128)(2,1)}, u32[]{:S(2)}, u32[]{:S(2)}) async-start(bf16[8,8,3584]{2,1,0:T(8,128)(2,1)} %fusion.6), calls=%async_computation.1 | async-start | bytes 917504 | tf_op jit(solution)/shard_map/all_to_all | solution.py:33
  128.0 8.1 %shard_map.114 = (f32[64,3584]{1,0:T(8,128)S(1)}, bf16[64,3584]{1,0:T(8,128)(2,1)S(1)}) custom-call(bf16[64,3584]{1,0:T(8,128)(2,1)S(1)} %bitcast.80, bf16[64,3584]{1,0:T(8,128)(2,1)} %collective-permute-done.12.visiting, bf16[4,2,128,128]{3,2,1,0:T(8,128)(2,1)S(1)} %bitcast.81, bf16[3584,128]{1,0:T(8,128)(2,1)S(1)} %bitcast.70, ...), custom_call_target="tpu_custom_call" | custom-call | flops 1409286144 | bytes 13303808 | tf_op jit(solution)/shard_map/pallas_call | solution.py:136
  136.2 3.7 %collective-permute-start.15 = (bf16[64,3584]{1,0:T(8,128)(2,1)S(1)}, bf16[64,3584]{1,0:T(8,128)(2,1)S(1)}, u32[]{:S(2)}, u32[]{:S(2)}) collective-permute-start(bf16[64,3584]{1,0:T(8,128)(2,1)S(1)} %get-tuple-element.17), channel_id=1, source_target_pairs={{0,6},{2,4},{4,2},{6,0},{1,7},{3,5},{5,3},{7,1},{8,14},{10,12},{12... | collective-permute-start | bytes 1376264 | tf_op jit(solution)/shard_map/ppermute | solution.py:17
  139.9 11.6 %collective-permute-done.15 = bf16[64,3584]{1,0:T(8,128)(2,1)S(1)} collective-permute-done((bf16[64,3584]{1,0:T(8,128)(2,1)S(1)}, bf16[64,3584]{1,0:T(8,128)(2,1)S(1)}, u32[]{:S(2)}, u32[]{:S(2)}) %collective-permute-start.15) | collective-permute-done | bytes 458784 | tf_op jit(solution)/shard_map/ppermute | solution.py:17
  152.5 9.5 %all-to-all-start.3 = ((bf16[8,8,3584]{2,1,0:T(8,128)(2,1)}), bf16[8,8,3584]{2,1,0:T(8,128)(2,1)S(1)}, u32[]{:S(2)}, u32[]{:S(2)}) async-start(bf16[8,8,3584]{2,1,0:T(8,128)(2,1)} %fusion.7), calls=%async_computation.3 | async-start | bytes 917504 | tf_op jit(solution)/shard_map/all_to_all | solution.py:33
  164.0 7.9 %collective-permute-start.11 = (bf16[64,3584]{1,0:T(8,128)(2,1)S(1)}, bf16[64,3584]{1,0:T(8,128)(2,1)S(1)}, u32[]{:S(2)}, u32[]{:S(2)}) collective-permute-start(bf16[64,3584]{1,0:T(8,128)(2,1)S(1)} %fusion.3), channel_id=1, source_target_pairs={{0,64},{64,128},{128,192},{192,256},{256,320},{320,384},{384,448},... | collective-permute-start | bytes 1376264 | tf_op jit(solution)/shard_map/ppermute | solution.py:17
  171.9 54.3 %all-to-all-done.3 = bf16[8,8,3584]{2,1,0:T(8,128)(2,1)S(1)} async-done(((bf16[8,8,3584]{2,1,0:T(8,128)(2,1)}), bf16[8,8,3584]{2,1,0:T(8,128)(2,1)S(1)}, u32[]{:S(2)}, u32[]{:S(2)}) %all-to-all-start.3) | async-done | bytes 458784 | tf_op jit(solution)/shard_map/all_to_all | solution.py:33
  226.5 1.9 collective-permute-start.16
  228.5 33.8 %collective-permute-done.16 = bf16[64,3584]{1,0:T(8,128)(2,1)S(1)} collective-permute-done((bf16[64,3584]{1,0:T(8,128)(2,1)S(1)}, bf16[64,3584]{1,0:T(8,128)(2,1)S(1)}, u32[]{:S(2)}, u32[]{:S(2)}) %collective-permute-start.16) | collective-permute-done | bytes 458784 | tf_op jit(solution)/shard_map/ppermute | solution.py:17
  (58 shorter events, 15.2 us)
Async XLA Ops:
  0.6 0.7 copy-start.7
  1.6 14.7 %copy-start = (bf16[1,3584,128]{2,1,0:T(8,128)(2,1)S(1)}, bf16[1,3584,128]{2,1,0:T(8,128)(2,1)}, u32[]{:S(2)}) copy-start(bf16[1,3584,128]{2,1,0:T(8,128)(2,1)} %param.17) | copy-start | bytes 2752516
  1.7 18.1 %copy-start.1 = (bf16[1,3584,128]{2,1,0:T(8,128)(2,1)S(1)}, bf16[1,3584,128]{2,1,0:T(8,128)(2,1)}, u32[]{:S(2)}) copy-start(bf16[1,3584,128]{2,1,0:T(8,128)(2,1)} %param.18) | copy-start | bytes 2752516
  3.9 38.6 %all-to-all-start = ((bf16[8,8,3584]{2,1,0:T(8,128)(2,1)}), bf16[8,8,3584]{2,1,0:T(8,128)(2,1)}, u32[]{:S(2)}, u32[]{:S(2)}) async-start(bf16[8,8,3584]{2,1,0:T(8,128)(2,1)} %fusion.4), calls=%async_computation | async-start | bytes 917504 | tf_op jit(solution)/shard_map/all_to_all | solution.py:33
  16.4 37.9 %collective-permute-start.1 = (bf16[3584,128]{1,0:T(8,128)(2,1)S(1)}, bf16[3584,128]{1,0:T(8,128)(2,1)}, u32[]{:S(2)}, u32[]{:S(2)}) collective-permute-start(bf16[3584,128]{1,0:T(8,128)(2,1)S(1)} %bitcast.67), channel_id=1, source_target_pairs={{0,2},{2,0},{4,6},{6,4},{1,3},{3,1},{5,7},{7,5},{8,10},{10,8},{12,... | collective-permute-start | bytes 2752520 | tf_op jit(solution)/shard_map/ppermute | solution.py:17
  19.8 41.5 %collective-permute-start.2 = (bf16[3584,128]{1,0:T(8,128)(2,1)S(1)}, bf16[3584,128]{1,0:T(8,128)(2,1)}, u32[]{:S(2)}, u32[]{:S(2)}) collective-permute-start(bf16[3584,128]{1,0:T(8,128)(2,1)S(1)} %bitcast.71), channel_id=1, source_target_pairs={{0,2},{2,0},{4,6},{6,4},{1,3},{3,1},{5,7},{7,5},{8,10},{10,8},{12,... | collective-permute-start | bytes 2752520 | tf_op jit(solution)/shard_map/ppermute | solution.py:17
  22.3 5.3 %copy-start.8 = (s32[1,64,1]{1,2,0:T(1,128)S(1)}, s32[1,64,1]{1,2,0:T(1,128)}, u32[]{:S(2)}) copy-start(s32[1,64,1]{1,2,0:T(1,128)} %param.14) | copy-start | bytes 772
  22.3 57.3 %collective-permute-start.3 = (bf16[128,3584]{1,0:T(8,128)(2,1)}, bf16[128,3584]{1,0:T(8,128)(2,1)}, u32[]{:S(2)}, u32[]{:S(2)}) collective-permute-start(bf16[128,3584]{1,0:T(8,128)(2,1)} %bitcast.75), channel_id=1, source_target_pairs={{0,2},{2,0},{4,6},{6,4},{1,3},{3,1},{5,7},{7,5},{8,10},{10,8},{12,... | collective-permute-start | bytes 2752520 | tf_op jit(solution)/shard_map/ppermute | solution.py:17
  25.7 58.2 %collective-permute-start.4 = (bf16[3584,128]{1,0:T(8,128)(2,1)S(1)}, bf16[3584,128]{1,0:T(8,128)(2,1)}, u32[]{:S(2)}, u32[]{:S(2)}) collective-permute-start(bf16[3584,128]{1,0:T(8,128)(2,1)S(1)} %bitcast.68), channel_id=1, source_target_pairs={{0,1},{1,0},{2,3},{3,2},{4,5},{5,4},{6,7},{7,6},{8,9},{9,8},{10,11... | collective-permute-start | bytes 2752520 | tf_op jit(solution)/shard_map/ppermute | solution.py:17
  42.4 37.1 %collective-permute-start = (bf16[64,3584]{1,0:T(8,128)(2,1)}, bf16[64,3584]{1,0:T(8,128)(2,1)}, u32[]{:S(2)}, u32[]{:S(2)}) collective-permute-start(bf16[64,3584]{1,0:T(8,128)(2,1)} %bitcast.5.own), channel_id=1, source_target_pairs={{0,6},{2,4},{4,2},{6,0},{1,7},{3,5},{5,3},{7,1},{8,14},{10,12},{12... | collective-permute-start | bytes 1376264 | tf_op jit(solution)/shard_map/ppermute | solution.py:17
  47.3 0.7 copy-start.10
  47.9 13.4 %copy-start.2 = (bf16[1,128,3584]{2,1,0:T(8,128)(2,1)S(1)}, bf16[1,128,3584]{2,1,0:T(8,128)(2,1)}, u32[]{:S(2)}) copy-start(bf16[1,128,3584]{2,1,0:T(8,128)(2,1)} %param.19) | copy-start | bytes 2752516
  50.0 61.9 %all-to-all-start.2 = ((bf16[8,8,3584]{2,1,0:T(8,128)(2,1)}), bf16[8,8,3584]{2,1,0:T(8,128)(2,1)S(1)}, u32[]{:S(2)}, u32[]{:S(2)}) async-start(bf16[8,8,3584]{2,1,0:T(8,128)(2,1)} %fusion.5), calls=%async_computation.2 | async-start | bytes 917504 | tf_op jit(solution)/shard_map/all_to_all | solution.py:33
  54.3 31.5 %collective-permute-start.6 = (bf16[3584,128]{1,0:T(8,128)(2,1)S(1)}, bf16[3584,128]{1,0:T(8,128)(2,1)}, u32[]{:S(2)}, u32[]{:S(2)}) collective-permute-start(bf16[3584,128]{1,0:T(8,128)(2,1)S(1)} %bitcast.72), channel_id=1, source_target_pairs={{0,1},{1,0},{2,3},{3,2},{4,5},{5,4},{6,7},{7,6},{8,9},{9,8},{10,11... | collective-permute-start | bytes 2752520 | tf_op jit(solution)/shard_map/ppermute | solution.py:17
  61.3 24.5 %collective-permute-start.8 = (bf16[128,3584]{1,0:T(8,128)(2,1)S(1)}, bf16[128,3584]{1,0:T(8,128)(2,1)}, u32[]{:S(2)}, u32[]{:S(2)}) collective-permute-start(bf16[128,3584]{1,0:T(8,128)(2,1)S(1)} %bitcast.76), channel_id=1, source_target_pairs={{0,1},{1,0},{2,3},{3,2},{4,5},{5,4},{6,7},{7,6},{8,9},{9,8},{10,11... | collective-permute-start | bytes 2752520 | tf_op jit(solution)/shard_map/ppermute | solution.py:17
  79.5 6.3 %collective-permute-start.5 = (bf16[3584,128]{1,0:T(8,128)(2,1)}, bf16[3584,128]{1,0:T(8,128)(2,1)}, u32[]{:S(2)}, u32[]{:S(2)}) collective-permute-start(bf16[3584,128]{1,0:T(8,128)(2,1)} %collective-permute-done.1.refs_2_), channel_id=1, source_target_pairs={{0,1},{1,0},{2,3},{3,2},{4,5},{5,4},{6,7},{7,6},{8,9},{9,8},{10,11... | collective-permute-start | bytes 2752520 | tf_op jit(solution)/shard_map/ppermute | solution.py:17
  81.4 4.8 %collective-permute-start.7 = (bf16[3584,128]{1,0:T(8,128)(2,1)}, bf16[3584,128]{1,0:T(8,128)(2,1)}, u32[]{:S(2)}, u32[]{:S(2)}) collective-permute-start(bf16[3584,128]{1,0:T(8,128)(2,1)} %collective-permute-done.2.refs_6_), channel_id=1, source_target_pairs={{0,1},{1,0},{2,3},{3,2},{4,5},{5,4},{6,7},{7,6},{8,9},{9,8},{10,11... | collective-permute-start | bytes 2752520 | tf_op jit(solution)/shard_map/ppermute | solution.py:17
  83.9 4.7 %collective-permute-start.9 = (bf16[128,3584]{1,0:T(8,128)(2,1)}, bf16[128,3584]{1,0:T(8,128)(2,1)}, u32[]{:S(2)}, u32[]{:S(2)}) collective-permute-start(bf16[128,3584]{1,0:T(8,128)(2,1)} %collective-permute-done.3.refs_10_), channel_id=1, source_target_pairs={{0,1},{1,0},{2,3},{3,2},{4,5},{5,4},{6,7},{7,6},{8,9},{9,8},{10,11... | collective-permute-start | bytes 2752520 | tf_op jit(solution)/shard_map/ppermute | solution.py:17
  85.8 15.9 %copy-start.6 = (bf16[1,2,64,8,128]{4,3,2,1,0:T(8,128)(2,1)S(1)}, bf16[1,2,64,8,128]{4,3,2,1,0:T(8,128)(2,1)}, u32[]{:S(2)}) copy-start(bf16[1,2,64,8,128]{4,3,2,1,0:T(8,128)(2,1)} %param.16) | copy-start | bytes 786436
  96.0 1.0 copy-start.3
  97.0 17.3 %collective-permute-start.10 = (bf16[64,3584]{1,0:T(8,128)(2,1)}, bf16[64,3584]{1,0:T(8,128)(2,1)}, u32[]{:S(2)}, u32[]{:S(2)}) collective-permute-start(bf16[64,3584]{1,0:T(8,128)(2,1)} %get-tuple-element.15), channel_id=1, source_target_pairs={{0,6},{2,4},{4,2},{6,0},{1,7},{3,5},{5,3},{7,1},{8,14},{10,12},{12... | collective-permute-start | bytes 1376264 | tf_op jit(solution)/shard_map/ppermute | solution.py:17
  101.8 7.3 %collective-permute-start.13 = (bf16[2,2,8,2,8,128]{5,4,3,2,0,1:T(8,128)(2,1)S(1)}, bf16[2,2,8,2,8,128]{5,4,3,2,0,1:T(8,128)(2,1)}, u32[]{:S(2)}, u32[]{:S(2)}) collective-permute-start(bf16[2,2,8,2,8,128]{5,4,3,2,0,1:T(8,128)(2,1)S(1)} %pad_maximum_fusion.1), channel_id=1, source_target_pairs={{0,2},{2,0},{4,6},{6,4},{1,3},{3,1},{5,7},{7,5},{8,10},{10,8},{12,... | collective-permute-start | bytes 393224 | tf_op jit(solution)/shard_map/ppermute | solution.py:17
  110.0 16.1 %collective-permute-start.14 = (bf16[2,2,2,8,8,128]{5,4,3,2,1,0:T(8,128)(2,1)S(1)}, bf16[2,2,2,8,8,128]{5,4,3,2,1,0:T(8,128)(2,1)}, u32[]{:S(2)}, u32[]{:S(2)}) collective-permute-start(bf16[2,2,2,8,8,128]{5,4,3,2,1,0:T(8,128)(2,1)S(1)} %bitcast.86), channel_id=1, source_target_pairs={{0,1},{1,0},{2,3},{3,2},{4,5},{5,4},{6,7},{7,6},{8,9},{9,8},{10,11... | collective-permute-start | bytes 393224 | tf_op jit(solution)/shard_map/ppermute | solution.py:17
  111.9 16.1 %collective-permute-start.12 = (bf16[64,3584]{1,0:T(8,128)(2,1)S(1)}, bf16[64,3584]{1,0:T(8,128)(2,1)}, u32[]{:S(2)}, u32[]{:S(2)}) collective-permute-start(bf16[64,3584]{1,0:T(8,128)(2,1)S(1)} %bitcast.79), channel_id=1, source_target_pairs={{0,6},{2,4},{4,2},{6,0},{1,7},{3,5},{5,3},{7,1},{8,14},{10,12},{12... | collective-permute-start | bytes 1376264 | tf_op jit(solution)/shard_map/ppermute | solution.py:17
  116.5 36.0 %all-to-all-start.1 = ((bf16[8,8,3584]{2,1,0:T(8,128)(2,1)}), bf16[8,8,3584]{2,1,0:T(8,128)(2,1)}, u32[]{:S(2)}, u32[]{:S(2)}) async-start(bf16[8,8,3584]{2,1,0:T(8,128)(2,1)} %fusion.6), calls=%async_computation.1 | async-start | bytes 917504 | tf_op jit(solution)/shard_map/all_to_all | solution.py:33
  136.2 15.2 %collective-permute-start.15 = (bf16[64,3584]{1,0:T(8,128)(2,1)S(1)}, bf16[64,3584]{1,0:T(8,128)(2,1)S(1)}, u32[]{:S(2)}, u32[]{:S(2)}) collective-permute-start(bf16[64,3584]{1,0:T(8,128)(2,1)S(1)} %get-tuple-element.17), channel_id=1, source_target_pairs={{0,6},{2,4},{4,2},{6,0},{1,7},{3,5},{5,3},{7,1},{8,14},{10,12},{12... | collective-permute-start | bytes 1376264 | tf_op jit(solution)/shard_map/ppermute | solution.py:17
  152.3 9.7 %copy-start.4 = (bf16[1,64,3584]{2,1,0:T(8,128)(2,1)S(1)}, bf16[1,64,3584]{2,1,0:T(8,128)(2,1)}, u32[]{:S(2)}) copy-start(bf16[1,64,3584]{2,1,0:T(8,128)(2,1)} %param.10) | copy-start | bytes 1376260
  152.5 73.7 %all-to-all-start.3 = ((bf16[8,8,3584]{2,1,0:T(8,128)(2,1)}), bf16[8,8,3584]{2,1,0:T(8,128)(2,1)S(1)}, u32[]{:S(2)}, u32[]{:S(2)}) async-start(bf16[8,8,3584]{2,1,0:T(8,128)(2,1)} %fusion.7), calls=%async_computation.3 | async-start | bytes 917504 | tf_op jit(solution)/shard_map/all_to_all | solution.py:33
  162.0 0.7 copy-start.9
  162.6 63.6 %copy-start.5 = (bf16[1,64,3584]{2,1,0:T(8,128)(2,1)S(1)}, bf16[1,64,3584]{2,1,0:T(8,128)(2,1)}, u32[]{:S(2)}) copy-start(bf16[1,64,3584]{2,1,0:T(8,128)(2,1)} %param.11) | copy-start | bytes 1376260
  164.0 64.4 %collective-permute-start.11 = (bf16[64,3584]{1,0:T(8,128)(2,1)S(1)}, bf16[64,3584]{1,0:T(8,128)(2,1)S(1)}, u32[]{:S(2)}, u32[]{:S(2)}) collective-permute-start(bf16[64,3584]{1,0:T(8,128)(2,1)S(1)} %fusion.3), channel_id=1, source_target_pairs={{0,64},{64,128},{128,192},{192,256},{256,320},{320,384},{384,448},... | collective-permute-start | bytes 1376264 | tf_op jit(solution)/shard_map/ppermute | solution.py:17
  226.5 35.7 %collective-permute-start.16 = (bf16[64,3584]{1,0:T(8,128)(2,1)S(1)}, bf16[64,3584]{1,0:T(8,128)(2,1)S(1)}, u32[]{:S(2)}, u32[]{:S(2)}) collective-permute-start(bf16[64,3584]{1,0:T(8,128)(2,1)S(1)} %fusion.2), channel_id=1, source_target_pairs={{0,448},{64,0},{128,64},{192,128},{256,192},{320,256},{384,320},{4... | collective-permute-start | bytes 1376264 | tf_op jit(solution)/shard_map/ppermute | solution.py:17

commit v3 on v2

v3 whole, which is shorter than its diff:
```python
import jax
import jax.numpy as jnp
from jax import lax
from jax.experimental import pallas as pl
from jax.experimental.pallas import tpu as pltpu
from jax.sharding import Mesh, PartitionSpec as P

BF = jnp.bfloat16
F32 = jnp.float32
ROWS_T = (((1,), (1,)), ((), ()))
COLUMNS = 512
GATE_COLUMNS = 128
VMEM = pl.BlockSpec(memory_space=pltpu.VMEM)


def permute(block, axis, targets):
    return lax.ppermute(block, axis, list(enumerate(targets)))


def swap_core(block):
    return permute(block, "c", (1, 0))


def swap_weights_x(block):
    return permute(block, "x", (1, 0, 3, 2))


def swap_rows_x(block):
    return permute(block, "x", (3, 2, 1, 0))


def exchange(block):
    return lax.all_to_all(block, "z", split_axis=0, concat_axis=0, tiled=True)


def pair_mask(r_col, r_row, passes):
    rows = jax.lax.broadcasted_iota(jnp.int32, (r_col.shape[0], r_row.shape[1]), 0)
    cols = jax.lax.broadcasted_iota(jnp.int32, (r_col.shape[0], r_row.shape[1]), 1)
    same = r_col == r_row
    if passes > 1:
        per_pass = r_row.shape[1] // passes
        same = same & ((rows >= per_pass) == (cols >= per_pass))
    return same, rows, cols


def pack_kernel(r_row, r_col, gate_col, x, y, out):
    tokens, width = x.shape
    same, rows, cols = pair_mask(r_col[...], r_row[...], 2)
    slot = jnp.sum((same & (rows < cols)).astype(jnp.int32), axis=0, keepdims=True)
    second = (cols[:1] >= tokens).astype(jnp.int32)
    key = r_row[...] * 16 + second * 8 + slot
    table = (rows == key).astype(F32).astype(BF)
    for start in range(0, width, COLUMNS):
        at = pl.ds(start, COLUMNS)
        picked = jnp.dot(table[:, :tokens], x[:, at], preferred_element_type=F32)
        picked = picked + jnp.dot(table[:, tokens:], y[:, at], preferred_element_type=F32)
        out[:, at] = picked.astype(BF)
    gates = jnp.broadcast_to(gate_col[...], (2 * tokens, GATE_COLUMNS)).astype(BF)
    out[:, pl.ds(width, GATE_COLUMNS)] = jnp.dot(
        table, gates, preferred_element_type=F32
    ).astype(BF)


def pack(f_routes, b_routes, f_gates, b_gates, x, y):
    tokens, width = x.shape
    routes = jnp.concatenate([f_routes, b_routes])
    gates = jnp.concatenate([f_gates, b_gates]).astype(F32)
    return pl.pallas_call(
        pack_kernel,
        out_shape=jax.ShapeDtypeStruct((2 * tokens, width + GATE_COLUMNS), BF),
        in_specs=[VMEM] * 5,
        out_specs=VMEM,
        cost_estimate=pl.CostEstimate(
            flops=8 * tokens * tokens * width, bytes_accessed=8 * tokens * width, transcendentals=0
        ),
    )(routes.reshape(1, -1), routes, gates, x, y)


def unpack_kernel(r_row, r_col, slots, out):
    width = slots.shape[1]
    same, rows, cols = pair_mask(r_col[...], r_row[...], 1)
    slot = jnp.sum((same & (cols < rows)).astype(jnp.int32), axis=1, keepdims=True)
    table = (cols == r_col[...] * 8 + slot).astype(F32).astype(BF)
    for start in range(0, width, COLUMNS):
        at = pl.ds(start, COLUMNS)
        out[:, at] = jnp.dot(table, slots[:, at], preferred_element_type=F32).astype(BF)


def unpack(routes, slots):
    tokens, width = slots.shape
    return pl.pallas_call(
        unpack_kernel,
        out_shape=jax.ShapeDtypeStruct((tokens, width), BF),
        in_specs=[VMEM] * 3,
        out_specs=VMEM,
        cost_estimate=pl.CostEstimate(
            flops=2 * tokens * tokens * width, bytes_accessed=4 * tokens * width, transcendentals=0
        ),
    )(routes.reshape(1, -1), routes, slots)


def to_section(block, step):
    last, first, beside = (3, 0, 2) if step == 1 else (0, 3, 1)
    half = block.shape[0] // 2
    pairs = [(i, (i + step) % 8) for i in range(8)]
    axes = ("h", "y")
    straight = lax.ppermute(block[:half], axes, pairs)
    inside = lax.ppermute(block[half:], axes, [(a, b) for a, b in pairs if a // 4 == b // 4])
    away = lax.ppermute(block[half:], axes, [(4 * h + last, 4 * h + beside) for h in (0, 1)])
    across = lax.ppermute(away, axes, [(4 * h + beside, 4 * (1 - h) + first) for h in (0, 1)])
    rest = jnp.where(lax.axis_index("y") == first, across, inside)
    return jnp.concatenate([straight, rest])


def load_weights(refs, gate_up, down, sems):
    units = down.shape[1]
    copies = []
    for u in range(4):
        copies.append(pltpu.make_async_copy(refs[u], gate_up.at[u, :, pl.ds(0, units)], sems.at[u]))
        copies.append(
            pltpu.make_async_copy(refs[4 + u], gate_up.at[u, :, pl.ds(units, units)], sems.at[4 + u])
        )
        copies.append(pltpu.make_async_copy(refs[8 + u], down.at[u], sems.at[8 + u]))
    return copies


def forward_kernel(own, visiting, *refs):
    weights, (out_own, out_visiting, rows, gate_up, down, hidden, sems) = refs[:12], refs[12:]
    copies = load_weights(weights, gate_up, down, sems)
    for copy in copies:
        copy.start()
    half, width = out_own.shape
    units = down.shape[1]
    gates = [ref[:, pl.ds(width, GATE_COLUMNS)].astype(F32)[:, :1] for ref in (own, visiting)]
    rows[pl.ds(0, half), :] = own[:, pl.ds(0, width)]
    rows[pl.ds(half, half), :] = visiting[:, pl.ds(0, width)]
    for u in range(4):
        copies[3 * u].wait()
        copies[3 * u + 1].wait()
        pre = jnp.dot(rows[...], gate_up[u], preferred_element_type=F32)
        gate, up = pre[:, :units], pre[:, units:]
        hidden[u] = (gate * jax.nn.sigmoid(gate) * up).astype(BF)
    for u in range(4):
        copies[3 * u + 2].wait()
    for start in range(0, width, COLUMNS):
        at = pl.ds(start, COLUMNS)
        total = jnp.dot(hidden[0], down[0, :, at], preferred_element_type=F32)
        for u in range(1, 4):
            total = total + jnp.dot(hidden[u], down[u, :, at], preferred_element_type=F32)
        out_own[:, at] = own[:, at].astype(F32) + gates[0] * total[:half]
        out_visiting[:, at] = (gates[1] * total[half:]).astype(BF)


def backward_kernel(own, visiting, saved, *refs):
    weights, (out_own, out_visiting, rows, gate_up, down, grads, sems) = refs[:12], refs[12:]
    copies = load_weights(weights, gate_up, down, sems)
    for copy in copies:
        copy.start()
    half, width = out_own.shape
    units = down.shape[1]
    for at_row, ref in ((0, own), (half, visiting)):
        gate = ref[:, pl.ds(width, GATE_COLUMNS)].astype(F32)[:, :1]
        for start in range(0, width, COLUMNS):
            at = pl.ds(start, COLUMNS)
            rows[pl.ds(at_row, half), at] = (gate * ref[:, at].astype(F32)).astype(BF)
    for u in range(4):
        copies[3 * u + 2].wait()
        grad = lax.dot_general(rows[...], down[u], ROWS_T, preferred_element_type=F32)
        a, b = saved[u, 0].astype(F32), saved[u, 1].astype(F32)
        sig = jax.nn.sigmoid(a)
        grads[u, :, pl.ds(0, units)] = (grad * b * sig * (1.0 + a * (1.0 - sig))).astype(BF)
        grads[u, :, pl.ds(units, units)] = (grad * a * sig).astype(BF)
    for u in range(4):
        copies[3 * u].wait()
        copies[3 * u + 1].wait()
    for start in range(0, width, COLUMNS):
        at = pl.ds(start, COLUMNS)
        total = lax.dot_general(grads[0], gate_up[0, at, :], ROWS_T, preferred_element_type=F32)
        for u in range(1, 4):
            total = total + lax.dot_general(
                grads[u], gate_up[u, at, :], ROWS_T, preferred_element_type=F32
            )
        out_own[:, at] = own[:, at].astype(F32) + total[:half]
        out_visiting[:, at] = total[half:].astype(BF)


def expert_pass(kernel, own, visiting, extra, weights, middle):
    half, units = own.shape[0], weights[8].shape[0]
    width = own.shape[1] - GATE_COLUMNS
    rows, flops = 2 * half, 2 * 2 * half * width * 4 * units * 3
    return pl.pallas_call(
        kernel,
        out_shape=(
            jax.ShapeDtypeStruct((half, width), F32),
            jax.ShapeDtypeStruct((half, width), BF),
        ),
        in_specs=[VMEM] * (2 + len(extra)) + [pl.BlockSpec(memory_space=pl.ANY)] * 12,
        out_specs=(VMEM, VMEM),
        scratch_shapes=[
            pltpu.VMEM((rows, width), BF),
            pltpu.VMEM((4, width, 2 * units), BF),
            pltpu.VMEM((4, units, width), BF),
            pltpu.VMEM((4, rows, middle), BF),
            pltpu.SemaphoreType.DMA((12,)),
        ],
        compiler_params=pltpu.CompilerParams(vmem_limit_bytes=40 * 1024 * 1024),
        cost_estimate=pl.CostEstimate(
            flops=flops, bytes_accessed=12 * width * units * 2 + 5 * half * width * 2, transcendentals=0
        ),
    )(own, visiting, *extra, *weights)


def body(
    forward_state, grad_state, forward_routes, forward_gates, backward_routes, backward_gates,
    saved_preacts, gate_weight, up_weight, down_weight,
):
    x, y, saved = forward_state[0], grad_state[0], saved_preacts[0]
    width = x.shape[1]
    capacity, units = saved.shape[2], saved.shape[3]
    nz, nx, nc = lax.axis_size("z"), lax.axis_size("x"), lax.axis_size("c")
    packed = pack(
        forward_routes[0], backward_routes[0], forward_gates[0], backward_gates[0], x, y
    )
    arrived = exchange(packed.reshape(nz, 2 * capacity, packed.shape[1]))
    f_rows = arrived[:, :capacity].reshape(nz * capacity, -1)
    b_rows = arrived[:, capacity:].reshape(nz * capacity, -1)
    f_visiting, b_visiting = swap_rows_x(f_rows), swap_rows_x(b_rows)

    me_x, me_c = lax.axis_index("x"), lax.axis_index("c")
    by_place = saved.reshape(2, nz, nx, nc, capacity, units)

    def kept_for(at_x):
        rows_of = [
            lax.dynamic_index_in_dim(by_place, at, 2, keepdims=False) for at in (at_x, nx - 1 - at_x)
        ]
        return jnp.stack(rows_of, 1)

    here = jnp.stack([kept_for(me_x), swap_weights_x(kept_for(me_x ^ 1))])
    mine = lax.dynamic_index_in_dim(here, me_c, 4, keepdims=False)
    theirs = swap_core(lax.dynamic_index_in_dim(here, 1 - me_c, 4, keepdims=False))
    kept = jnp.stack([mine, theirs], 1).reshape(4, 2, 2 * nz * capacity, units)

    own_weights = (gate_weight[0], up_weight[0], down_weight[0])
    beside_weights = [swap_weights_x(mine) for mine in own_weights]
    f_visiting, beside_weights[2], kept = lax.optimization_barrier(
        (f_visiting, beside_weights[2], kept)
    )
    weights = []
    for mine, beside in zip(own_weights, beside_weights):
        weights += [mine, swap_core(mine), beside, swap_core(beside)]

    f_own, f_visited = expert_pass(forward_kernel, f_rows, f_visiting, (), weights, units)
    b_own, b_visited = expert_pass(
        backward_kernel, b_rows, b_visiting, (kept,), weights, 2 * units
    )
    f_out = (f_own + swap_rows_x(f_visited).astype(F32)).astype(BF)
    b_out = (b_own + swap_rows_x(b_visited).astype(F32)).astype(BF)
    f_back = exchange(f_out.reshape(nz, capacity, width)).reshape(-1, width)
    forward_next = to_section(unpack(forward_routes[0], f_back), 1)
    b_moved = to_section(b_out, -1)
    b_back = exchange(b_moved.reshape(nz, capacity, width)).reshape(-1, width)
    pairs = [(i, (i - 1) % 8) for i in range(8)]
    backward_next = unpack(lax.ppermute(backward_routes[0], ("h", "y"), pairs), b_back)
    return forward_next[None], backward_next[None]


def solution(mesh):
    pipes = mesh.shape["pipe"]
    fine = Mesh(mesh.devices.reshape(2, pipes // 2, 8, 4, 2), ("h", "y", "z", "x", "c"))
    pipe, expert = ("h", "y"), ("z", "x", "c")
    tokens = P(pipe, expert, None)
    return jax.shard_map(
        body,
        mesh=fine,
        in_specs=(
            tokens, tokens, tokens, tokens, tokens, tokens,
            P(pipe, None, None, None, expert),
            P(pipe, None, expert),
            P(pipe, None, expert),
            P(pipe, expert, None),
        ),
        out_specs=(tokens, tokens),
        check_vma=False,
    )
```

time: 265 us -> 245 us (0.925)
  the two profiles are of different devices: /device:TPU:24 before, /device:TPU:97 now
where the time goes in v3:
time: 245 us; the launch traced here: 244 us
  starting transfers between devices  105 us (43%)
  waiting for transfers between devices  105 us (43%)
  Pallas kernels  19.7 us (8%)
  local copies, waits for them, and re-layouts  8.51 us (3%)
  other arithmetic  4.09 us (2%)
    all_to_all x3, waiting for transfers between devices, exchange(): return lax.all_to_all(block, 'z', split_axis=0, concat_axis=0, tiled=True)  45.2 us
    ppermute x15, starting transfers between devices, permute(): return lax.ppermute(block, axis, list(enumerate(targets)))  43.4 us
    ppermute x2, waiting for transfers between devices, to_section(): straight = lax.ppermute(block[:half], axes, pairs)  34 us
    all_to_all x3, starting transfers between devices, exchange(): return lax.all_to_all(block, 'z', split_axis=0, concat_axis=0, tiled=True)  30.9 us
    ppermute x15, waiting for transfers between devices, permute(): return lax.ppermute(block, axis, list(enumerate(targets)))  21.8 us
    pallas_call x2, Pallas kernels, expert_pass(): pl.pallas_call(kernel, out_shape=(jax.ShapeDtypeStruct((half, width), F32...  12.1 us
    ppermute x1, starting transfers between devices, body(): lax.ppermute(backward_routes[0], ('h', 'y'), pairs)  11.6 us
    ppermute x2, starting transfers between devices, to_section(): straight = lax.ppermute(block[:half], axes, pairs)  10.9 us
  transfers between devices with their start and end apart: 27, of which 7 were waited for; matrix products, arithmetic and copies ran while one was open for 3% of the time, Pallas kernels for 6%

profile of v3, /device:TPU:97, one launch (start us, length us, event | category | flops | bytes accessed | tf_op | source)
XLA Modules:
  0.0 243.8 jit_solution(16071825867250266905)
XLA Ops:
  4.3 3.0 %shard_map.113 = bf16[128,3712]{1,0:T(8,128)(2,1)} custom-call(s32[1,128]{1,0:T(1,128)} %fusion.5.r_row, s32[128,1]{1,0:T(8,128)} %copy.40.r_col, f32[128,1]{1,0:T(8,128)} %copy.41.gate_col, bf16[64,3584]{1,0:T(8,128)(2,1)} %bitcast.65, bf16[64,3584]{1,0:T(8,128)(2,1)} %bitcast.66), custom_call_target="tpu_custom_call" | custom-call | flops 117440512 | bytes 1835008 | tf_op jit(solution)/shard_map/pallas_call | solution.py:68
  7.3 11.3 %all-to-all-start = ((bf16[8,16,3712]{2,1,0:T(8,128)(2,1)}), bf16[8,16,3712]{2,1,0:T(8,128)(2,1)}, u32[]{:S(2)}, u32[]{:S(2)}) async-start(bf16[8,16,3712]{2,1,0:T(8,128)(2,1)} %bitcast.60), calls=%async_computation | async-start | bytes 1900544 | tf_op jit(solution)/shard_map/all_to_all | solution.py:33
  18.7 3.1 %collective-permute-start.2 = (bf16[2,2,8,2,8,128]{5,4,3,2,0,1:T(8,128)(2,1)S(1)}, bf16[2,2,8,2,8,128]{5,4,3,2,0,1:T(8,128)(2,1)S(1)}, u32[]{:S(2)}, u32[]{:S(2)}) collective-permute-start(bf16[2,2,8,2,8,128]{5,4,3,2,0,1:T(8,128)(2,1)S(1)} %pad_maximum_fusion.1), channel_id=1, source_target_pairs={{0,2},{2,0},{4,6},{6,4},{1,3},{3,1},{5,7},{7,5},{8,10},{10,8},{12,... | collective-permute-start | bytes 393224 | tf_op jit(solution)/shard_map/ppermute | solution.py:17
  21.8 3.4 %collective-permute-start.4 = (bf16[3584,128]{1,0:T(8,128)(2,1)S(1)}, bf16[3584,128]{1,0:T(8,128)(2,1)}, u32[]{:S(2)}, u32[]{:S(2)}) collective-permute-start(bf16[3584,128]{1,0:T(8,128)(2,1)S(1)} %bitcast.47), channel_id=1, source_target_pairs={{0,1},{1,0},{2,3},{3,2},{4,5},{5,4},{6,7},{7,6},{8,9},{9,8},{10,11... | collective-permute-start | bytes 2752520 | tf_op jit(solution)/shard_map/ppermute | solution.py:17
  25.2 2.2 collective-permute-start.5
  27.4 3.1 %collective-permute-start.1 = (bf16[128,3584]{1,0:T(8,128)(2,1)S(1)}, bf16[128,3584]{1,0:T(8,128)(2,1)}, u32[]{:S(2)}, u32[]{:S(2)}) collective-permute-start(bf16[128,3584]{1,0:T(8,128)(2,1)S(1)} %bitcast.55), channel_id=1, source_target_pairs={{0,2},{2,0},{4,6},{6,4},{1,3},{3,1},{5,7},{7,5},{8,10},{10,8},{12,... | collective-permute-start | bytes 2752520 | tf_op jit(solution)/shard_map/ppermute | solution.py:17
  30.6 2.2 collective-permute-start.8
  32.8 2.8 %collective-permute-start.3 = (bf16[2,2,2,8,8,128]{5,4,3,2,1,0:T(8,128)(2,1)S(1)}, bf16[2,2,2,8,8,128]{5,4,3,2,1,0:T(8,128)(2,1)S(1)}, u32[]{:S(2)}, u32[]{:S(2)}) collective-permute-start(bf16[2,2,2,8,8,128]{5,4,3,2,1,0:T(8,128)(2,1)S(1)} %bitcast.68), channel_id=1, source_target_pairs={{0,1},{1,0},{2,3},{3,2},{4,5},{5,4},{6,7},{7,6},{8,9},{9,8},{10,11... | collective-permute-start | bytes 393224 | tf_op jit(solution)/shard_map/ppermute | solution.py:17
  35.6 24.2 %all-to-all-done = bf16[8,16,3712]{2,1,0:T(8,128)(2,1)} async-done(((bf16[8,16,3712]{2,1,0:T(8,128)(2,1)}), bf16[8,16,3712]{2,1,0:T(8,128)(2,1)}, u32[]{:S(2)}, u32[]{:S(2)}) %all-to-all-start) | async-done | bytes 950304 | tf_op jit(solution)/shard_map/all_to_all | solution.py:33
  61.1 4.4 %collective-permute-start = (bf16[64,3712]{1,0:T(8,128)(2,1)S(1)}, bf16[64,3712]{1,0:T(8,128)(2,1)S(1)}, u32[]{:S(2)}, u32[]{:S(2)}) collective-permute-start(bf16[64,3712]{1,0:T(8,128)(2,1)S(1)} %get-tuple-element.17.own), channel_id=1, source_target_pairs={{0,6},{2,4},{4,2},{6,0},{1,7},{3,5},{5,3},{7,1},{8,14},{10,12},{12... | collective-permute-start | bytes 1425416 | tf_op jit(solution)/shard_map/ppermute | solution.py:17
  65.5 3.4 %collective-permute-done.1.refs_10_ = bf16[128,3584]{1,0:T(8,128)(2,1)} collective-permute-done((bf16[128,3584]{1,0:T(8,128)(2,1)S(1)}, bf16[128,3584]{1,0:T(8,128)(2,1)}, u32[]{:S(2)}, u32[]{:S(2)}) %collective-permute-start.1) | collective-permute-done | bytes 917536 | tf_op jit(solution)/shard_map/ppermute | solution.py:17
  68.9 3.1 %collective-permute-start.7 = (bf16[3584,128]{1,0:T(8,128)(2,1)S(1)}, bf16[3584,128]{1,0:T(8,128)(2,1)S(1)}, u32[]{:S(2)}, u32[]{:S(2)}) collective-permute-start(bf16[3584,128]{1,0:T(8,128)(2,1)S(1)} %bitcast.52), channel_id=1, source_target_pairs={{0,1},{1,0},{2,3},{3,2},{4,5},{5,4},{6,7},{7,6},{8,9},{9,8},{10,11... | collective-permute-start | bytes 2752520 | tf_op jit(solution)/shard_map/ppermute | solution.py:17
  72.0 1.9 collective-permute-start.10
  74.0 14.6 %collective-permute-done.8.refs_6_ = bf16[3584,128]{1,0:T(8,128)(2,1)} collective-permute-done((bf16[3584,128]{1,0:T(8,128)(2,1)S(1)}, bf16[3584,128]{1,0:T(8,128)(2,1)}, u32[]{:S(2)}, u32[]{:S(2)}) %collective-permute-start.8) | collective-permute-done | bytes 917536 | tf_op jit(solution)/shard_map/ppermute | solution.py:17
  88.5 2.7 %collective-permute-start.6 = (bf16[3584,128]{1,0:T(8,128)(2,1)}, bf16[3584,128]{1,0:T(8,128)(2,1)S(1)}, u32[]{:S(2)}, u32[]{:S(2)}) collective-permute-start(bf16[3584,128]{1,0:T(8,128)(2,1)} %collective-permute-done.5.refs_2_), channel_id=1, source_target_pairs={{0,1},{1,0},{2,3},{3,2},{4,5},{5,4},{6,7},{7,6},{8,9},{9,8},{10,11... | collective-permute-start | bytes 2752520 | tf_op jit(solution)/shard_map/ppermute | solution.py:17
  93.2 2.4 collective-permute-start.11
  95.6 3.7 %collective-permute-start.18 = (bf16[64,3712]{1,0:T(8,128)(2,1)S(1)}, bf16[64,3712]{1,0:T(8,128)(2,1)S(1)}, u32[]{:S(2)}, u32[]{:S(2)}) collective-permute-start(bf16[64,3712]{1,0:T(8,128)(2,1)S(1)} %get-tuple-element.16.own), channel_id=1, source_target_pairs={{0,6},{2,4},{4,2},{6,0},{1,7},{3,5},{5,3},{7,1},{8,14},{10,12},{12... | collective-permute-start | bytes 1425416 | tf_op jit(solution)/shard_map/ppermute | solution.py:17
  99.4 5.3 %shard_map.114 = (f32[64,3584]{1,0:T(8,128)S(1)}, bf16[64,3584]{1,0:T(8,128)(2,1)S(1)}) custom-call(bf16[64,3712]{1,0:T(8,128)(2,1)S(1)} %get-tuple-element.17.own, bf16[64,3712]{1,0:T(8,128)(2,1)S(1)} %collective-permute-done.visiting, bf16[3584,128]{1,0:T(8,128)(2,1)S(1)} %bitcast.49, bf16[3584,128]{1,0:T(8,128)(2,1)} %collective-permute-done.4.refs_1_, ...), custom_call_target="tpu_custom_call" | custom-call | flops 1409286144 | bytes 13303808 | tf_op jit(solution)/shard_map/pallas_call | solution.py:191
  104.7 2.8 %collective-permute-start.12 = (bf16[64,3584]{1,0:T(8,128)(2,1)S(1)}, bf16[64,3584]{1,0:T(8,128)(2,1)S(1)}, u32[]{:S(2)}, u32[]{:S(2)}) collective-permute-start(bf16[64,3584]{1,0:T(8,128)(2,1)S(1)} %get-tuple-element.12), channel_id=1, source_target_pairs={{0,6},{2,4},{4,2},{6,0},{1,7},{3,5},{5,3},{7,1},{8,14},{10,12},{12... | collective-permute-start | bytes 1376264 | tf_op jit(solution)/shard_map/ppermute | solution.py:17
  107.4 3.8 %collective-permute-done.18.visiting = bf16[64,3712]{1,0:T(8,128)(2,1)S(1)} collective-permute-done((bf16[64,3712]{1,0:T(8,128)(2,1)S(1)}, bf16[64,3712]{1,0:T(8,128)(2,1)S(1)}, u32[]{:S(2)}, u32[]{:S(2)}) %collective-permute-start.18) | collective-permute-done | bytes 475168 | tf_op jit(solution)/shard_map/ppermute | solution.py:17
  111.2 6.8 %shard_map.116 = (f32[64,3584]{1,0:T(8,128)S(1)}, bf16[64,3584]{1,0:T(8,128)(2,1)S(1)}) custom-call(bf16[64,3712]{1,0:T(8,128)(2,1)S(1)} %get-tuple-element.16.own, bf16[64,3712]{1,0:T(8,128)(2,1)S(1)} %collective-permute-done.18.visiting, bf16[4,2,128,128]{3,2,1,0:T(8,128)(2,1)S(1)} %bitcast.59, bf16[3584,128]{1,0:T(8,128)(2,1)S(1)} %bitcast.50, ...), custom_call_target="tpu_custom_call" | custom-call | flops 1409286144 | bytes 13303808 | tf_op jit(solution)/shard_map/pallas_call | solution.py:191
  118.9 3.7 %collective-permute-start.19 = (bf16[64,3584]{1,0:T(8,128)(2,1)S(1)}, bf16[64,3584]{1,0:T(8,128)(2,1)S(1)}, u32[]{:S(2)}, u32[]{:S(2)}) collective-permute-start(bf16[64,3584]{1,0:T(8,128)(2,1)S(1)} %get-tuple-element.15), channel_id=1, source_target_pairs={{0,6},{2,4},{4,2},{6,0},{1,7},{3,5},{5,3},{7,1},{8,14},{10,12},{12... | collective-permute-start | bytes 1376264 | tf_op jit(solution)/shard_map/ppermute | solution.py:17
  123.5 9.5 %all-to-all-start.1 = ((bf16[8,8,3584]{2,1,0:T(8,128)(2,1)}), bf16[8,8,3584]{2,1,0:T(8,128)(2,1)S(1)}, u32[]{:S(2)}, u32[]{:S(2)}) async-start(bf16[8,8,3584]{2,1,0:T(8,128)(2,1)} %fusion), calls=%async_computation.1 | async-start | bytes 917504 | tf_op jit(solution)/shard_map/all_to_all | solution.py:33
  133.1 3.2 %collective-permute-start.21 = (bf16[32,3584]{1,0:T(8,128)(2,1)S(1)}, bf16[32,3584]{1,0:T(8,128)(2,1)S(1)}, u32[]{:S(2)}, u32[]{:S(2)}) collective-permute-start(bf16[32,3584]{1,0:T(8,128)(2,1)S(1)} %get-tuple-element.19), channel_id=1, source_target_pairs={{0,64},{256,320},{1,65},{257,321},{2,66},{258,322},{3,67},{259,323... | collective-permute-start | bytes 688136 | tf_op jit(solution)/shard_map/ppermute | solution.py:109
  138.3 9.0 %collective-permute-start.20 = (bf16[32,3584]{1,0:T(8,128)(2,1)S(1)}, bf16[32,3584]{1,0:T(8,128)(2,1)S(1)}, u32[]{:S(2)}, u32[]{:S(2)}) collective-permute-start(bf16[32,3584]{1,0:T(8,128)(2,1)S(1)} %get-tuple-element.18), channel_id=1, source_target_pairs={{0,448},{64,0},{128,64},{192,128},{256,192},{320,256},{384,320},{4... | collective-permute-start | bytes 688136 | tf_op jit(solution)/shard_map/ppermute | solution.py:107
  148.0 21.0 %all-to-all-done.1 = bf16[8,8,3584]{2,1,0:T(8,128)(2,1)S(1)} async-done(((bf16[8,8,3584]{2,1,0:T(8,128)(2,1)}), bf16[8,8,3584]{2,1,0:T(8,128)(2,1)S(1)}, u32[]{:S(2)}, u32[]{:S(2)}) %all-to-all-start.1) | async-done | bytes 458784 | tf_op jit(solution)/shard_map/all_to_all | solution.py:33
  169.8 2.3 shard_map.115
  177.3 10.2 %all-to-all-start.2 = ((bf16[8,8,3584]{2,1,0:T(8,128)(2,1)}), bf16[8,8,3584]{2,1,0:T(8,128)(2,1)S(1)}, u32[]{:S(2)}, u32[]{:S(2)}) async-start(bf16[8,8,3584]{2,1,0:T(8,128)(2,1)} %maximum_bitcast_fusion.1), calls=%async_computation.2 | async-start | bytes 917504 | tf_op jit(solution)/shard_map/all_to_all | solution.py:33
  187.6 11.6 %collective-permute-start.17 = (s32[64,1]{1,0:T(8,128)S(1)}, s32[64,1]{1,0:T(8,128)S(1)}, u32[]{:S(2)}, u32[]{:S(2)}) collective-permute-start(s32[64,1]{1,0:T(8,128)S(1)} %copy.46), channel_id=1, source_target_pairs={{0,448},{64,0},{128,64},{192,128},{256,192},{320,256},{384,320},{4... | collective-permute-start | bytes 776 | tf_op jit(solution)/shard_map/ppermute | solution.py:263
  199.2 4.2 %collective-permute-done.17.r_col = s32[64,1]{1,0:T(8,128)S(1)} collective-permute-done((s32[64,1]{1,0:T(8,128)S(1)}, s32[64,1]{1,0:T(8,128)S(1)}, u32[]{:S(2)}, u32[]{:S(2)}) %collective-permute-start.17) | collective-permute-done | bytes 288 | tf_op jit(solution)/shard_map/ppermute | solution.py:263
  206.0 34.0 %collective-permute-done.13 = bf16[32,3584]{1,0:T(8,128)(2,1)S(1)} collective-permute-done((bf16[32,3584]{1,0:T(8,128)(2,1)S(1)}, bf16[32,3584]{1,0:T(8,128)(2,1)S(1)}, u32[]{:S(2)}, u32[]{:S(2)}) %collective-permute-start.13) | collective-permute-done | bytes 229408 | tf_op jit(solution)/shard_map/ppermute | solution.py:107
  241.5 2.3 shard_map.117
  (78 shorter events, 21.7 us)
Async XLA Ops:
  4.3 14.4 %copy-start.7 = (bf16[1,2,64,8,128]{4,3,2,1,0:T(8,128)(2,1)S(1)}, bf16[1,2,64,8,128]{4,3,2,1,0:T(8,128)(2,1)}, u32[]{:S(2)}) copy-start(bf16[1,2,64,8,128]{4,3,2,1,0:T(8,128)(2,1)} %param.16) | copy-start | bytes 786436
  4.3 23.2 %copy-start.2 = (bf16[1,128,3584]{2,1,0:T(8,128)(2,1)S(1)}, bf16[1,128,3584]{2,1,0:T(8,128)(2,1)}, u32[]{:S(2)}) copy-start(bf16[1,128,3584]{2,1,0:T(8,128)(2,1)} %param.19) | copy-start | bytes 2752516
  7.3 14.5 %copy-start = (bf16[1,3584,128]{2,1,0:T(8,128)(2,1)S(1)}, bf16[1,3584,128]{2,1,0:T(8,128)(2,1)}, u32[]{:S(2)}) copy-start(bf16[1,3584,128]{2,1,0:T(8,128)(2,1)} %param.17) | copy-start | bytes 2752516
  7.3 23.2 %copy-start.1 = (bf16[1,3584,128]{2,1,0:T(8,128)(2,1)S(1)}, bf16[1,3584,128]{2,1,0:T(8,128)(2,1)}, u32[]{:S(2)}) copy-start(bf16[1,3584,128]{2,1,0:T(8,128)(2,1)} %param.18) | copy-start | bytes 2752516
  7.3 52.5 %all-to-all-start = ((bf16[8,16,3712]{2,1,0:T(8,128)(2,1)}), bf16[8,16,3712]{2,1,0:T(8,128)(2,1)}, u32[]{:S(2)}, u32[]{:S(2)}) async-start(bf16[8,16,3712]{2,1,0:T(8,128)(2,1)} %bitcast.60), calls=%async_computation | async-start | bytes 1900544 | tf_op jit(solution)/shard_map/all_to_all | solution.py:33
  18.7 14.1 %collective-permute-start.2 = (bf16[2,2,8,2,8,128]{5,4,3,2,0,1:T(8,128)(2,1)S(1)}, bf16[2,2,8,2,8,128]{5,4,3,2,0,1:T(8,128)(2,1)S(1)}, u32[]{:S(2)}, u32[]{:S(2)}) collective-permute-start(bf16[2,2,8,2,8,128]{5,4,3,2,0,1:T(8,128)(2,1)S(1)} %pad_maximum_fusion.1), channel_id=1, source_target_pairs={{0,2},{2,0},{4,6},{6,4},{1,3},{3,1},{5,7},{7,5},{8,10},{10,8},{12,... | collective-permute-start | bytes 393224 | tf_op jit(solution)/shard_map/ppermute | solution.py:17
  21.8 71.4 %collective-permute-start.4 = (bf16[3584,128]{1,0:T(8,128)(2,1)S(1)}, bf16[3584,128]{1,0:T(8,128)(2,1)}, u32[]{:S(2)}, u32[]{:S(2)}) collective-permute-start(bf16[3584,128]{1,0:T(8,128)(2,1)S(1)} %bitcast.47), channel_id=1, source_target_pairs={{0,1},{1,0},{2,3},{3,2},{4,5},{5,4},{6,7},{7,6},{8,9},{9,8},{10,11... | collective-permute-start | bytes 2752520 | tf_op jit(solution)/shard_map/ppermute | solution.py:17
  25.2 46.8 %collective-permute-start.5 = (bf16[3584,128]{1,0:T(8,128)(2,1)S(1)}, bf16[3584,128]{1,0:T(8,128)(2,1)}, u32[]{:S(2)}, u32[]{:S(2)}) collective-permute-start(bf16[3584,128]{1,0:T(8,128)(2,1)S(1)} %bitcast.48), channel_id=1, source_target_pairs={{0,2},{2,0},{4,6},{6,4},{1,3},{3,1},{5,7},{7,5},{8,10},{10,8},{12,... | collective-permute-start | bytes 2752520 | tf_op jit(solution)/shard_map/ppermute | solution.py:17
  27.4 41.5 %collective-permute-start.1 = (bf16[128,3584]{1,0:T(8,128)(2,1)S(1)}, bf16[128,3584]{1,0:T(8,128)(2,1)}, u32[]{:S(2)}, u32[]{:S(2)}) collective-permute-start(bf16[128,3584]{1,0:T(8,128)(2,1)S(1)} %bitcast.55), channel_id=1, source_target_pairs={{0,2},{2,0},{4,6},{6,4},{1,3},{3,1},{5,7},{7,5},{8,10},{10,8},{12,... | collective-permute-start | bytes 2752520 | tf_op jit(solution)/shard_map/ppermute | solution.py:17
  30.6 58.0 %collective-permute-start.8 = (bf16[3584,128]{1,0:T(8,128)(2,1)S(1)}, bf16[3584,128]{1,0:T(8,128)(2,1)}, u32[]{:S(2)}, u32[]{:S(2)}) collective-permute-start(bf16[3584,128]{1,0:T(8,128)(2,1)S(1)} %bitcast.51), channel_id=1, source_target_pairs={{0,2},{2,0},{4,6},{6,4},{1,3},{3,1},{5,7},{7,5},{8,10},{10,8},{12,... | collective-permute-start | bytes 2752520 | tf_op jit(solution)/shard_map/ppermute | solution.py:17
  32.8 28.2 %collective-permute-start.3 = (bf16[2,2,2,8,8,128]{5,4,3,2,1,0:T(8,128)(2,1)S(1)}, bf16[2,2,2,8,8,128]{5,4,3,2,1,0:T(8,128)(2,1)S(1)}, u32[]{:S(2)}, u32[]{:S(2)}) collective-permute-start(bf16[2,2,2,8,8,128]{5,4,3,2,1,0:T(8,128)(2,1)S(1)} %bitcast.68), channel_id=1, source_target_pairs={{0,1},{1,0},{2,3},{3,2},{4,5},{5,4},{6,7},{7,6},{8,9},{9,8},{10,11... | collective-permute-start | bytes 393224 | tf_op jit(solution)/shard_map/ppermute | solution.py:17
  61.1 30.2 %collective-permute-start = (bf16[64,3712]{1,0:T(8,128)(2,1)S(1)}, bf16[64,3712]{1,0:T(8,128)(2,1)S(1)}, u32[]{:S(2)}, u32[]{:S(2)}) collective-permute-start(bf16[64,3712]{1,0:T(8,128)(2,1)S(1)} %get-tuple-element.17.own), channel_id=1, source_target_pairs={{0,6},{2,4},{4,2},{6,0},{1,7},{3,5},{5,3},{7,1},{8,14},{10,12},{12... | collective-permute-start | bytes 1425416 | tf_op jit(solution)/shard_map/ppermute | solution.py:17
  68.9 26.7 %collective-permute-start.7 = (bf16[3584,128]{1,0:T(8,128)(2,1)S(1)}, bf16[3584,128]{1,0:T(8,128)(2,1)S(1)}, u32[]{:S(2)}, u32[]{:S(2)}) collective-permute-start(bf16[3584,128]{1,0:T(8,128)(2,1)S(1)} %bitcast.52), channel_id=1, source_target_pairs={{0,1},{1,0},{2,3},{3,2},{4,5},{5,4},{6,7},{7,6},{8,9},{9,8},{10,11... | collective-permute-start | bytes 2752520 | tf_op jit(solution)/shard_map/ppermute | solution.py:17
  72.0 27.3 %collective-permute-start.10 = (bf16[128,3584]{1,0:T(8,128)(2,1)S(1)}, bf16[128,3584]{1,0:T(8,128)(2,1)S(1)}, u32[]{:S(2)}, u32[]{:S(2)}) collective-permute-start(bf16[128,3584]{1,0:T(8,128)(2,1)S(1)} %bitcast.56), channel_id=1, source_target_pairs={{0,1},{1,0},{2,3},{3,2},{4,5},{5,4},{6,7},{7,6},{8,9},{9,8},{10,11... | collective-permute-start | bytes 2752520 | tf_op jit(solution)/shard_map/ppermute | solution.py:17
  88.5 10.8 %collective-permute-start.6 = (bf16[3584,128]{1,0:T(8,128)(2,1)}, bf16[3584,128]{1,0:T(8,128)(2,1)S(1)}, u32[]{:S(2)}, u32[]{:S(2)}) collective-permute-start(bf16[3584,128]{1,0:T(8,128)(2,1)} %collective-permute-done.5.refs_2_), channel_id=1, source_target_pairs={{0,1},{1,0},{2,3},{3,2},{4,5},{5,4},{6,7},{7,6},{8,9},{9,8},{10,11... | collective-permute-start | bytes 2752520 | tf_op jit(solution)/shard_map/ppermute | solution.py:17
  91.3 8.1 %collective-permute-start.9 = (bf16[3584,128]{1,0:T(8,128)(2,1)}, bf16[3584,128]{1,0:T(8,128)(2,1)S(1)}, u32[]{:S(2)}, u32[]{:S(2)}) collective-permute-start(bf16[3584,128]{1,0:T(8,128)(2,1)} %collective-permute-done.8.refs_6_), channel_id=1, source_target_pairs={{0,1},{1,0},{2,3},{3,2},{4,5},{5,4},{6,7},{7,6},{8,9},{9,8},{10,11... | collective-permute-start | bytes 2752520 | tf_op jit(solution)/shard_map/ppermute | solution.py:17
  93.2 6.2 %collective-permute-start.11 = (bf16[128,3584]{1,0:T(8,128)(2,1)}, bf16[128,3584]{1,0:T(8,128)(2,1)S(1)}, u32[]{:S(2)}, u32[]{:S(2)}) collective-permute-start(bf16[128,3584]{1,0:T(8,128)(2,1)} %collective-permute-done.1.refs_10_), channel_id=1, source_target_pairs={{0,1},{1,0},{2,3},{3,2},{4,5},{5,4},{6,7},{7,6},{8,9},{9,8},{10,11... | collective-permute-start | bytes 2752520 | tf_op jit(solution)/shard_map/ppermute | solution.py:17
  95.6 15.6 %collective-permute-start.18 = (bf16[64,3712]{1,0:T(8,128)(2,1)S(1)}, bf16[64,3712]{1,0:T(8,128)(2,1)S(1)}, u32[]{:S(2)}, u32[]{:S(2)}) collective-permute-start(bf16[64,3712]{1,0:T(8,128)(2,1)S(1)} %get-tuple-element.16.own), channel_id=1, source_target_pairs={{0,6},{2,4},{4,2},{6,0},{1,7},{3,5},{5,3},{7,1},{8,14},{10,12},{12... | collective-permute-start | bytes 1425416 | tf_op jit(solution)/shard_map/ppermute | solution.py:17
  104.7 18.0 %collective-permute-start.12 = (bf16[64,3584]{1,0:T(8,128)(2,1)S(1)}, bf16[64,3584]{1,0:T(8,128)(2,1)S(1)}, u32[]{:S(2)}, u32[]{:S(2)}) collective-permute-start(bf16[64,3584]{1,0:T(8,128)(2,1)S(1)} %get-tuple-element.12), channel_id=1, source_target_pairs={{0,6},{2,4},{4,2},{6,0},{1,7},{3,5},{5,3},{7,1},{8,14},{10,12},{12... | collective-permute-start | bytes 1376264 | tf_op jit(solution)/shard_map/ppermute | solution.py:17
  118.9 14.1 %collective-permute-start.19 = (bf16[64,3584]{1,0:T(8,128)(2,1)S(1)}, bf16[64,3584]{1,0:T(8,128)(2,1)S(1)}, u32[]{:S(2)}, u32[]{:S(2)}) collective-permute-start(bf16[64,3584]{1,0:T(8,128)(2,1)S(1)} %get-tuple-element.15), channel_id=1, source_target_pairs={{0,6},{2,4},{4,2},{6,0},{1,7},{3,5},{5,3},{7,1},{8,14},{10,12},{12... | collective-permute-start | bytes 1376264 | tf_op jit(solution)/shard_map/ppermute | solution.py:17
  123.5 9.5 %copy-start.4 = (f32[64,3584]{1,0:T(8,128)S(1)}, f32[64,3584]{1,0:T(8,128)}, u32[]{:S(2)}) copy-start(f32[64,3584]{1,0:T(8,128)} %copy-done.3) | copy-start | bytes 2752516
  123.5 45.5 %all-to-all-start.1 = ((bf16[8,8,3584]{2,1,0:T(8,128)(2,1)}), bf16[8,8,3584]{2,1,0:T(8,128)(2,1)S(1)}, u32[]{:S(2)}, u32[]{:S(2)}) async-start(bf16[8,8,3584]{2,1,0:T(8,128)(2,1)} %fusion), calls=%async_computation.1 | async-start | bytes 917504 | tf_op jit(solution)/shard_map/all_to_all | solution.py:33
  133.1 14.2 %collective-permute-start.21 = (bf16[32,3584]{1,0:T(8,128)(2,1)S(1)}, bf16[32,3584]{1,0:T(8,128)(2,1)S(1)}, u32[]{:S(2)}, u32[]{:S(2)}) collective-permute-start(bf16[32,3584]{1,0:T(8,128)(2,1)S(1)} %get-tuple-element.19), channel_id=1, source_target_pairs={{0,64},{256,320},{1,65},{257,321},{2,66},{258,322},{3,67},{259,323... | collective-permute-start | bytes 688136 | tf_op jit(solution)/shard_map/ppermute | solution.py:109
  137.1 36.8 %collective-permute-start.23 = (bf16[32,3584]{1,0:T(8,128)(2,1)S(1)}, bf16[32,3584]{1,0:T(8,128)(2,1)S(1)}, u32[]{:S(2)}, u32[]{:S(2)}) collective-permute-start(bf16[32,3584]{1,0:T(8,128)(2,1)S(1)} %get-tuple-element.19), channel_id=1, source_target_pairs={{64,0},{128,64},{192,128},{320,256},{384,320},{448,384},{65,1},{12... | collective-permute-start | bytes 688136 | tf_op jit(solution)/shard_map/ppermute | solution.py:108
  138.3 38.2 %collective-permute-start.20 = (bf16[32,3584]{1,0:T(8,128)(2,1)S(1)}, bf16[32,3584]{1,0:T(8,128)(2,1)S(1)}, u32[]{:S(2)}, u32[]{:S(2)}) collective-permute-start(bf16[32,3584]{1,0:T(8,128)(2,1)S(1)} %get-tuple-element.18), channel_id=1, source_target_pairs={{0,448},{64,0},{128,64},{192,128},{256,192},{320,256},{384,320},{4... | collective-permute-start | bytes 688136 | tf_op jit(solution)/shard_map/ppermute | solution.py:107
  147.3 26.5 %collective-permute-start.22 = (bf16[32,3584]{1,0:T(8,128)(2,1)S(1)}, bf16[32,3584]{1,0:T(8,128)(2,1)S(1)}, u32[]{:S(2)}, u32[]{:S(2)}) collective-permute-start(bf16[32,3584]{1,0:T(8,128)(2,1)S(1)} %collective-permute-done.21), channel_id=1, source_target_pairs={{64,448},{320,192},{65,449},{321,193},{66,450},{322,194},{67,451},... | collective-permute-start | bytes 688136 | tf_op jit(solution)/shard_map/ppermute | solution.py:110
  173.1 2.1 collective-permute-start.14
  173.9 32.0 %collective-permute-start.16 = (bf16[32,3584]{1,0:T(8,128)(2,1)S(1)}, bf16[32,3584]{1,0:T(8,128)(2,1)S(1)}, u32[]{:S(2)}, u32[]{:S(2)}) collective-permute-start(bf16[32,3584]{1,0:T(8,128)(2,1)S(1)} %get-tuple-element.21), channel_id=1, source_target_pairs={{0,64},{64,128},{128,192},{256,320},{320,384},{384,448},{1,65},{65... | collective-permute-start | bytes 688136 | tf_op jit(solution)/shard_map/ppermute | solution.py:108
  175.2 30.7 %collective-permute-start.15 = (bf16[32,3584]{1,0:T(8,128)(2,1)S(1)}, bf16[32,3584]{1,0:T(8,128)(2,1)S(1)}, u32[]{:S(2)}, u32[]{:S(2)}) collective-permute-start(bf16[32,3584]{1,0:T(8,128)(2,1)S(1)} %collective-permute-done.14), channel_id=1, source_target_pairs={{128,256},{384,0},{129,257},{385,1},{130,258},{386,2},{131,259},{3... | collective-permute-start | bytes 688136 | tf_op jit(solution)/shard_map/ppermute | solution.py:110
  177.3 63.4 %all-to-all-start.2 = ((bf16[8,8,3584]{2,1,0:T(8,128)(2,1)}), bf16[8,8,3584]{2,1,0:T(8,128)(2,1)S(1)}, u32[]{:S(2)}, u32[]{:S(2)}) async-start(bf16[8,8,3584]{2,1,0:T(8,128)(2,1)} %maximum_bitcast_fusion.1), calls=%async_computation.2 | async-start | bytes 917504 | tf_op jit(solution)/shard_map/all_to_all | solution.py:33
  187.6 15.8 %collective-permute-start.17 = (s32[64,1]{1,0:T(8,128)S(1)}, s32[64,1]{1,0:T(8,128)S(1)}, u32[]{:S(2)}, u32[]{:S(2)}) collective-permute-start(s32[64,1]{1,0:T(8,128)S(1)} %copy.46), channel_id=1, source_target_pairs={{0,448},{64,0},{128,64},{192,128},{256,192},{320,256},{384,320},{4... | collective-permute-start | bytes 776 | tf_op jit(solution)/shard_map/ppermute | solution.py:263
  204.0 36.0 %collective-permute-start.13 = (bf16[32,3584]{1,0:T(8,128)(2,1)S(1)}, bf16[32,3584]{1,0:T(8,128)(2,1)S(1)}, u32[]{:S(2)}, u32[]{:S(2)}) collective-permute-start(bf16[32,3584]{1,0:T(8,128)(2,1)S(1)} %get-tuple-element.20), channel_id=1, source_target_pairs={{0,64},{64,128},{128,192},{192,256},{256,320},{320,384},{384,448},... | collective-permute-start | bytes 688136 | tf_op jit(solution)/shard_map/ppermute | solution.py:107
  (8 other events, 7.7 us)

commit v4 on v2

v4 whole, which is shorter than its diff:
```python
import jax
import jax.numpy as jnp
from jax import lax
from jax.experimental import pallas as pl
from jax.experimental.pallas import tpu as pltpu
from jax.sharding import Mesh, PartitionSpec as P

BF = jnp.bfloat16
F32 = jnp.float32
ROWS_T = (((1,), (1,)), ((), ()))
COLUMNS = 512
QUARTERS = 4
GATE_COLUMNS = 128
VMEM = pl.BlockSpec(memory_space=pltpu.VMEM)


def permute(block, axis, targets):
    return lax.ppermute(block, axis, list(enumerate(targets)))


def swap_core(block):
    return permute(block, "c", (1, 0))


def swap_weights(block):
    targets = [((x ^ (1 + 2 * c)) * 2 + c) for x in range(4) for c in range(2)]
    return permute(block, ("x", "c"), targets)


def swap_rows(block):
    return permute(block, "x", (2, 3, 0, 1))


def exchange(block):
    return lax.all_to_all(block, "z", split_axis=0, concat_axis=0, tiled=True)


def order_of(routes_row):
    tokens = routes_row.shape[1]
    rows = jax.lax.broadcasted_iota(jnp.int32, (tokens, tokens), 0)
    cols = jax.lax.broadcasted_iota(jnp.int32, (tokens, tokens), 1)
    column = jnp.sum(jnp.where(rows == cols, routes_row, 0), axis=1, keepdims=True)
    same = (column == routes_row).astype(jnp.int32)
    slot_row = jnp.sum(jnp.where(rows < cols, same, 0), axis=0, keepdims=True)
    slot_column = jnp.sum(jnp.where(cols < rows, same, 0), axis=1, keepdims=True)
    return column, slot_column, slot_row, rows, cols


def pack_kernel(f_routes, b_routes, f_gates, b_gates, x, y, out):
    tokens, width = x.shape
    tables, gates = [], []
    for number, (routes, gate) in enumerate(((f_routes, f_gates), (b_routes, b_gates))):
        routes_row, gate_row = routes[...], gate[...].astype(F32)
        _, _, slot_row, rows, cols = order_of(routes_row)
        key = routes_row * 16 + number * 8 + slot_row
        places = jax.lax.broadcasted_iota(jnp.int32, (2 * tokens, tokens), 0)
        tables.append((places == key).astype(F32).astype(BF))
        gate_column = jnp.sum(jnp.where(rows == cols, gate_row, 0.0), axis=1, keepdims=True)
        gates.append(jnp.broadcast_to(gate_column, (tokens, GATE_COLUMNS)).astype(BF))
    for start in range(0, width, COLUMNS):
        at = pl.ds(start, COLUMNS)
        picked = jnp.dot(tables[0], x[:, at], preferred_element_type=F32)
        picked = picked + jnp.dot(tables[1], y[:, at], preferred_element_type=F32)
        out[:, at] = picked.astype(BF)
    picked = jnp.dot(tables[0], gates[0], preferred_element_type=F32)
    picked = picked + jnp.dot(tables[1], gates[1], preferred_element_type=F32)
    out[:, pl.ds(width, GATE_COLUMNS)] = picked.astype(BF)


def pack(f_routes, b_routes, f_gates, b_gates, x, y):
    tokens, width = x.shape
    return pl.pallas_call(
        pack_kernel,
        out_shape=jax.ShapeDtypeStruct((2 * tokens, width + GATE_COLUMNS), BF),
        in_specs=[VMEM] * 6,
        out_specs=VMEM,
        cost_estimate=pl.CostEstimate(
            flops=8 * tokens * tokens * width, bytes_accessed=8 * tokens * width, transcendentals=0
        ),
    )(f_routes, b_routes, f_gates, b_gates, x, y)


def unpack_into(routes, slots, out):
    column, slot_column, _, _, places = order_of(routes[...])
    table = (places == column * 8 + slot_column).astype(F32).astype(BF)
    for q, within, at in column_chunks(out.shape[1]):
        out[:, at] = jnp.dot(table, slots[q, :, within], preferred_element_type=F32).astype(BF)


def unpack_first_kernel(odd, f_routes, b_routes, slots, out):
    @pl.when(odd[0] == 1)
    def _():
        unpack_into(f_routes, slots, out)

    @pl.when(odd[0] == 0)
    def _():
        unpack_into(b_routes, slots, out)


def unpack_second_kernel(odd, f_routes, b_routes, first, slots, f_out, b_out):
    @pl.when(odd[0] == 1)
    def _():
        f_out[...] = first[...]
        unpack_into(b_routes, slots, b_out)

    @pl.when(odd[0] == 0)
    def _():
        b_out[...] = first[...]
        unpack_into(f_routes, slots, f_out)


def unpack(odd, f_routes, b_routes, first, second):
    quarters, tokens, part = first.shape
    width = quarters * part
    rows = jax.ShapeDtypeStruct((tokens, width), BF)
    scalar = pl.BlockSpec(memory_space=pltpu.SMEM)
    cost = pl.CostEstimate(
        flops=2 * tokens * tokens * width, bytes_accessed=4 * tokens * width, transcendentals=0
    )
    done = pl.pallas_call(
        unpack_first_kernel,
        out_shape=rows,
        in_specs=[scalar] + [VMEM] * 3,
        out_specs=VMEM,
        cost_estimate=cost,
    )(odd, f_routes, b_routes, first)
    return pl.pallas_call(
        unpack_second_kernel,
        out_shape=(rows, rows),
        in_specs=[scalar] + [VMEM] * 4,
        out_specs=(VMEM, VMEM),
        cost_estimate=cost,
    )(odd, f_routes, b_routes, done, second)


def spread(quarters):
    return lax.all_to_all(quarters, "y", split_axis=0, concat_axis=0, tiled=True)


def go_home(parts, capacity):
    blocks = jnp.stack(parts).reshape(-1, capacity, parts[0].shape[1])
    homed = lax.all_to_all(blocks, ("y", "z"), split_axis=0, concat_axis=0, tiled=True)
    return homed.reshape(len(parts), -1, blocks.shape[2])


def column_chunks(width):
    quarter = width // QUARTERS
    for q in range(QUARTERS):
        for start in range(0, quarter, COLUMNS):
            size = min(COLUMNS, quarter - start)
            yield q, pl.ds(start, size), pl.ds(q * quarter + start, size)


def load_weights(refs, gate_up, down, sems):
    for u in range(4):
        yield (
            pltpu.make_async_copy(refs[u], gate_up.at[u], sems.at[u]),
            pltpu.make_async_copy(refs[4 + u], down.at[u], sems.at[4 + u]),
        )


def forward_kernel(own, visiting, *refs):
    weights, (out_own, out_visiting, rows, gate_up, down, hidden, sems) = refs[:8], refs[8:]
    copies = list(load_weights(weights, gate_up, down, sems))
    for pair in copies:
        pair[0].start()
        pair[1].start()
    half, width = own.shape[0], rows.shape[1]
    units = down.shape[1]
    gates = [ref[:, pl.ds(width, GATE_COLUMNS)].astype(F32)[:, :1] for ref in (own, visiting)]
    rows[pl.ds(0, half), :] = own[:, pl.ds(0, width)]
    rows[pl.ds(half, half), :] = visiting[:, pl.ds(0, width)]
    for u in range(4):
        copies[u][0].wait()
        pre = jnp.dot(rows[...], gate_up[u], preferred_element_type=F32)
        gate, up = pre[:, :units], pre[:, units:]
        hidden[u] = (gate * jax.nn.sigmoid(gate) * up).astype(BF)
    for u in range(4):
        copies[u][1].wait()
    for q, within, at in column_chunks(width):
        total = jnp.dot(hidden[0], down[0, :, at], preferred_element_type=F32)
        for u in range(1, 4):
            total = total + jnp.dot(hidden[u], down[u, :, at], preferred_element_type=F32)
        out_own[q, :, within] = own[:, at].astype(F32) + gates[0] * total[:half]
        out_visiting[q, :, within] = (gates[1] * total[half:]).astype(BF)


def backward_kernel(own, visiting, saved, *refs):
    weights, (out_own, out_visiting, rows, gate_up, down, grads, sems) = refs[:8], refs[8:]
    copies = list(load_weights(weights, gate_up, down, sems))
    for pair in copies:
        pair[1].start()
        pair[0].start()
    half, width = own.shape[0], rows.shape[1]
    units = down.shape[1]
    for at_row, ref in ((0, own), (half, visiting)):
        gate = ref[:, pl.ds(width, GATE_COLUMNS)].astype(F32)[:, :1]
        for start in range(0, width, COLUMNS):
            at = pl.ds(start, COLUMNS)
            rows[pl.ds(at_row, half), at] = (gate * ref[:, at].astype(F32)).astype(BF)
    for u in range(4):
        copies[u][1].wait()
        grad = lax.dot_general(rows[...], down[u], ROWS_T, preferred_element_type=F32)
        a, b = saved[u, 0].astype(F32), saved[u, 1].astype(F32)
        sig = jax.nn.sigmoid(a)
        grads[u, :, pl.ds(0, units)] = (grad * b * sig * (1.0 + a * (1.0 - sig))).astype(BF)
        grads[u, :, pl.ds(units, units)] = (grad * a * sig).astype(BF)
    for u in range(4):
        copies[u][0].wait()
    for q, within, at in column_chunks(width):
        total = lax.dot_general(grads[0], gate_up[0, at, :], ROWS_T, preferred_element_type=F32)
        for u in range(1, 4):
            total = total + lax.dot_general(
                grads[u], gate_up[u, at, :], ROWS_T, preferred_element_type=F32
            )
        out_own[q, :, within] = own[:, at].astype(F32) + total[:half]
        out_visiting[q, :, within] = total[half:].astype(BF)


def expert_pass(kernel, own, visiting, extra, weights, middle):
    half, units = own.shape[0], weights[4].shape[0]
    width = own.shape[1] - GATE_COLUMNS
    quarters = (QUARTERS, half, width // QUARTERS)
    rows, flops = 2 * half, 2 * 2 * half * width * 4 * units * 3
    return pl.pallas_call(
        kernel,
        out_shape=(jax.ShapeDtypeStruct(quarters, F32), jax.ShapeDtypeStruct(quarters, BF)),
        in_specs=[VMEM] * (2 + len(extra)) + [pl.BlockSpec(memory_space=pl.ANY)] * 8,
        out_specs=(VMEM, VMEM),
        scratch_shapes=[
            pltpu.VMEM((rows, width), BF),
            pltpu.VMEM((4, width, 2 * units), BF),
            pltpu.VMEM((4, units, width), BF),
            pltpu.VMEM((4, rows, middle), BF),
            pltpu.SemaphoreType.DMA((8,)),
        ],
        compiler_params=pltpu.CompilerParams(vmem_limit_bytes=40 * 1024 * 1024),
        cost_estimate=pl.CostEstimate(
            flops=flops, bytes_accessed=12 * width * units * 2 + 5 * half * width * 2, transcendentals=0
        ),
    )(own, visiting, *extra, *weights)


def body(
    forward_state, grad_state, forward_routes, forward_gates, backward_routes, backward_gates,
    saved_preacts, gate_weight, up_weight, down_weight,
):
    x, y, saved = forward_state[0], grad_state[0], saved_preacts[0]
    width = x.shape[1]
    capacity, units = saved.shape[2], saved.shape[3]
    nz, nx, nc = lax.axis_size("z"), lax.axis_size("x"), lax.axis_size("c")
    f_routes, b_routes, f_gates, b_gates = (
        array[0].reshape(1, -1)
        for array in (forward_routes, backward_routes, forward_gates, backward_gates)
    )
    packed = pack(f_routes, b_routes, f_gates, b_gates, x, y)
    packed, gate_here, up_here, down_here = lax.optimization_barrier(
        (packed, gate_weight[0], up_weight[0], down_weight[0])
    )
    arrived = exchange(packed.reshape(nz, 2 * capacity, packed.shape[1]))

    own_weights = [jnp.concatenate([gate_here, up_here], axis=1), down_here]
    beside_weights = [swap_weights(mine) for mine in own_weights]
    across_weights = [swap_core(mine) for mine in own_weights]
    across_weights[0], saved = lax.optimization_barrier((across_weights[0], saved))
    weights = []
    for mine, across, beside in zip(own_weights, across_weights, beside_weights):
        weights += [mine, across, beside, swap_core(beside)]

    me_x, me_c = lax.axis_index("x"), lax.axis_index("c")
    by_place = saved.reshape(2, nz, nx, nc, capacity, units)

    def kept_for(at_x):
        rows_of = [
            lax.dynamic_index_in_dim(by_place, at, 2, keepdims=False) for at in (at_x, at_x ^ 2)
        ]
        return jnp.stack(rows_of, 1)

    here = jnp.stack([kept_for(me_x), swap_weights(kept_for(me_x ^ (1 + 2 * me_c)))])
    mine = lax.dynamic_index_in_dim(here, me_c, 4, keepdims=False)
    theirs = swap_core(lax.dynamic_index_in_dim(here, 1 - me_c, 4, keepdims=False))
    kept = jnp.stack([mine, theirs], 1).reshape(4, 2, 2 * nz * capacity, units)

    f_moved = permute(f_routes, ("h", "y"), [(i + 1) % 8 for i in range(8)])
    b_moved = permute(b_routes, ("h", "y"), [(i - 1) % 8 for i in range(8)])
    arrived, weights, kept = lax.optimization_barrier((arrived, weights, kept))

    f_rows = arrived[:, :capacity].reshape(nz * capacity, -1)
    b_rows = arrived[:, capacity:].reshape(nz * capacity, -1)
    f_own, f_visited = expert_pass(forward_kernel, f_rows, swap_rows(f_rows), (), weights, units)
    b_own, b_visited = expert_pass(
        backward_kernel, b_rows, swap_rows(b_rows), (kept,), weights, 2 * units
    )
    f_out = (f_own + swap_rows(f_visited).astype(F32)).astype(BF)
    b_out = (b_own + swap_rows(b_visited).astype(F32)).astype(BF)
    f_spread, b_spread = spread(f_out), spread(b_out)
    crossed = permute(jnp.stack([f_spread[3], b_spread[0]]), "h", (1, 0))
    first = go_home([b_spread[1], f_spread[0], b_spread[3], f_spread[2]], capacity)
    second = go_home([crossed[0], b_spread[2], f_spread[1], crossed[1]], capacity)
    odd = lax.rem(lax.axis_index("y"), 2).astype(jnp.int32).reshape(1)
    forward_next, backward_next = unpack(odd, f_moved, b_moved, first, second)
    return forward_next[None], backward_next[None]


def solution(mesh):
    pipes = mesh.shape["pipe"]
    fine = Mesh(mesh.devices.reshape(2, pipes // 2, 8, 4, 2), ("h", "y", "z", "x", "c"))
    pipe, expert = ("h", "y"), ("z", "x", "c")
    tokens = P(pipe, expert, None)
    return jax.shard_map(
        body,
        mesh=fine,
        in_specs=(
            tokens, tokens, tokens, tokens, tokens, tokens,
            P(pipe, None, None, None, expert),
            P(pipe, None, expert),
            P(pipe, None, expert),
            P(pipe, expert, None),
        ),
        out_specs=(tokens, tokens),
        check_vma=False,
    )
```

time: 265 us -> 221 us (0.83)
  waiting for transfers between devices: 145 us -> 93.6 us
  starting transfers between devices: 86.4 us -> 96.9 us
  matrix products: 6.02 us -> 0 us
  Pallas kernels: 15.5 us -> 19.2 us
    all_to_all x4 -> x1, waiting for transfers between devices: 69.1 us -> 16.5 us  [exchange(): return lax.all_to_all(block, 'z', split_axis=0, concat_axis=0, tiled=True)]
    all_to_all x0 -> x4, starting transfers between devices: none -> 33.4 us  [the longest x2 23.2 us: go_home(): lax.all_to_all(blocks, ('y', 'z'), split_axis=0, concat_axis=0, tiled=True)]
    all_to_all x0 -> x4, waiting for transfers between devices: none -> 24.1 us  [the longest x2 18.1 us: go_home(): lax.all_to_all(blocks, ('y', 'z'), split_axis=0, concat_axis=0, tiled=True)]
    all_to_all x4 -> x1, starting transfers between devices: 35.9 us -> 12.5 us  [exchange(): return lax.all_to_all(block, 'z', split_axis=0, concat_axis=0, tiled=True)]
    ppermute x17 -> x15, waiting for transfers between devices: 75.6 us -> 53 us  [permute(): return lax.ppermute(block, axis, list(enumerate(targets)))]
    dot_general x4 -> x0, matrix products: 6.02 us -> none  [the longest x2 4.3 us: pack(): return jnp.dot(table, rows, preferred_element_type=F32).astype(BF)]
    pallas_call x2 -> x5, Pallas kernels: 15.5 us -> 19.2 us  [the longest x2 11.5 us: expert_pass(): pl.pallas_call(kernel, out_shape=(jax.ShapeDtypeStruct(quarters, F32), ja...]
    reshape x2 -> x0, other arithmetic: 2.98 us -> none  [the longest x1 2.14 us: body(): f_back = exchange(f_out.reshape(nz, capacity, width)).reshape(-1, width)]
  transfers between devices with their start and end apart: 21 -> 20, of which waited for: 11 -> 12; matrix products, arithmetic and copies ran while one was open for 3% -> 1% of each run, Pallas kernels for 6% -> 6%
where the time goes in v4:
time: 221 us; the launch traced here: 219 us
  starting transfers between devices  96.9 us (44%)
  waiting for transfers between devices  93.6 us (42%)
  Pallas kernels  19.2 us (9%)
  local copies, waits for them, and re-layouts  5.07 us (2%)
  other arithmetic  3.51 us (2%)
    ppermute x15, waiting for transfers between devices, permute(): return lax.ppermute(block, axis, list(enumerate(targets)))  53 us
    ppermute x15, starting transfers between devices, permute(): return lax.ppermute(block, axis, list(enumerate(targets)))  50.9 us
    all_to_all x2, starting transfers between devices, go_home(): lax.all_to_all(blocks, ('y', 'z'), split_axis=0, concat_axis=0, tiled=True)  23.2 us
    all_to_all x2, waiting for transfers between devices, go_home(): lax.all_to_all(blocks, ('y', 'z'), split_axis=0, concat_axis=0, tiled=True)  18.1 us
    all_to_all x1, waiting for transfers between devices, exchange(): return lax.all_to_all(block, 'z', split_axis=0, concat_axis=0, tiled=True)  16.5 us
    all_to_all x1, starting transfers between devices, exchange(): return lax.all_to_all(block, 'z', split_axis=0, concat_axis=0, tiled=True)  12.5 us
    pallas_call x2, Pallas kernels, expert_pass(): pl.pallas_call(kernel, out_shape=(jax.ShapeDtypeStruct(quarters, F32), ja...  11.5 us
    all_to_all x2, starting transfers between devices, spread(): lax.all_to_all(quarters, 'y', split_axis=0, concat_axis=0, tiled=True)  10.2 us
  transfers between devices with their start and end apart: 20, of which 12 were waited for; matrix products, arithmetic and copies ran while one was open for 1% of the time, Pallas kernels for 6%

profile of v4, /device:TPU:24, one launch (start us, length us, event | category | flops | bytes accessed | tf_op | source)
XLA Modules:
  0.0 219.3 jit_solution(17862083224724986451)
XLA Ops:
  0.6 3.0 %shard_map.113 = bf16[128,3712]{1,0:T(8,128)(2,1)} custom-call(s32[1,64]{1,0:T(1,128)} %bitcast.61, s32[1,64]{1,0:T(1,128)} %bitcast.63, bf16[1,64]{1,0:T(2,128)(2,1)} %bitcast.59, bf16[1,64]{1,0:T(2,128)(2,1)} %bitcast.60, bf16[64,3584]{1,0:T(8,128)(2,1)} %bitcast.53, bf16[64,3584]{1,0:T(8,128)(2,1)} %bitcast.54), custom_call_target="tpu_custom_call" | custom-call | flops 117440512 | bytes 1835008 | tf_op jit(solution)/shard_map/pallas_call | solution.py:72
  5.0 3.5 %collective-permute-start.3 = (bf16[3584,256]{1,0:T(8,128)(2,1)S(1)}, bf16[3584,256]{1,0:T(8,128)(2,1)}, u32[]{:S(2)}, u32[]{:S(2)}) collective-permute-start(bf16[3584,256]{1,0:T(8,128)(2,1)S(1)} %constant_dynamic-update-slice_fusion.refs_0_), channel_id=1, source_target_pairs={{0,2},{1,7},{2,0},{3,5},{4,6},{5,3},{6,4},{7,1},{8,10},{9,15},{10,... | collective-permute-start | bytes 5505032 | tf_op jit(solution)/shard_map/ppermute | solution.py:18
  8.6 12.5 %all-to-all-start = ((bf16[8,16,3712]{2,1,0:T(8,128)(2,1)}), bf16[8,16,3712]{2,1,0:T(8,128)(2,1)}, u32[]{:S(2)}, u32[]{:S(2)}) async-start(bf16[8,16,3712]{2,1,0:T(8,128)(2,1)} %bitcast.47), calls=%async_computation | async-start | bytes 1900544 | tf_op jit(solution)/shard_map/all_to_all | solution.py:35
  21.1 2.4 %collective-permute-start.2 = (bf16[3584,256]{1,0:T(8,128)(2,1)S(1)}, bf16[3584,256]{1,0:T(8,128)(2,1)}, u32[]{:S(2)}, u32[]{:S(2)}) collective-permute-start(bf16[3584,256]{1,0:T(8,128)(2,1)S(1)} %constant_dynamic-update-slice_fusion.refs_0_), channel_id=1, source_target_pairs={{0,1},{1,0},{2,3},{3,2},{4,5},{5,4},{6,7},{7,6},{8,9},{9,8},{10,11... | collective-permute-start | bytes 5505032 | tf_op jit(solution)/shard_map/ppermute | solution.py:18
  23.6 2.1 collective-permute-start.6
  25.7 4.7 %collective-permute-done.3.refs_2_ = bf16[3584,256]{1,0:T(8,128)(2,1)} collective-permute-done((bf16[3584,256]{1,0:T(8,128)(2,1)S(1)}, bf16[3584,256]{1,0:T(8,128)(2,1)}, u32[]{:S(2)}, u32[]{:S(2)}) %collective-permute-start.3) | collective-permute-done | bytes 1835040 | tf_op jit(solution)/shard_map/ppermute | solution.py:18
  32.3 2.4 %collective-permute-start.5 = (bf16[128,3584]{1,0:T(8,128)(2,1)S(1)}, bf16[128,3584]{1,0:T(8,128)(2,1)}, u32[]{:S(2)}, u32[]{:S(2)}) collective-permute-start(bf16[128,3584]{1,0:T(8,128)(2,1)S(1)} %bitcast.43), channel_id=1, source_target_pairs={{0,1},{1,0},{2,3},{3,2},{4,5},{5,4},{6,7},{7,6},{8,9},{9,8},{10,11... | collective-permute-start | bytes 2752520 | tf_op jit(solution)/shard_map/ppermute | solution.py:18
  34.7 5.5 %collective-permute-done.6.refs_6_ = bf16[128,3584]{1,0:T(8,128)(2,1)} collective-permute-done((bf16[128,3584]{1,0:T(8,128)(2,1)S(1)}, bf16[128,3584]{1,0:T(8,128)(2,1)}, u32[]{:S(2)}, u32[]{:S(2)}) %collective-permute-start.6) | collective-permute-done | bytes 917536 | tf_op jit(solution)/shard_map/ppermute | solution.py:18
  42.4 3.2 %collective-permute-start.8 = (bf16[2,2,8,2,8,128]{5,4,3,2,0,1:T(8,128)(2,1)S(1)}, bf16[2,2,8,2,8,128]{5,4,3,2,0,1:T(8,128)(2,1)S(1)}, u32[]{:S(2)}, u32[]{:S(2)}) collective-permute-start(bf16[2,2,8,2,8,128]{5,4,3,2,0,1:T(8,128)(2,1)S(1)} %pad_maximum_fusion.4), channel_id=1, source_target_pairs={{0,2},{1,7},{2,0},{3,5},{4,6},{5,3},{6,4},{7,1},{8,10},{9,15},{10,... | collective-permute-start | bytes 393224 | tf_op jit(solution)/shard_map/ppermute | solution.py:18
  45.7 3.6 %collective-permute-done.8 = bf16[2,2,8,2,8,128]{5,4,3,2,0,1:T(8,128)(2,1)S(1)} collective-permute-done((bf16[2,2,8,2,8,128]{5,4,3,2,0,1:T(8,128)(2,1)S(1)}, bf16[2,2,8,2,8,128]{5,4,3,2,0,1:T(8,128)(2,1)S(1)}, u32[]{:S(2)}, u32[]{:S(2)}) %collective-permute-start.8) | collective-permute-done | bytes 131104 | tf_op jit(solution)/shard_map/ppermute | solution.py:18
  49.4 2.3 %collective-permute-start.9 = (bf16[2,2,2,8,8,128]{5,4,3,2,1,0:T(8,128)(2,1)S(1)}, bf16[2,2,2,8,8,128]{5,4,3,2,1,0:T(8,128)(2,1)S(1)}, u32[]{:S(2)}, u32[]{:S(2)}) collective-permute-start(bf16[2,2,2,8,8,128]{5,4,3,2,1,0:T(8,128)(2,1)S(1)} %bitcast.56), channel_id=1, source_target_pairs={{0,1},{1,0},{2,3},{3,2},{4,5},{5,4},{6,7},{7,6},{8,9},{9,8},{10,11... | collective-permute-start | bytes 393224 | tf_op jit(solution)/shard_map/ppermute | solution.py:18
  52.7 16.5 %all-to-all-done = bf16[8,16,3712]{2,1,0:T(8,128)(2,1)} async-done(((bf16[8,16,3712]{2,1,0:T(8,128)(2,1)}), bf16[8,16,3712]{2,1,0:T(8,128)(2,1)}, u32[]{:S(2)}, u32[]{:S(2)}) %all-to-all-start) | async-done | bytes 950304 | tf_op jit(solution)/shard_map/all_to_all | solution.py:35
  70.5 2.7 %collective-permute-start.10 = (bf16[64,3712]{1,0:T(8,128)(2,1)S(1)}, bf16[64,3712]{1,0:T(8,128)(2,1)S(1)}, u32[]{:S(2)}, u32[]{:S(2)}) collective-permute-start(bf16[64,3712]{1,0:T(8,128)(2,1)S(1)} %get-tuple-element.46.own), channel_id=1, source_target_pairs={{0,4},{2,6},{4,0},{6,2},{1,5},{3,7},{5,1},{7,3},{8,12},{10,14},{12... | collective-permute-start | bytes 1425416 | tf_op jit(solution)/shard_map/ppermute | solution.py:18
  73.2 4.6 %collective-permute-start.12 = (bf16[64,3712]{1,0:T(8,128)(2,1)S(1)}, bf16[64,3712]{1,0:T(8,128)(2,1)S(1)}, u32[]{:S(2)}, u32[]{:S(2)}) collective-permute-start(bf16[64,3712]{1,0:T(8,128)(2,1)S(1)} %get-tuple-element.47.own), channel_id=1, source_target_pairs={{0,4},{2,6},{4,0},{6,2},{1,5},{3,7},{5,1},{7,3},{8,12},{10,14},{12... | collective-permute-start | bytes 1425416 | tf_op jit(solution)/shard_map/ppermute | solution.py:18
  77.8 9.8 %collective-permute-done.10.visiting = bf16[64,3712]{1,0:T(8,128)(2,1)S(1)} collective-permute-done((bf16[64,3712]{1,0:T(8,128)(2,1)S(1)}, bf16[64,3712]{1,0:T(8,128)(2,1)S(1)}, u32[]{:S(2)}, u32[]{:S(2)}) %collective-permute-start.10) | collective-permute-done | bytes 475168 | tf_op jit(solution)/shard_map/ppermute | solution.py:18
  87.6 6.2 %shard_map.114 = (f32[4,64,896]{2,1,0:T(8,128)S(1)}, bf16[4,64,896]{2,1,0:T(8,128)(2,1)S(1)}) custom-call(bf16[64,3712]{1,0:T(8,128)(2,1)S(1)} %get-tuple-element.46.own, bf16[64,3712]{1,0:T(8,128)(2,1)S(1)} %collective-permute-done.10.visiting, bf16[4,2,128,128]{3,2,1,0:T(8,128)(2,1)S(1)} %bitcast.46, ...), custom_call_target="tpu_custom_call" | custom-call | flops 1409286144 | bytes 13303808 | tf_op jit(solution)/shard_map/pallas_call | solution.py:225
  93.9 2.8 %collective-permute-start.11 = (bf16[4,64,896]{2,1,0:T(8,128)(2,1)S(1)}, bf16[4,64,896]{2,1,0:T(8,128)(2,1)S(1)}, u32[]{:S(2)}, u32[]{:S(2)}) collective-permute-start(bf16[4,64,896]{2,1,0:T(8,128)(2,1)S(1)} %get-tuple-element.41), channel_id=1, source_target_pairs={{0,4},{2,6},{4,0},{6,2},{1,5},{3,7},{5,1},{7,3},{8,12},{10,14},{12... | collective-permute-start | bytes 1376264 | tf_op jit(solution)/shard_map/ppermute | solution.py:18
  96.6 5.3 %shard_map.115 = (f32[4,64,896]{2,1,0:T(8,128)S(1)}, bf16[4,64,896]{2,1,0:T(8,128)(2,1)S(1)}) custom-call(bf16[64,3712]{1,0:T(8,128)(2,1)S(1)} %get-tuple-element.47.own, bf16[64,3712]{1,0:T(8,128)(2,1)S(1)} %collective-permute-done.12.visiting, bf16[3584,256]{1,0:T(8,128)(2,1)S(1)} %constant_dynamic-update-slice_fusion.refs_0_, ...), custom_call_target="tpu_custom_call" | custom-call | flops 1409286144 | bytes 13303808 | tf_op jit(solution)/shard_map/pallas_call | solution.py:225
  102.9 4.7 %collective-permute-start.13 = (bf16[4,64,896]{2,1,0:T(8,128)(2,1)S(1)}, bf16[4,64,896]{2,1,0:T(8,128)(2,1)S(1)}, u32[]{:S(2)}, u32[]{:S(2)}) collective-permute-start(bf16[4,64,896]{2,1,0:T(8,128)(2,1)S(1)} %get-tuple-element.43), channel_id=1, source_target_pairs={{0,4},{2,6},{4,0},{6,2},{1,5},{3,7},{5,1},{7,3},{8,12},{10,14},{12... | collective-permute-start | bytes 1376264 | tf_op jit(solution)/shard_map/ppermute | solution.py:18
  108.5 4.7 %all-to-all-start.1 = ((bf16[4,64,896]{2,1,0:T(8,128)(2,1)}), bf16[4,64,896]{2,1,0:T(8,128)(2,1)S(1)}, u32[]{:S(2)}, u32[]{:S(2)}) async-start(bf16[4,64,896]{2,1,0:T(8,128)(2,1)} %add_convert_fusion.1), calls=%async_computation.1 | async-start | bytes 917504 | tf_op jit(solution)/shard_map/all_to_all | solution.py:137
  113.2 4.5 %collective-permute-done.13 = bf16[4,64,896]{2,1,0:T(8,128)(2,1)S(1)} collective-permute-done((bf16[4,64,896]{2,1,0:T(8,128)(2,1)S(1)}, bf16[4,64,896]{2,1,0:T(8,128)(2,1)S(1)}, u32[]{:S(2)}, u32[]{:S(2)}) %collective-permute-start.13) | collective-permute-done | bytes 458784 | tf_op jit(solution)/shard_map/ppermute | solution.py:18
  118.8 5.5 %all-to-all-start.2 = ((bf16[4,64,896]{2,1,0:T(8,128)(2,1)}), bf16[4,64,896]{2,1,0:T(8,128)(2,1)S(1)}, u32[]{:S(2)}, u32[]{:S(2)}) async-start(bf16[4,64,896]{2,1,0:T(8,128)(2,1)} %add_convert_fusion), calls=%async_computation.2 | async-start | bytes 917504 | tf_op jit(solution)/shard_map/all_to_all | solution.py:137
  124.4 5.6 %all-to-all-done.2 = bf16[4,64,896]{2,1,0:T(8,128)(2,1)S(1)} async-done(((bf16[4,64,896]{2,1,0:T(8,128)(2,1)}), bf16[4,64,896]{2,1,0:T(8,128)(2,1)S(1)}, u32[]{:S(2)}, u32[]{:S(2)}) %all-to-all-start.2) | async-done | bytes 458784 | tf_op jit(solution)/shard_map/all_to_all | solution.py:137
  130.9 7.6 %all-to-all-start.3 = ((bf16[32,8,896]{2,1,0:T(8,128)(2,1)}), bf16[32,8,896]{2,1,0:T(8,128)(2,1)S(1)}, u32[]{:S(2)}, u32[]{:S(2)}) async-start(bf16[32,8,896]{2,1,0:T(8,128)(2,1)} %bitcast.25), calls=%async_computation.3 | async-start | bytes 917504 | tf_op jit(solution)/shard_map/all_to_all | solution.py:142
  138.6 8.2 %collective-permute-start.14 = (bf16[2,64,896]{2,1,0:T(8,128)(2,1)S(1)}, bf16[2,64,896]{2,1,0:T(8,128)(2,1)S(1)}, u32[]{:S(2)}, u32[]{:S(2)}) collective-permute-start(bf16[2,64,896]{2,1,0:T(8,128)(2,1)S(1)} %pad_maximum_fusion.3), channel_id=1, source_target_pairs={{0,256},{256,0},{1,257},{257,1},{2,258},{258,2},{3,259},{259,3},{4... | collective-permute-start | bytes 688136 | tf_op jit(solution)/shard_map/ppermute | solution.py:18
  146.8 9.6 %collective-permute-done.14 = bf16[2,64,896]{2,1,0:T(8,128)(2,1)S(1)} collective-permute-done((bf16[2,64,896]{2,1,0:T(8,128)(2,1)S(1)}, bf16[2,64,896]{2,1,0:T(8,128)(2,1)S(1)}, u32[]{:S(2)}, u32[]{:S(2)}) %collective-permute-start.14) | collective-permute-done | bytes 229408 | tf_op jit(solution)/shard_map/ppermute | solution.py:18
  157.2 18.1 %all-to-all-done.3 = bf16[32,8,896]{2,1,0:T(8,128)(2,1)S(1)} async-done(((bf16[32,8,896]{2,1,0:T(8,128)(2,1)}), bf16[32,8,896]{2,1,0:T(8,128)(2,1)S(1)}, u32[]{:S(2)}, u32[]{:S(2)}) %all-to-all-start.3) | async-done | bytes 458784 | tf_op jit(solution)/shard_map/all_to_all | solution.py:142
  175.4 15.6 %all-to-all-start.4 = ((bf16[32,8,896]{2,1,0:T(8,128)(2,1)}), bf16[32,8,896]{2,1,0:T(8,128)(2,1)S(1)}, u32[]{:S(2)}, u32[]{:S(2)}) async-start(bf16[32,8,896]{2,1,0:T(8,128)(2,1)} %bitcast.27), calls=%async_computation.4 | async-start | bytes 917504 | tf_op jit(solution)/shard_map/all_to_all | solution.py:142
  191.0 6.0 %collective-permute-start = (s32[1,64]{1,0:T(1,128)S(1)}, s32[1,64]{1,0:T(1,128)S(1)}, u32[]{:S(2)}, u32[]{:S(2)}) collective-permute-start(s32[1,64]{1,0:T(1,128)S(1)} %bitcast.62), channel_id=1, source_target_pairs={{0,64},{64,128},{128,192},{192,256},{256,320},{320,384},{384,448},... | collective-permute-start | bytes 776 | tf_op jit(solution)/shard_map/ppermute | solution.py:18
  199.0 14.3 %collective-permute-done.1.b_routes = s32[1,64]{1,0:T(1,128)S(1)} collective-permute-done((s32[1,64]{1,0:T(1,128)S(1)}, s32[1,64]{1,0:T(1,128)S(1)}, u32[]{:S(2)}, u32[]{:S(2)}) %collective-permute-start.1) | collective-permute-done | bytes 288 | tf_op jit(solution)/shard_map/ppermute | solution.py:18
  213.8 2.2 %shard_map.116.first = bf16[64,3584]{1,0:T(8,128)(2,1)} custom-call(s32[1]{0:T(128)} %bitcast.odd, s32[1,64]{1,0:T(1,128)} %copy-done.8, s32[1,64]{1,0:T(1,128)} %copy-done.9, bf16[4,64,896]{2,1,0:T(8,128)(2,1)} %bitcast.48), custom_call_target="tpu_custom_call" | custom-call | flops 29360128 | bytes 917504 | tf_op jit(solution)/shard_map/pallas_call | solution.py:120
  216.8 2.5 %shard_map.117 = (bf16[64,3584]{1,0:T(8,128)(2,1)}, bf16[64,3584]{1,0:T(8,128)(2,1)}) custom-call(s32[1]{0:T(128)} %bitcast.odd, s32[1,64]{1,0:T(1,128)} %copy-done.8, s32[1,64]{1,0:T(1,128)} %copy-done.9, bf16[64,3584]{1,0:T(8,128)(2,1)} %shard_map.116.first, bf16[4,64,896]{2,1,0:T(8,128)(2,1)} %bitcast.49), custom_call_target="tpu_custom_call" | custom-call | flops 29360128 | bytes 917504 | tf_op jit(solution)/shard_map/pallas_call | solution.py:127
  (56 shorter events, 15.8 us)
Async XLA Ops:
  0.6 3.0 %copy-start.5 = (bf16[1,3584,128]{2,1,0:T(8,128)(2,1)S(1)}, bf16[1,3584,128]{2,1,0:T(8,128)(2,1)}, u32[]{:S(2)}) copy-start(bf16[1,3584,128]{2,1,0:T(8,128)(2,1)} %param.17) | copy-start | bytes 2752516
  3.6 1.2 copy-start.6
  4.8 18.8 %copy-start = (bf16[1,128,3584]{2,1,0:T(8,128)(2,1)S(1)}, bf16[1,128,3584]{2,1,0:T(8,128)(2,1)}, u32[]{:S(2)}) copy-start(bf16[1,128,3584]{2,1,0:T(8,128)(2,1)} %param.19) | copy-start | bytes 2752516
  4.8 37.5 %copy-start.7 = (bf16[1,2,64,8,128]{4,3,2,1,0:T(8,128)(2,1)S(1)}, bf16[1,2,64,8,128]{4,3,2,1,0:T(8,128)(2,1)}, u32[]{:S(2)}) copy-start(bf16[1,2,64,8,128]{4,3,2,1,0:T(8,128)(2,1)} %param.16) | copy-start | bytes 786436
  5.0 25.4 %collective-permute-start.3 = (bf16[3584,256]{1,0:T(8,128)(2,1)S(1)}, bf16[3584,256]{1,0:T(8,128)(2,1)}, u32[]{:S(2)}, u32[]{:S(2)}) collective-permute-start(bf16[3584,256]{1,0:T(8,128)(2,1)S(1)} %constant_dynamic-update-slice_fusion.refs_0_), channel_id=1, source_target_pairs={{0,2},{1,7},{2,0},{3,5},{4,6},{5,3},{6,4},{7,1},{8,10},{9,15},{10,... | collective-permute-start | bytes 5505032 | tf_op jit(solution)/shard_map/ppermute | solution.py:18
  8.6 60.7 %all-to-all-start = ((bf16[8,16,3712]{2,1,0:T(8,128)(2,1)}), bf16[8,16,3712]{2,1,0:T(8,128)(2,1)}, u32[]{:S(2)}, u32[]{:S(2)}) async-start(bf16[8,16,3712]{2,1,0:T(8,128)(2,1)} %bitcast.47), calls=%async_computation | async-start | bytes 1900544 | tf_op jit(solution)/shard_map/all_to_all | solution.py:35
  21.1 21.2 %collective-permute-start.2 = (bf16[3584,256]{1,0:T(8,128)(2,1)S(1)}, bf16[3584,256]{1,0:T(8,128)(2,1)}, u32[]{:S(2)}, u32[]{:S(2)}) collective-permute-start(bf16[3584,256]{1,0:T(8,128)(2,1)S(1)} %constant_dynamic-update-slice_fusion.refs_0_), channel_id=1, source_target_pairs={{0,1},{1,0},{2,3},{3,2},{4,5},{5,4},{6,7},{7,6},{8,9},{9,8},{10,11... | collective-permute-start | bytes 5505032 | tf_op jit(solution)/shard_map/ppermute | solution.py:18
  23.6 16.7 %collective-permute-start.6 = (bf16[128,3584]{1,0:T(8,128)(2,1)S(1)}, bf16[128,3584]{1,0:T(8,128)(2,1)}, u32[]{:S(2)}, u32[]{:S(2)}) collective-permute-start(bf16[128,3584]{1,0:T(8,128)(2,1)S(1)} %bitcast.42), channel_id=1, source_target_pairs={{0,2},{1,7},{2,0},{3,5},{4,6},{5,3},{6,4},{7,1},{8,10},{9,15},{10,... | collective-permute-start | bytes 2752520 | tf_op jit(solution)/shard_map/ppermute | solution.py:18
  30.4 38.8 %collective-permute-start.4 = (bf16[3584,256]{1,0:T(8,128)(2,1)}, bf16[3584,256]{1,0:T(8,128)(2,1)}, u32[]{:S(2)}, u32[]{:S(2)}) collective-permute-start(bf16[3584,256]{1,0:T(8,128)(2,1)} %collective-permute-done.3.refs_2_), channel_id=1, source_target_pairs={{0,1},{1,0},{2,3},{3,2},{4,5},{5,4},{6,7},{7,6},{8,9},{9,8},{10,11... | collective-permute-start | bytes 5505032 | tf_op jit(solution)/shard_map/ppermute | solution.py:18
  32.3 20.3 %collective-permute-start.5 = (bf16[128,3584]{1,0:T(8,128)(2,1)S(1)}, bf16[128,3584]{1,0:T(8,128)(2,1)}, u32[]{:S(2)}, u32[]{:S(2)}) collective-permute-start(bf16[128,3584]{1,0:T(8,128)(2,1)S(1)} %bitcast.43), channel_id=1, source_target_pairs={{0,1},{1,0},{2,3},{3,2},{4,5},{5,4},{6,7},{7,6},{8,9},{9,8},{10,11... | collective-permute-start | bytes 2752520 | tf_op jit(solution)/shard_map/ppermute | solution.py:18
  40.2 12.5 %collective-permute-start.7 = (bf16[128,3584]{1,0:T(8,128)(2,1)}, bf16[128,3584]{1,0:T(8,128)(2,1)}, u32[]{:S(2)}, u32[]{:S(2)}) collective-permute-start(bf16[128,3584]{1,0:T(8,128)(2,1)} %collective-permute-done.6.refs_6_), channel_id=1, source_target_pairs={{0,1},{1,0},{2,3},{3,2},{4,5},{5,4},{6,7},{7,6},{8,9},{9,8},{10,11... | collective-permute-start | bytes 2752520 | tf_op jit(solution)/shard_map/ppermute | solution.py:18
  42.4 6.9 %collective-permute-start.8 = (bf16[2,2,8,2,8,128]{5,4,3,2,0,1:T(8,128)(2,1)S(1)}, bf16[2,2,8,2,8,128]{5,4,3,2,0,1:T(8,128)(2,1)S(1)}, u32[]{:S(2)}, u32[]{:S(2)}) collective-permute-start(bf16[2,2,8,2,8,128]{5,4,3,2,0,1:T(8,128)(2,1)S(1)} %pad_maximum_fusion.4), channel_id=1, source_target_pairs={{0,2},{1,7},{2,0},{3,5},{4,6},{5,3},{6,4},{7,1},{8,10},{9,15},{10,... | collective-permute-start | bytes 393224 | tf_op jit(solution)/shard_map/ppermute | solution.py:18
  49.4 3.3 %collective-permute-start.9 = (bf16[2,2,2,8,8,128]{5,4,3,2,1,0:T(8,128)(2,1)S(1)}, bf16[2,2,2,8,8,128]{5,4,3,2,1,0:T(8,128)(2,1)S(1)}, u32[]{:S(2)}, u32[]{:S(2)}) collective-permute-start(bf16[2,2,2,8,8,128]{5,4,3,2,1,0:T(8,128)(2,1)S(1)} %bitcast.56), channel_id=1, source_target_pairs={{0,1},{1,0},{2,3},{3,2},{4,5},{5,4},{6,7},{7,6},{8,9},{9,8},{10,11... | collective-permute-start | bytes 393224 | tf_op jit(solution)/shard_map/ppermute | solution.py:18
  70.5 17.2 %collective-permute-start.10 = (bf16[64,3712]{1,0:T(8,128)(2,1)S(1)}, bf16[64,3712]{1,0:T(8,128)(2,1)S(1)}, u32[]{:S(2)}, u32[]{:S(2)}) collective-permute-start(bf16[64,3712]{1,0:T(8,128)(2,1)S(1)} %get-tuple-element.46.own), channel_id=1, source_target_pairs={{0,4},{2,6},{4,0},{6,2},{1,5},{3,7},{5,1},{7,3},{8,12},{10,14},{12... | collective-permute-start | bytes 1425416 | tf_op jit(solution)/shard_map/ppermute | solution.py:18
  73.2 23.4 %collective-permute-start.12 = (bf16[64,3712]{1,0:T(8,128)(2,1)S(1)}, bf16[64,3712]{1,0:T(8,128)(2,1)S(1)}, u32[]{:S(2)}, u32[]{:S(2)}) collective-permute-start(bf16[64,3712]{1,0:T(8,128)(2,1)S(1)} %get-tuple-element.47.own), channel_id=1, source_target_pairs={{0,4},{2,6},{4,0},{6,2},{1,5},{3,7},{5,1},{7,3},{8,12},{10,14},{12... | collective-permute-start | bytes 1425416 | tf_op jit(solution)/shard_map/ppermute | solution.py:18
  93.9 13.8 %collective-permute-start.11 = (bf16[4,64,896]{2,1,0:T(8,128)(2,1)S(1)}, bf16[4,64,896]{2,1,0:T(8,128)(2,1)S(1)}, u32[]{:S(2)}, u32[]{:S(2)}) collective-permute-start(bf16[4,64,896]{2,1,0:T(8,128)(2,1)S(1)} %get-tuple-element.41), channel_id=1, source_target_pairs={{0,4},{2,6},{4,0},{6,2},{1,5},{3,7},{5,1},{7,3},{8,12},{10,14},{12... | collective-permute-start | bytes 1376264 | tf_op jit(solution)/shard_map/ppermute | solution.py:18
  102.0 0.9 copy-start.1
  102.9 14.8 %copy-start.2 = (f32[4,64,896]{2,1,0:T(8,128)S(1)}, f32[4,64,896]{2,1,0:T(8,128)}, u32[]{:S(2)}) copy-start(f32[4,64,896]{2,1,0:T(8,128)} %copy-done.1) | copy-start | bytes 2752516
  102.9 14.8 %collective-permute-start.13 = (bf16[4,64,896]{2,1,0:T(8,128)(2,1)S(1)}, bf16[4,64,896]{2,1,0:T(8,128)(2,1)S(1)}, u32[]{:S(2)}, u32[]{:S(2)}) collective-permute-start(bf16[4,64,896]{2,1,0:T(8,128)(2,1)S(1)} %get-tuple-element.43), channel_id=1, source_target_pairs={{0,4},{2,6},{4,0},{6,2},{1,5},{3,7},{5,1},{7,3},{8,12},{10,14},{12... | collective-permute-start | bytes 1376264 | tf_op jit(solution)/shard_map/ppermute | solution.py:18
  108.5 10.3 %all-to-all-start.1 = ((bf16[4,64,896]{2,1,0:T(8,128)(2,1)}), bf16[4,64,896]{2,1,0:T(8,128)(2,1)S(1)}, u32[]{:S(2)}, u32[]{:S(2)}) async-start(bf16[4,64,896]{2,1,0:T(8,128)(2,1)} %add_convert_fusion.1), calls=%async_computation.1 | async-start | bytes 917504 | tf_op jit(solution)/shard_map/all_to_all | solution.py:137
  118.8 11.2 %all-to-all-start.2 = ((bf16[4,64,896]{2,1,0:T(8,128)(2,1)}), bf16[4,64,896]{2,1,0:T(8,128)(2,1)S(1)}, u32[]{:S(2)}, u32[]{:S(2)}) async-start(bf16[4,64,896]{2,1,0:T(8,128)(2,1)} %add_convert_fusion), calls=%async_computation.2 | async-start | bytes 917504 | tf_op jit(solution)/shard_map/all_to_all | solution.py:137
  130.9 60.1 %copy-start.10 = (s32[1,64,1]{1,2,0:T(1,128)S(1)}, s32[1,64,1]{1,2,0:T(1,128)}, u32[]{:S(2)}) copy-start(s32[1,64,1]{1,2,0:T(1,128)} %param.12) | copy-start | bytes 772
  130.9 66.1 %copy-start.11 = (s32[1,64,1]{1,2,0:T(1,128)S(1)}, s32[1,64,1]{1,2,0:T(1,128)}, u32[]{:S(2)}) copy-start(s32[1,64,1]{1,2,0:T(1,128)} %param.14) | copy-start | bytes 772
  130.9 44.5 %all-to-all-start.3 = ((bf16[32,8,896]{2,1,0:T(8,128)(2,1)}), bf16[32,8,896]{2,1,0:T(8,128)(2,1)S(1)}, u32[]{:S(2)}, u32[]{:S(2)}) async-start(bf16[32,8,896]{2,1,0:T(8,128)(2,1)} %bitcast.25), calls=%async_computation.3 | async-start | bytes 917504 | tf_op jit(solution)/shard_map/all_to_all | solution.py:142
  138.6 17.8 %collective-permute-start.14 = (bf16[2,64,896]{2,1,0:T(8,128)(2,1)S(1)}, bf16[2,64,896]{2,1,0:T(8,128)(2,1)S(1)}, u32[]{:S(2)}, u32[]{:S(2)}) collective-permute-start(bf16[2,64,896]{2,1,0:T(8,128)(2,1)S(1)} %pad_maximum_fusion.3), channel_id=1, source_target_pairs={{0,256},{256,0},{1,257},{257,1},{2,258},{258,2},{3,259},{259,3},{4... | collective-permute-start | bytes 688136 | tf_op jit(solution)/shard_map/ppermute | solution.py:18
  175.4 37.9 %copy-start.3 = (bf16[32,8,896]{2,1,0:T(8,128)(2,1)}, bf16[32,8,896]{2,1,0:T(8,128)(2,1)S(1)}, u32[]{:S(2)}) copy-start(bf16[32,8,896]{2,1,0:T(8,128)(2,1)S(1)} %all-to-all-done.3) | copy-start | bytes 1376260
  175.4 40.6 %all-to-all-start.4 = ((bf16[32,8,896]{2,1,0:T(8,128)(2,1)}), bf16[32,8,896]{2,1,0:T(8,128)(2,1)S(1)}, u32[]{:S(2)}, u32[]{:S(2)}) async-start(bf16[32,8,896]{2,1,0:T(8,128)(2,1)} %bitcast.27), calls=%async_computation.4 | async-start | bytes 917504 | tf_op jit(solution)/shard_map/all_to_all | solution.py:142
  191.0 7.9 %collective-permute-start = (s32[1,64]{1,0:T(1,128)S(1)}, s32[1,64]{1,0:T(1,128)S(1)}, u32[]{:S(2)}, u32[]{:S(2)}) collective-permute-start(s32[1,64]{1,0:T(1,128)S(1)} %bitcast.62), channel_id=1, source_target_pairs={{0,64},{64,128},{128,192},{192,256},{256,320},{320,384},{384,448},... | collective-permute-start | bytes 776 | tf_op jit(solution)/shard_map/ppermute | solution.py:18
  197.0 16.3 %collective-permute-start.1 = (s32[1,64]{1,0:T(1,128)S(1)}, s32[1,64]{1,0:T(1,128)S(1)}, u32[]{:S(2)}, u32[]{:S(2)}) collective-permute-start(s32[1,64]{1,0:T(1,128)S(1)} %bitcast.64), channel_id=1, source_target_pairs={{0,448},{64,0},{128,64},{192,128},{256,192},{320,256},{384,320},{4... | collective-permute-start | bytes 776 | tf_op jit(solution)/shard_map/ppermute | solution.py:18
  198.9 14.3 %copy-start.8 = (s32[1,64]{1,0:T(1,128)}, s32[1,64]{1,0:T(1,128)S(1)}, u32[]{:S(2)}) copy-start(s32[1,64]{1,0:T(1,128)S(1)} %collective-permute-done.f_routes) | copy-start | bytes 772
  213.3 0.5 copy-start.9
  216.0 0.8 copy-start.4

commit v5 on v4

--- a/solution.py
+++ b/solution.py
@@ -80,57 +80,30 @@
     )(f_routes, b_routes, f_gates, b_gates, x, y)
 
 
-def unpack_into(routes, slots, out):
-    column, slot_column, _, _, places = order_of(routes[...])
-    table = (places == column * 8 + slot_column).astype(F32).astype(BF)
-    for q, within, at in column_chunks(out.shape[1]):
-        out[:, at] = jnp.dot(table, slots[q, :, within], preferred_element_type=F32).astype(BF)
-
-
-def unpack_first_kernel(odd, f_routes, b_routes, slots, out):
-    @pl.when(odd[0] == 1)
-    def _():
-        unpack_into(f_routes, slots, out)
-
-    @pl.when(odd[0] == 0)
-    def _():
-        unpack_into(b_routes, slots, out)
-
-
-def unpack_second_kernel(odd, f_routes, b_routes, first, slots, f_out, b_out):
-    @pl.when(odd[0] == 1)
-    def _():
-        f_out[...] = first[...]
-        unpack_into(b_routes, slots, b_out)
-
-    @pl.when(odd[0] == 0)
-    def _():
-        b_out[...] = first[...]
-        unpack_into(f_routes, slots, f_out)
-
-
-def unpack(odd, f_routes, b_routes, first, second):
-    quarters, tokens, part = first.shape
-    width = quarters * part
-    rows = jax.ShapeDtypeStruct((tokens, width), BF)
-    scalar = pl.BlockSpec(memory_space=pltpu.SMEM)
-    cost = pl.CostEstimate(
-        flops=2 * tokens * tokens * width, bytes_accessed=4 * tokens * width, transcendentals=0
-    )
-    done = pl.pallas_call(
-        unpack_first_kernel,
-        out_shape=rows,
-        in_specs=[scalar] + [VMEM] * 3,
-        out_specs=VMEM,
-        cost_estimate=cost,
-    )(odd, f_routes, b_routes, first)
+def unpack_kernel(f_routes, b_routes, slots, f_out, b_out):
+    tokens, width = f_out.shape
+    for number, (routes, out) in enumerate(((f_routes, f_out), (b_routes, b_out))):
+        column, slot_column, _, _, _ = order_of(routes[...])
+        places = jax.lax.broadcasted_iota(jnp.int32, (tokens, 2 * tokens), 1)
+        table = (places == column * 16 + number * 8 + slot_column).astype(F32).astype(BF)
+        for q, within, at in column_chunks(width):
+            out[:, at] = jnp.dot(table, slots[q, :, within], preferred_element_type=F32).astype(BF)
+
+
+def unpack(f_routes, b_routes, slots):
+    quarters, tokens, part = slots.shape
+    rows = jax.ShapeDtypeStruct((tokens // 2, quarters * part), BF)
     return pl.pallas_call(
-        unpack_second_kernel,
+        unpack_kernel,
         out_shape=(rows, rows),
-        in_specs=[scalar] + [VMEM] * 4,
+        in_specs=[VMEM] * 3,
         out_specs=(VMEM, VMEM),
-        cost_estimate=cost,
-    )(odd, f_routes, b_routes, done, second)
+        cost_estimate=pl.CostEstimate(
+            flops=2 * tokens * tokens * quarters * part,
+            bytes_accessed=4 * tokens * quarters * part,
+            transcendentals=0,
+        ),
+    )(f_routes, b_routes, slots)
 
 
 def spread(quarters):
@@ -138,9 +111,14 @@
 
 
 def go_home(parts, capacity):
-    blocks = jnp.stack(parts).reshape(-1, capacity, parts[0].shape[1])
-    homed = lax.all_to_all(blocks, ("y", "z"), split_axis=0, concat_axis=0, tiled=True)
-    return homed.reshape(len(parts), -1, blocks.shape[2])
+    width = parts[0][0].shape[1]
+    blocks = [
+        jnp.concatenate([rows.reshape(-1, capacity, width) for rows in pair], axis=1) for pair in parts
+    ]
+    homed = lax.all_to_all(
+        jnp.concatenate(blocks), ("y", "z"), split_axis=0, concat_axis=0, tiled=True
+    )
+    return homed.reshape(len(parts), -1, width)
 
 
 def column_chunks(width):
@@ -294,11 +272,17 @@
     f_out = (f_own + swap_rows(f_visited).astype(F32)).astype(BF)
     b_out = (b_own + swap_rows(b_visited).astype(F32)).astype(BF)
     f_spread, b_spread = spread(f_out), spread(b_out)
-    crossed = permute(jnp.stack([f_spread[3], b_spread[0]]), "h", (1, 0))
-    first = go_home([b_spread[1], f_spread[0], b_spread[3], f_spread[2]], capacity)
-    second = go_home([crossed[0], b_spread[2], f_spread[1], crossed[1]], capacity)
-    odd = lax.rem(lax.axis_index("y"), 2).astype(jnp.int32).reshape(1)
-    forward_next, backward_next = unpack(odd, f_moved, b_moved, first, second)
+    crossed = [permute(rows, "h", (1, 0)) for rows in (f_spread[3], b_spread[0])]
+    home = go_home(
+        [
+            (crossed[0], b_spread[1]),
+            (f_spread[0], b_spread[2]),
+            (f_spread[1], b_spread[3]),
+            (f_spread[2], crossed[1]),
+        ],
+        capacity,
+    )
+    forward_next, backward_next = unpack(f_moved, b_moved, home)
     return forward_next[None], backward_next[None]
 
 

time: 221 us -> 214 us (0.968)
  starting transfers between devices: 96.9 us -> 90.3 us
    all_to_all x2 -> x1, starting transfers between devices: 23.2 us -> 11.8 us  [go_home(): lax.all_to_all(jnp.concatenate(blocks), ('y', 'z'), split_axis=0, concat_...]
    all_to_all x2, waiting for transfers between devices: 5.92 us -> 0.01 us  [spread(): lax.all_to_all(quarters, 'y', split_axis=0, concat_axis=0, tiled=True)]
    ppermute x15 -> x16, starting transfers between devices: 50.9 us -> 56.4 us  [permute(): return lax.ppermute(block, axis, list(enumerate(targets)))]
    ppermute x15 -> x16, waiting for transfers between devices: 53 us -> 57.1 us  [permute(): return lax.ppermute(block, axis, list(enumerate(targets)))]
    all_to_all x2 -> x1, waiting for transfers between devices: 18.1 us -> 21.6 us  [go_home(): lax.all_to_all(jnp.concatenate(blocks), ('y', 'z'), split_axis=0, concat_...]
    pallas_call x2 -> x1, Pallas kernels: 4.73 us -> 2.56 us  [unpack(): pl.pallas_call(unpack_kernel, out_shape=(rows, rows), in_specs=[VMEM] * 3...]
  transfers between devices with their start and end apart: 20 -> 20, of which waited for: 12 -> 13; matrix products, arithmetic and copies ran while one was open for 1% -> 1% of each run, Pallas kernels for 6% -> 5%
where the time goes in v5:
time: 214 us; the launch traced here: 211 us
  waiting for transfers between devices  95.2 us (44%)
  starting transfers between devices  90.3 us (42%)
  Pallas kernels  17 us (8%)
  local copies, waits for them, and re-layouts  4.69 us (2%)
  other arithmetic  2.82 us (1%)
    ppermute x16, waiting for transfers between devices, permute(): return lax.ppermute(block, axis, list(enumerate(targets)))  57.1 us
    ppermute x16, starting transfers between devices, permute(): return lax.ppermute(block, axis, list(enumerate(targets)))  56.4 us
    all_to_all x1, waiting for transfers between devices, go_home(): lax.all_to_all(jnp.concatenate(blocks), ('y', 'z'), split_axis=0, concat_...  21.6 us
    all_to_all x1, waiting for transfers between devices, exchange(): return lax.all_to_all(block, 'z', split_axis=0, concat_axis=0, tiled=True)  16.5 us
    all_to_all x1, starting transfers between devices, exchange(): return lax.all_to_all(block, 'z', split_axis=0, concat_axis=0, tiled=True)  12.5 us
    all_to_all x1, starting transfers between devices, go_home(): lax.all_to_all(jnp.concatenate(blocks), ('y', 'z'), split_axis=0, concat_...  11.8 us
    pallas_call x2, Pallas kernels, expert_pass(): pl.pallas_call(kernel, out_shape=(jax.ShapeDtypeStruct(quarters, F32), ja...  11.5 us
    all_to_all x2, starting transfers between devices, spread(): lax.all_to_all(quarters, 'y', split_axis=0, concat_axis=0, tiled=True)  9.59 us
  transfers between devices with their start and end apart: 20, of which 13 were waited for; matrix products, arithmetic and copies ran while one was open for 1% of the time, Pallas kernels for 5%

profile of v5, /device:TPU:24, one launch (start us, length us, event | category | flops | bytes accessed | tf_op | source)
XLA Modules:
  0.0 211.1 jit_solution(6272730152826774275)
XLA Ops:
  0.6 3.0 %shard_map.113 = bf16[128,3712]{1,0:T(8,128)(2,1)} custom-call(s32[1,64]{1,0:T(1,128)} %bitcast.76, s32[1,64]{1,0:T(1,128)} %bitcast.78, bf16[1,64]{1,0:T(2,128)(2,1)} %bitcast.74, bf16[1,64]{1,0:T(2,128)(2,1)} %bitcast.75, bf16[64,3584]{1,0:T(8,128)(2,1)} %bitcast.66, bf16[64,3584]{1,0:T(8,128)(2,1)} %bitcast.67), custom_call_target="tpu_custom_call" | custom-call | flops 117440512 | bytes 1835008 | tf_op jit(solution)/shard_map/pallas_call | solution.py:72
  5.0 3.5 %collective-permute-start.3 = (bf16[3584,256]{1,0:T(8,128)(2,1)S(1)}, bf16[3584,256]{1,0:T(8,128)(2,1)}, u32[]{:S(2)}, u32[]{:S(2)}) collective-permute-start(bf16[3584,256]{1,0:T(8,128)(2,1)S(1)} %constant_dynamic-update-slice_fusion.refs_0_), channel_id=1, source_target_pairs={{0,2},{1,7},{2,0},{3,5},{4,6},{5,3},{6,4},{7,1},{8,10},{9,15},{10,... | collective-permute-start | bytes 5505032 | tf_op jit(solution)/shard_map/ppermute | solution.py:18
  8.6 12.5 %all-to-all-start = ((bf16[8,16,3712]{2,1,0:T(8,128)(2,1)}), bf16[8,16,3712]{2,1,0:T(8,128)(2,1)}, u32[]{:S(2)}, u32[]{:S(2)}) async-start(bf16[8,16,3712]{2,1,0:T(8,128)(2,1)} %bitcast.61), calls=%async_computation | async-start | bytes 1900544 | tf_op jit(solution)/shard_map/all_to_all | solution.py:35
  21.1 2.4 %collective-permute-start.2 = (bf16[3584,256]{1,0:T(8,128)(2,1)S(1)}, bf16[3584,256]{1,0:T(8,128)(2,1)}, u32[]{:S(2)}, u32[]{:S(2)}) collective-permute-start(bf16[3584,256]{1,0:T(8,128)(2,1)S(1)} %constant_dynamic-update-slice_fusion.refs_0_), channel_id=1, source_target_pairs={{0,1},{1,0},{2,3},{3,2},{4,5},{5,4},{6,7},{7,6},{8,9},{9,8},{10,11... | collective-permute-start | bytes 5505032 | tf_op jit(solution)/shard_map/ppermute | solution.py:18
  23.6 2.1 %collective-permute-start.6 = (bf16[128,3584]{1,0:T(8,128)(2,1)S(1)}, bf16[128,3584]{1,0:T(8,128)(2,1)}, u32[]{:S(2)}, u32[]{:S(2)}) collective-permute-start(bf16[128,3584]{1,0:T(8,128)(2,1)S(1)} %bitcast.56), channel_id=1, source_target_pairs={{0,2},{1,7},{2,0},{3,5},{4,6},{5,3},{6,4},{7,1},{8,10},{9,15},{10,... | collective-permute-start | bytes 2752520 | tf_op jit(solution)/shard_map/ppermute | solution.py:18
  25.7 4.7 %collective-permute-done.3.refs_2_ = bf16[3584,256]{1,0:T(8,128)(2,1)} collective-permute-done((bf16[3584,256]{1,0:T(8,128)(2,1)S(1)}, bf16[3584,256]{1,0:T(8,128)(2,1)}, u32[]{:S(2)}, u32[]{:S(2)}) %collective-permute-start.3) | collective-permute-done | bytes 1835040 | tf_op jit(solution)/shard_map/ppermute | solution.py:18
  32.3 2.4 %collective-permute-start.5 = (bf16[128,3584]{1,0:T(8,128)(2,1)S(1)}, bf16[128,3584]{1,0:T(8,128)(2,1)}, u32[]{:S(2)}, u32[]{:S(2)}) collective-permute-start(bf16[128,3584]{1,0:T(8,128)(2,1)S(1)} %bitcast.57), channel_id=1, source_target_pairs={{0,1},{1,0},{2,3},{3,2},{4,5},{5,4},{6,7},{7,6},{8,9},{9,8},{10,11... | collective-permute-start | bytes 2752520 | tf_op jit(solution)/shard_map/ppermute | solution.py:18
  34.7 5.5 %collective-permute-done.6.refs_6_ = bf16[128,3584]{1,0:T(8,128)(2,1)} collective-permute-done((bf16[128,3584]{1,0:T(8,128)(2,1)S(1)}, bf16[128,3584]{1,0:T(8,128)(2,1)}, u32[]{:S(2)}, u32[]{:S(2)}) %collective-permute-start.6) | collective-permute-done | bytes 917536 | tf_op jit(solution)/shard_map/ppermute | solution.py:18
  42.4 3.2 %collective-permute-start.8 = (bf16[2,2,8,2,8,128]{5,4,3,2,0,1:T(8,128)(2,1)S(1)}, bf16[2,2,8,2,8,128]{5,4,3,2,0,1:T(8,128)(2,1)S(1)}, u32[]{:S(2)}, u32[]{:S(2)}) collective-permute-start(bf16[2,2,8,2,8,128]{5,4,3,2,0,1:T(8,128)(2,1)S(1)} %pad_maximum_fusion.1), channel_id=1, source_target_pairs={{0,2},{1,7},{2,0},{3,5},{4,6},{5,3},{6,4},{7,1},{8,10},{9,15},{10,... | collective-permute-start | bytes 393224 | tf_op jit(solution)/shard_map/ppermute | solution.py:18
  45.7 3.6 %collective-permute-done.8 = bf16[2,2,8,2,8,128]{5,4,3,2,0,1:T(8,128)(2,1)S(1)} collective-permute-done((bf16[2,2,8,2,8,128]{5,4,3,2,0,1:T(8,128)(2,1)S(1)}, bf16[2,2,8,2,8,128]{5,4,3,2,0,1:T(8,128)(2,1)S(1)}, u32[]{:S(2)}, u32[]{:S(2)}) %collective-permute-start.8) | collective-permute-done | bytes 131104 | tf_op jit(solution)/shard_map/ppermute | solution.py:18
  49.3 2.3 %collective-permute-start.9 = (bf16[2,2,2,8,8,128]{5,4,3,2,1,0:T(8,128)(2,1)S(1)}, bf16[2,2,2,8,8,128]{5,4,3,2,1,0:T(8,128)(2,1)S(1)}, u32[]{:S(2)}, u32[]{:S(2)}) collective-permute-start(bf16[2,2,2,8,8,128]{5,4,3,2,1,0:T(8,128)(2,1)S(1)} %bitcast.69), channel_id=1, source_target_pairs={{0,1},{1,0},{2,3},{3,2},{4,5},{5,4},{6,7},{7,6},{8,9},{9,8},{10,11... | collective-permute-start | bytes 393224 | tf_op jit(solution)/shard_map/ppermute | solution.py:18
  52.7 16.5 %all-to-all-done = bf16[8,16,3712]{2,1,0:T(8,128)(2,1)} async-done(((bf16[8,16,3712]{2,1,0:T(8,128)(2,1)}), bf16[8,16,3712]{2,1,0:T(8,128)(2,1)}, u32[]{:S(2)}, u32[]{:S(2)}) %all-to-all-start) | async-done | bytes 950304 | tf_op jit(solution)/shard_map/all_to_all | solution.py:35
  70.5 2.7 %collective-permute-start.10 = (bf16[64,3712]{1,0:T(8,128)(2,1)S(1)}, bf16[64,3712]{1,0:T(8,128)(2,1)S(1)}, u32[]{:S(2)}, u32[]{:S(2)}) collective-permute-start(bf16[64,3712]{1,0:T(8,128)(2,1)S(1)} %get-tuple-element.46.own), channel_id=1, source_target_pairs={{0,4},{2,6},{4,0},{6,2},{1,5},{3,7},{5,1},{7,3},{8,12},{10,14},{12... | collective-permute-start | bytes 1425416 | tf_op jit(solution)/shard_map/ppermute | solution.py:18
  73.2 4.6 %collective-permute-start.13 = (bf16[64,3712]{1,0:T(8,128)(2,1)S(1)}, bf16[64,3712]{1,0:T(8,128)(2,1)S(1)}, u32[]{:S(2)}, u32[]{:S(2)}) collective-permute-start(bf16[64,3712]{1,0:T(8,128)(2,1)S(1)} %get-tuple-element.47.own), channel_id=1, source_target_pairs={{0,4},{2,6},{4,0},{6,2},{1,5},{3,7},{5,1},{7,3},{8,12},{10,14},{12... | collective-permute-start | bytes 1425416 | tf_op jit(solution)/shard_map/ppermute | solution.py:18
  77.8 9.8 %collective-permute-done.10.visiting = bf16[64,3712]{1,0:T(8,128)(2,1)S(1)} collective-permute-done((bf16[64,3712]{1,0:T(8,128)(2,1)S(1)}, bf16[64,3712]{1,0:T(8,128)(2,1)S(1)}, u32[]{:S(2)}, u32[]{:S(2)}) %collective-permute-start.10) | collective-permute-done | bytes 475168 | tf_op jit(solution)/shard_map/ppermute | solution.py:18
  87.6 5.3 %shard_map.114 = (f32[4,64,896]{2,1,0:T(8,128)S(1)}, bf16[4,64,896]{2,1,0:T(8,128)(2,1)S(1)}) custom-call(bf16[64,3712]{1,0:T(8,128)(2,1)S(1)} %get-tuple-element.46.own, bf16[64,3712]{1,0:T(8,128)(2,1)S(1)} %collective-permute-done.10.visiting, bf16[3584,256]{1,0:T(8,128)(2,1)S(1)} %constant_dynamic-update-slice_fusion.refs_0_, ...), custom_call_target="tpu_custom_call" | custom-call | flops 1409286144 | bytes 13303808 | tf_op jit(solution)/shard_map/pallas_call | solution.py:203
  92.9 2.8 %collective-permute-start.11 = (bf16[4,64,896]{2,1,0:T(8,128)(2,1)S(1)}, bf16[4,64,896]{2,1,0:T(8,128)(2,1)S(1)}, u32[]{:S(2)}, u32[]{:S(2)}) collective-permute-start(bf16[4,64,896]{2,1,0:T(8,128)(2,1)S(1)} %get-tuple-element.40), channel_id=1, source_target_pairs={{0,4},{2,6},{4,0},{6,2},{1,5},{3,7},{5,1},{7,3},{8,12},{10,14},{12... | collective-permute-start | bytes 1376264 | tf_op jit(solution)/shard_map/ppermute | solution.py:18
  96.6 6.2 %shard_map.115 = (f32[4,64,896]{2,1,0:T(8,128)S(1)}, bf16[4,64,896]{2,1,0:T(8,128)(2,1)S(1)}) custom-call(bf16[64,3712]{1,0:T(8,128)(2,1)S(1)} %get-tuple-element.47.own, bf16[64,3712]{1,0:T(8,128)(2,1)S(1)} %collective-permute-done.13.visiting, bf16[4,2,128,128]{3,2,1,0:T(8,128)(2,1)S(1)} %bitcast.60, ...), custom_call_target="tpu_custom_call" | custom-call | flops 1409286144 | bytes 13303808 | tf_op jit(solution)/shard_map/pallas_call | solution.py:203
  103.7 3.9 %collective-permute-start.14 = (bf16[4,64,896]{2,1,0:T(8,128)(2,1)S(1)}, bf16[4,64,896]{2,1,0:T(8,128)(2,1)S(1)}, u32[]{:S(2)}, u32[]{:S(2)}) collective-permute-start(bf16[4,64,896]{2,1,0:T(8,128)(2,1)S(1)} %get-tuple-element.43), channel_id=1, source_target_pairs={{0,4},{2,6},{4,0},{6,2},{1,5},{3,7},{5,1},{7,3},{8,12},{10,14},{12... | collective-permute-start | bytes 1376264 | tf_op jit(solution)/shard_map/ppermute | solution.py:18
  108.5 4.7 %all-to-all-start.1 = ((bf16[4,64,896]{2,1,0:T(8,128)(2,1)}), bf16[4,64,896]{2,1,0:T(8,128)(2,1)S(1)}, u32[]{:S(2)}, u32[]{:S(2)}) async-start(bf16[4,64,896]{2,1,0:T(8,128)(2,1)} %add_convert_fusion.1), calls=%async_computation.1 | async-start | bytes 917504 | tf_op jit(solution)/shard_map/all_to_all | solution.py:110
  113.2 5.4 %collective-permute-done.14 = bf16[4,64,896]{2,1,0:T(8,128)(2,1)S(1)} collective-permute-done((bf16[4,64,896]{2,1,0:T(8,128)(2,1)S(1)}, bf16[4,64,896]{2,1,0:T(8,128)(2,1)S(1)}, u32[]{:S(2)}, u32[]{:S(2)}) %collective-permute-start.14) | collective-permute-done | bytes 458784 | tf_op jit(solution)/shard_map/ppermute | solution.py:18
  119.4 4.9 %all-to-all-start.2 = ((bf16[4,64,896]{2,1,0:T(8,128)(2,1)}), bf16[4,64,896]{2,1,0:T(8,128)(2,1)S(1)}, u32[]{:S(2)}, u32[]{:S(2)}) async-start(bf16[4,64,896]{2,1,0:T(8,128)(2,1)} %add_convert_fusion), calls=%async_computation.2 | async-start | bytes 917504 | tf_op jit(solution)/shard_map/all_to_all | solution.py:110
  124.4 8.2 %collective-permute-start.12 = (bf16[64,896]{1,0:T(8,128)(2,1)S(1)}, bf16[64,896]{1,0:T(8,128)(2,1)S(1)}, u32[]{:S(2)}, u32[]{:S(2)}) collective-permute-start(bf16[64,896]{1,0:T(8,128)(2,1)S(1)} %get-tuple-element.48), channel_id=1, source_target_pairs={{0,256},{256,0},{1,257},{257,1},{2,258},{258,2},{3,259},{259,3},{4... | collective-permute-start | bytes 344072 | tf_op jit(solution)/shard_map/ppermute | solution.py:18
  132.7 6.3 %collective-permute-start.15 = (bf16[64,896]{1,0:T(8,128)(2,1)S(1)}, bf16[64,896]{1,0:T(8,128)(2,1)S(1)}, u32[]{:S(2)}, u32[]{:S(2)}) collective-permute-start(bf16[64,896]{1,0:T(8,128)(2,1)S(1)} %get-tuple-element.53), channel_id=1, source_target_pairs={{0,256},{256,0},{1,257},{257,1},{2,258},{258,2},{3,259},{259,3},{4... | collective-permute-start | bytes 344072 | tf_op jit(solution)/shard_map/ppermute | solution.py:18
  139.0 7.2 %collective-permute-done.12 = bf16[64,896]{1,0:T(8,128)(2,1)S(1)} collective-permute-done((bf16[64,896]{1,0:T(8,128)(2,1)S(1)}, bf16[64,896]{1,0:T(8,128)(2,1)S(1)}, u32[]{:S(2)}, u32[]{:S(2)}) %collective-permute-start.12) | collective-permute-done | bytes 114720 | tf_op jit(solution)/shard_map/ppermute | solution.py:18
  146.2 4.7 %collective-permute-done.15 = bf16[64,896]{1,0:T(8,128)(2,1)S(1)} collective-permute-done((bf16[64,896]{1,0:T(8,128)(2,1)S(1)}, bf16[64,896]{1,0:T(8,128)(2,1)S(1)}, u32[]{:S(2)}, u32[]{:S(2)}) %collective-permute-start.15) | collective-permute-done | bytes 114720 | tf_op jit(solution)/shard_map/ppermute | solution.py:18
  151.9 11.8 %all-to-all-start.3 = ((bf16[32,16,896]{2,1,0:T(8,128)(2,1)}), bf16[32,16,896]{2,1,0:T(8,128)(2,1)S(1)}, u32[]{:S(2)}, u32[]{:S(2)}) async-start(bf16[32,16,896]{2,1,0:T(8,128)(2,1)} %maximum_maximum_fusion), calls=%async_computation.3 | async-start | bytes 1835008 | tf_op jit(solution)/shard_map/all_to_all | solution.py:118
  163.7 5.9 %collective-permute-start = (s32[1,64]{1,0:T(1,128)S(1)}, s32[1,64]{1,0:T(1,128)S(1)}, u32[]{:S(2)}, u32[]{:S(2)}) collective-permute-start(s32[1,64]{1,0:T(1,128)S(1)} %bitcast.77), channel_id=1, source_target_pairs={{0,64},{64,128},{128,192},{192,256},{256,320},{320,384},{384,448},... | collective-permute-start | bytes 776 | tf_op jit(solution)/shard_map/ppermute | solution.py:18
  171.6 9.3 %collective-permute-done.f_routes = s32[1,64]{1,0:T(1,128)S(1)} collective-permute-done((s32[1,64]{1,0:T(1,128)S(1)}, s32[1,64]{1,0:T(1,128)S(1)}, u32[]{:S(2)}, u32[]{:S(2)}) %collective-permute-start) | collective-permute-done | bytes 288 | tf_op jit(solution)/shard_map/ppermute | solution.py:18
  180.9 5.0 %collective-permute-done.1.b_routes = s32[1,64]{1,0:T(1,128)S(1)} collective-permute-done((s32[1,64]{1,0:T(1,128)S(1)}, s32[1,64]{1,0:T(1,128)S(1)}, u32[]{:S(2)}, u32[]{:S(2)}) %collective-permute-start.1) | collective-permute-done | bytes 288 | tf_op jit(solution)/shard_map/ppermute | solution.py:18
  185.9 21.6 %all-to-all-done.3 = bf16[32,16,896]{2,1,0:T(8,128)(2,1)S(1)} async-done(((bf16[32,16,896]{2,1,0:T(8,128)(2,1)}), bf16[32,16,896]{2,1,0:T(8,128)(2,1)S(1)}, u32[]{:S(2)}, u32[]{:S(2)}) %all-to-all-start.3) | async-done | bytes 917536 | tf_op jit(solution)/shard_map/all_to_all | solution.py:118
  208.5 2.6 %shard_map.116 = (bf16[64,3584]{1,0:T(8,128)(2,1)}, bf16[64,3584]{1,0:T(8,128)(2,1)}) custom-call(s32[1,64]{1,0:T(1,128)} %copy-done.9, s32[1,64]{1,0:T(1,128)} %copy-done.10, bf16[4,128,896]{2,1,0:T(8,128)(2,1)} %bitcast.62), custom_call_target="tpu_custom_call" | custom-call | flops 117440512 | bytes 1835008 | tf_op jit(solution)/shard_map/pallas_call | solution.py:96
  (50 shorter events, 15.3 us)
Async XLA Ops:
  0.6 3.0 %copy-start.4 = (bf16[1,3584,128]{2,1,0:T(8,128)(2,1)S(1)}, bf16[1,3584,128]{2,1,0:T(8,128)(2,1)}, u32[]{:S(2)}) copy-start(bf16[1,3584,128]{2,1,0:T(8,128)(2,1)} %param.17) | copy-start | bytes 2752516
  3.6 1.2 copy-start.5
  4.8 18.8 %copy-start = (bf16[1,128,3584]{2,1,0:T(8,128)(2,1)S(1)}, bf16[1,128,3584]{2,1,0:T(8,128)(2,1)}, u32[]{:S(2)}) copy-start(bf16[1,128,3584]{2,1,0:T(8,128)(2,1)} %param.19) | copy-start | bytes 2752516
  4.8 37.5 %copy-start.6 = (bf16[1,2,64,8,128]{4,3,2,1,0:T(8,128)(2,1)S(1)}, bf16[1,2,64,8,128]{4,3,2,1,0:T(8,128)(2,1)}, u32[]{:S(2)}) copy-start(bf16[1,2,64,8,128]{4,3,2,1,0:T(8,128)(2,1)} %param.16) | copy-start | bytes 786436
  5.0 25.4 %collective-permute-start.3 = (bf16[3584,256]{1,0:T(8,128)(2,1)S(1)}, bf16[3584,256]{1,0:T(8,128)(2,1)}, u32[]{:S(2)}, u32[]{:S(2)}) collective-permute-start(bf16[3584,256]{1,0:T(8,128)(2,1)S(1)} %constant_dynamic-update-slice_fusion.refs_0_), channel_id=1, source_target_pairs={{0,2},{1,7},{2,0},{3,5},{4,6},{5,3},{6,4},{7,1},{8,10},{9,15},{10,... | collective-permute-start | bytes 5505032 | tf_op jit(solution)/shard_map/ppermute | solution.py:18
  8.6 60.7 %all-to-all-start = ((bf16[8,16,3712]{2,1,0:T(8,128)(2,1)}), bf16[8,16,3712]{2,1,0:T(8,128)(2,1)}, u32[]{:S(2)}, u32[]{:S(2)}) async-start(bf16[8,16,3712]{2,1,0:T(8,128)(2,1)} %bitcast.61), calls=%async_computation | async-start | bytes 1900544 | tf_op jit(solution)/shard_map/all_to_all | solution.py:35
  21.1 21.2 %collective-permute-start.2 = (bf16[3584,256]{1,0:T(8,128)(2,1)S(1)}, bf16[3584,256]{1,0:T(8,128)(2,1)}, u32[]{:S(2)}, u32[]{:S(2)}) collective-permute-start(bf16[3584,256]{1,0:T(8,128)(2,1)S(1)} %constant_dynamic-update-slice_fusion.refs_0_), channel_id=1, source_target_pairs={{0,1},{1,0},{2,3},{3,2},{4,5},{5,4},{6,7},{7,6},{8,9},{9,8},{10,11... | collective-permute-start | bytes 5505032 | tf_op jit(solution)/shard_map/ppermute | solution.py:18
  23.6 16.7 %collective-permute-start.6 = (bf16[128,3584]{1,0:T(8,128)(2,1)S(1)}, bf16[128,3584]{1,0:T(8,128)(2,1)}, u32[]{:S(2)}, u32[]{:S(2)}) collective-permute-start(bf16[128,3584]{1,0:T(8,128)(2,1)S(1)} %bitcast.56), channel_id=1, source_target_pairs={{0,2},{1,7},{2,0},{3,5},{4,6},{5,3},{6,4},{7,1},{8,10},{9,15},{10,... | collective-permute-start | bytes 2752520 | tf_op jit(solution)/shard_map/ppermute | solution.py:18
  30.4 38.8 %collective-permute-start.4 = (bf16[3584,256]{1,0:T(8,128)(2,1)}, bf16[3584,256]{1,0:T(8,128)(2,1)}, u32[]{:S(2)}, u32[]{:S(2)}) collective-permute-start(bf16[3584,256]{1,0:T(8,128)(2,1)} %collective-permute-done.3.refs_2_), channel_id=1, source_target_pairs={{0,1},{1,0},{2,3},{3,2},{4,5},{5,4},{6,7},{7,6},{8,9},{9,8},{10,11... | collective-permute-start | bytes 5505032 | tf_op jit(solution)/shard_map/ppermute | solution.py:18
  32.3 20.3 %collective-permute-start.5 = (bf16[128,3584]{1,0:T(8,128)(2,1)S(1)}, bf16[128,3584]{1,0:T(8,128)(2,1)}, u32[]{:S(2)}, u32[]{:S(2)}) collective-permute-start(bf16[128,3584]{1,0:T(8,128)(2,1)S(1)} %bitcast.57), channel_id=1, source_target_pairs={{0,1},{1,0},{2,3},{3,2},{4,5},{5,4},{6,7},{7,6},{8,9},{9,8},{10,11... | collective-permute-start | bytes 2752520 | tf_op jit(solution)/shard_map/ppermute | solution.py:18
  40.2 12.5 %collective-permute-start.7 = (bf16[128,3584]{1,0:T(8,128)(2,1)}, bf16[128,3584]{1,0:T(8,128)(2,1)}, u32[]{:S(2)}, u32[]{:S(2)}) collective-permute-start(bf16[128,3584]{1,0:T(8,128)(2,1)} %collective-permute-done.6.refs_6_), channel_id=1, source_target_pairs={{0,1},{1,0},{2,3},{3,2},{4,5},{5,4},{6,7},{7,6},{8,9},{9,8},{10,11... | collective-permute-start | bytes 2752520 | tf_op jit(solution)/shard_map/ppermute | solution.py:18
  42.4 6.9 %collective-permute-start.8 = (bf16[2,2,8,2,8,128]{5,4,3,2,0,1:T(8,128)(2,1)S(1)}, bf16[2,2,8,2,8,128]{5,4,3,2,0,1:T(8,128)(2,1)S(1)}, u32[]{:S(2)}, u32[]{:S(2)}) collective-permute-start(bf16[2,2,8,2,8,128]{5,4,3,2,0,1:T(8,128)(2,1)S(1)} %pad_maximum_fusion.1), channel_id=1, source_target_pairs={{0,2},{1,7},{2,0},{3,5},{4,6},{5,3},{6,4},{7,1},{8,10},{9,15},{10,... | collective-permute-start | bytes 393224 | tf_op jit(solution)/shard_map/ppermute | solution.py:18
  49.3 3.3 %collective-permute-start.9 = (bf16[2,2,2,8,8,128]{5,4,3,2,1,0:T(8,128)(2,1)S(1)}, bf16[2,2,2,8,8,128]{5,4,3,2,1,0:T(8,128)(2,1)S(1)}, u32[]{:S(2)}, u32[]{:S(2)}) collective-permute-start(bf16[2,2,2,8,8,128]{5,4,3,2,1,0:T(8,128)(2,1)S(1)} %bitcast.69), channel_id=1, source_target_pairs={{0,1},{1,0},{2,3},{3,2},{4,5},{5,4},{6,7},{7,6},{8,9},{9,8},{10,11... | collective-permute-start | bytes 393224 | tf_op jit(solution)/shard_map/ppermute | solution.py:18
  70.5 17.2 %collective-permute-start.10 = (bf16[64,3712]{1,0:T(8,128)(2,1)S(1)}, bf16[64,3712]{1,0:T(8,128)(2,1)S(1)}, u32[]{:S(2)}, u32[]{:S(2)}) collective-permute-start(bf16[64,3712]{1,0:T(8,128)(2,1)S(1)} %get-tuple-element.46.own), channel_id=1, source_target_pairs={{0,4},{2,6},{4,0},{6,2},{1,5},{3,7},{5,1},{7,3},{8,12},{10,14},{12... | collective-permute-start | bytes 1425416 | tf_op jit(solution)/shard_map/ppermute | solution.py:18
  73.2 23.4 %collective-permute-start.13 = (bf16[64,3712]{1,0:T(8,128)(2,1)S(1)}, bf16[64,3712]{1,0:T(8,128)(2,1)S(1)}, u32[]{:S(2)}, u32[]{:S(2)}) collective-permute-start(bf16[64,3712]{1,0:T(8,128)(2,1)S(1)} %get-tuple-element.47.own), channel_id=1, source_target_pairs={{0,4},{2,6},{4,0},{6,2},{1,5},{3,7},{5,1},{7,3},{8,12},{10,14},{12... | collective-permute-start | bytes 1425416 | tf_op jit(solution)/shard_map/ppermute | solution.py:18
  92.9 14.7 %collective-permute-start.11 = (bf16[4,64,896]{2,1,0:T(8,128)(2,1)S(1)}, bf16[4,64,896]{2,1,0:T(8,128)(2,1)S(1)}, u32[]{:S(2)}, u32[]{:S(2)}) collective-permute-start(bf16[4,64,896]{2,1,0:T(8,128)(2,1)S(1)} %get-tuple-element.40), channel_id=1, source_target_pairs={{0,4},{2,6},{4,0},{6,2},{1,5},{3,7},{5,1},{7,3},{8,12},{10,14},{12... | collective-permute-start | bytes 1376264 | tf_op jit(solution)/shard_map/ppermute | solution.py:18
  102.8 0.9 copy-start.1
  103.7 14.8 %copy-start.2 = (f32[4,64,896]{2,1,0:T(8,128)S(1)}, f32[4,64,896]{2,1,0:T(8,128)}, u32[]{:S(2)}) copy-start(f32[4,64,896]{2,1,0:T(8,128)} %copy-done.1) | copy-start | bytes 2752516
  103.7 14.8 %collective-permute-start.14 = (bf16[4,64,896]{2,1,0:T(8,128)(2,1)S(1)}, bf16[4,64,896]{2,1,0:T(8,128)(2,1)S(1)}, u32[]{:S(2)}, u32[]{:S(2)}) collective-permute-start(bf16[4,64,896]{2,1,0:T(8,128)(2,1)S(1)} %get-tuple-element.43), channel_id=1, source_target_pairs={{0,4},{2,6},{4,0},{6,2},{1,5},{3,7},{5,1},{7,3},{8,12},{10,14},{12... | collective-permute-start | bytes 1376264 | tf_op jit(solution)/shard_map/ppermute | solution.py:18
  108.5 11.0 %all-to-all-start.1 = ((bf16[4,64,896]{2,1,0:T(8,128)(2,1)}), bf16[4,64,896]{2,1,0:T(8,128)(2,1)S(1)}, u32[]{:S(2)}, u32[]{:S(2)}) async-start(bf16[4,64,896]{2,1,0:T(8,128)(2,1)} %add_convert_fusion.1), calls=%async_computation.1 | async-start | bytes 917504 | tf_op jit(solution)/shard_map/all_to_all | solution.py:110
  119.4 13.2 %all-to-all-start.2 = ((bf16[4,64,896]{2,1,0:T(8,128)(2,1)}), bf16[4,64,896]{2,1,0:T(8,128)(2,1)S(1)}, u32[]{:S(2)}, u32[]{:S(2)}) async-start(bf16[4,64,896]{2,1,0:T(8,128)(2,1)} %add_convert_fusion), calls=%async_computation.2 | async-start | bytes 917504 | tf_op jit(solution)/shard_map/all_to_all | solution.py:110
  124.4 21.8 %collective-permute-start.12 = (bf16[64,896]{1,0:T(8,128)(2,1)S(1)}, bf16[64,896]{1,0:T(8,128)(2,1)S(1)}, u32[]{:S(2)}, u32[]{:S(2)}) collective-permute-start(bf16[64,896]{1,0:T(8,128)(2,1)S(1)} %get-tuple-element.48), channel_id=1, source_target_pairs={{0,256},{256,0},{1,257},{257,1},{2,258},{258,2},{3,259},{259,3},{4... | collective-permute-start | bytes 344072 | tf_op jit(solution)/shard_map/ppermute | solution.py:18
  132.7 18.2 %collective-permute-start.15 = (bf16[64,896]{1,0:T(8,128)(2,1)S(1)}, bf16[64,896]{1,0:T(8,128)(2,1)S(1)}, u32[]{:S(2)}, u32[]{:S(2)}) collective-permute-start(bf16[64,896]{1,0:T(8,128)(2,1)S(1)} %get-tuple-element.53), channel_id=1, source_target_pairs={{0,256},{256,0},{1,257},{257,1},{2,258},{258,2},{3,259},{259,3},{4... | collective-permute-start | bytes 344072 | tf_op jit(solution)/shard_map/ppermute | solution.py:18
  150.9 12.8 %copy-start.7 = (s32[1,64,1]{1,2,0:T(1,128)S(1)}, s32[1,64,1]{1,2,0:T(1,128)}, u32[]{:S(2)}) copy-start(s32[1,64,1]{1,2,0:T(1,128)} %param.12) | copy-start | bytes 772
  150.9 18.8 %copy-start.8 = (s32[1,64,1]{1,2,0:T(1,128)S(1)}, s32[1,64,1]{1,2,0:T(1,128)}, u32[]{:S(2)}) copy-start(s32[1,64,1]{1,2,0:T(1,128)} %param.14) | copy-start | bytes 772
  151.9 55.6 %all-to-all-start.3 = ((bf16[32,16,896]{2,1,0:T(8,128)(2,1)}), bf16[32,16,896]{2,1,0:T(8,128)(2,1)S(1)}, u32[]{:S(2)}, u32[]{:S(2)}) async-start(bf16[32,16,896]{2,1,0:T(8,128)(2,1)} %maximum_maximum_fusion), calls=%async_computation.3 | async-start | bytes 1835008 | tf_op jit(solution)/shard_map/all_to_all | solution.py:118
  163.7 17.2 %collective-permute-start = (s32[1,64]{1,0:T(1,128)S(1)}, s32[1,64]{1,0:T(1,128)S(1)}, u32[]{:S(2)}, u32[]{:S(2)}) collective-permute-start(s32[1,64]{1,0:T(1,128)S(1)} %bitcast.77), channel_id=1, source_target_pairs={{0,64},{64,128},{128,192},{192,256},{256,320},{320,384},{384,448},... | collective-permute-start | bytes 776 | tf_op jit(solution)/shard_map/ppermute | solution.py:18
  169.7 16.3 %collective-permute-start.1 = (s32[1,64]{1,0:T(1,128)S(1)}, s32[1,64]{1,0:T(1,128)S(1)}, u32[]{:S(2)}, u32[]{:S(2)}) collective-permute-start(s32[1,64]{1,0:T(1,128)S(1)} %bitcast.79), channel_id=1, source_target_pairs={{0,448},{64,0},{128,64},{192,128},{256,192},{320,256},{384,320},{4... | collective-permute-start | bytes 776 | tf_op jit(solution)/shard_map/ppermute | solution.py:18
  180.9 26.7 %copy-start.9 = (s32[1,64]{1,0:T(1,128)}, s32[1,64]{1,0:T(1,128)S(1)}, u32[]{:S(2)}) copy-start(s32[1,64]{1,0:T(1,128)S(1)} %collective-permute-done.f_routes) | copy-start | bytes 772
  185.9 21.6 %copy-start.10 = (s32[1,64]{1,0:T(1,128)}, s32[1,64]{1,0:T(1,128)S(1)}, u32[]{:S(2)}) copy-start(s32[1,64]{1,0:T(1,128)S(1)} %collective-permute-done.1.b_routes) | copy-start | bytes 772
  207.6 0.9 copy-start.3

commit v6 on v5

--- a/solution.py
+++ b/solution.py
@@ -240,7 +240,7 @@
     own_weights = [jnp.concatenate([gate_here, up_here], axis=1), down_here]
     beside_weights = [swap_weights(mine) for mine in own_weights]
     across_weights = [swap_core(mine) for mine in own_weights]
-    across_weights[0], saved = lax.optimization_barrier((across_weights[0], saved))
+    across_weights[1], saved = lax.optimization_barrier((across_weights[1], saved))
     weights = []
     for mine, across, beside in zip(own_weights, across_weights, beside_weights):
         weights += [mine, across, beside, swap_core(beside)]
@@ -261,7 +261,7 @@
 
     f_moved = permute(f_routes, ("h", "y"), [(i + 1) % 8 for i in range(8)])
     b_moved = permute(b_routes, ("h", "y"), [(i - 1) % 8 for i in range(8)])
-    arrived, weights, kept = lax.optimization_barrier((arrived, weights, kept))
+    arrived, across_weights[0], kept = lax.optimization_barrier((arrived, across_weights[0], kept))
 
     f_rows = arrived[:, :capacity].reshape(nz * capacity, -1)
     b_rows = arrived[:, capacity:].reshape(nz * capacity, -1)

time: 214 us -> 207 us (0.967)
  starting transfers between devices: 90.3 us -> 86.3 us
  waiting for transfers between devices: 95.2 us -> 92 us
    all_to_all x1, waiting for transfers between devices: 16.5 us -> 4.47 us  [exchange(): return lax.all_to_all(block, 'z', split_axis=0, concat_axis=0, tiled=True)]
    ppermute x16, waiting for transfers between devices: 57.1 us -> 65 us  [permute(): return lax.ppermute(block, axis, list(enumerate(targets)))]
    all_to_all x1, starting transfers between devices: 11.8 us -> 5.03 us  [go_home(): lax.all_to_all(jnp.concatenate(blocks), ('y', 'z'), split_axis=0, concat_...]
  transfers between devices with their start and end apart: 20 -> 20, of which waited for: 13 -> 12; matrix products, arithmetic and copies ran while one was open for 1% -> 2% of each run, Pallas kernels for 5% -> 6%
where the time goes in v6:
time: 207 us; the launch traced here: 204 us
  waiting for transfers between devices  92 us (44%)
  starting transfers between devices  86.3 us (42%)
  Pallas kernels  17 us (8%)
  local copies, waits for them, and re-layouts  4.98 us (2%)
  other arithmetic  2.81 us (1%)
    ppermute x16, waiting for transfers between devices, permute(): return lax.ppermute(block, axis, list(enumerate(targets)))  65 us
    ppermute x16, starting transfers between devices, permute(): return lax.ppermute(block, axis, list(enumerate(targets)))  58.5 us
    all_to_all x1, waiting for transfers between devices, go_home(): lax.all_to_all(jnp.concatenate(blocks), ('y', 'z'), split_axis=0, concat_...  20.5 us
    all_to_all x1, starting transfers between devices, exchange(): return lax.all_to_all(block, 'z', split_axis=0, concat_axis=0, tiled=True)  12.5 us
    pallas_call x2, Pallas kernels, expert_pass(): pl.pallas_call(kernel, out_shape=(jax.ShapeDtypeStruct(quarters, F32), ja...  11.5 us
    all_to_all x2, starting transfers between devices, spread(): lax.all_to_all(quarters, 'y', split_axis=0, concat_axis=0, tiled=True)  10.2 us
    all_to_all x1, starting transfers between devices, go_home(): lax.all_to_all(jnp.concatenate(blocks), ('y', 'z'), split_axis=0, concat_...  5.03 us
    all_to_all x1, waiting for transfers between devices, exchange(): return lax.all_to_all(block, 'z', split_axis=0, concat_axis=0, tiled=True)  4.47 us
  transfers between devices with their start and end apart: 20, of which 12 were waited for; matrix products, arithmetic and copies ran while one was open for 2% of the time, Pallas kernels for 6%

profile of v6, /device:TPU:24, one launch (start us, length us, event | category | flops | bytes accessed | tf_op | source)
XLA Modules:
  0.0 204.0 jit_solution(9445493065398185524)
XLA Ops:
  0.6 2.9 %shard_map.113 = bf16[128,3712]{1,0:T(8,128)(2,1)} custom-call(s32[1,64]{1,0:T(1,128)} %bitcast.76, s32[1,64]{1,0:T(1,128)} %bitcast.78, bf16[1,64]{1,0:T(2,128)(2,1)} %bitcast.74, bf16[1,64]{1,0:T(2,128)(2,1)} %bitcast.75, bf16[64,3584]{1,0:T(8,128)(2,1)} %bitcast.66, bf16[64,3584]{1,0:T(8,128)(2,1)} %bitcast.67), custom_call_target="tpu_custom_call" | custom-call | flops 117440512 | bytes 1835008 | tf_op jit(solution)/shard_map/pallas_call | solution.py:72
  3.5 12.5 %all-to-all-start = ((bf16[8,16,3712]{2,1,0:T(8,128)(2,1)}), bf16[8,16,3712]{2,1,0:T(8,128)(2,1)}, u32[]{:S(2)}, u32[]{:S(2)}) async-start(bf16[8,16,3712]{2,1,0:T(8,128)(2,1)} %bitcast.61), calls=%async_computation | async-start | bytes 1900544 | tf_op jit(solution)/shard_map/all_to_all | solution.py:35
  17.8 3.4 %collective-permute-start.7 = (bf16[3584,256]{1,0:T(8,128)(2,1)S(1)}, bf16[3584,256]{1,0:T(8,128)(2,1)}, u32[]{:S(2)}, u32[]{:S(2)}) collective-permute-start(bf16[3584,256]{1,0:T(8,128)(2,1)S(1)} %constant_dynamic-update-slice_fusion.refs_0_), channel_id=1, source_target_pairs={{0,2},{1,7},{2,0},{3,5},{4,6},{5,3},{6,4},{7,1},{8,10},{9,15},{10,... | collective-permute-start | bytes 5505032 | tf_op jit(solution)/shard_map/ppermute | solution.py:18
  21.2 2.5 %collective-permute-start.2 = (bf16[3584,256]{1,0:T(8,128)(2,1)S(1)}, bf16[3584,256]{1,0:T(8,128)(2,1)}, u32[]{:S(2)}, u32[]{:S(2)}) collective-permute-start(bf16[3584,256]{1,0:T(8,128)(2,1)S(1)} %constant_dynamic-update-slice_fusion.refs_0_), channel_id=1, source_target_pairs={{0,1},{1,0},{2,3},{3,2},{4,5},{5,4},{6,7},{7,6},{8,9},{9,8},{10,11... | collective-permute-start | bytes 5505032 | tf_op jit(solution)/shard_map/ppermute | solution.py:18
  25.6 2.4 %collective-permute-start.9 = (bf16[128,3584]{1,0:T(8,128)(2,1)S(1)}, bf16[128,3584]{1,0:T(8,128)(2,1)}, u32[]{:S(2)}, u32[]{:S(2)}) collective-permute-start(bf16[128,3584]{1,0:T(8,128)(2,1)S(1)} %bitcast.57), channel_id=1, source_target_pairs={{0,2},{1,7},{2,0},{3,5},{4,6},{5,3},{6,4},{7,1},{8,10},{9,15},{10,... | collective-permute-start | bytes 2752520 | tf_op jit(solution)/shard_map/ppermute | solution.py:18
  28.6 3.0 %collective-permute-start.4 = (bf16[2,2,8,2,8,128]{5,4,3,2,0,1:T(8,128)(2,1)S(1)}, bf16[2,2,8,2,8,128]{5,4,3,2,0,1:T(8,128)(2,1)S(1)}, u32[]{:S(2)}, u32[]{:S(2)}) collective-permute-start(bf16[2,2,8,2,8,128]{5,4,3,2,0,1:T(8,128)(2,1)S(1)} %pad_maximum_fusion.1), channel_id=1, source_target_pairs={{0,2},{1,7},{2,0},{3,5},{4,6},{5,3},{6,4},{7,1},{8,10},{9,15},{10,... | collective-permute-start | bytes 393224 | tf_op jit(solution)/shard_map/ppermute | solution.py:18
  31.6 11.4 %collective-permute-done.7.refs_2_ = bf16[3584,256]{1,0:T(8,128)(2,1)} collective-permute-done((bf16[3584,256]{1,0:T(8,128)(2,1)S(1)}, bf16[3584,256]{1,0:T(8,128)(2,1)}, u32[]{:S(2)}, u32[]{:S(2)}) %collective-permute-start.7) | collective-permute-done | bytes 1835040 | tf_op jit(solution)/shard_map/ppermute | solution.py:18
  45.0 9.2 %collective-permute-done.4 = bf16[2,2,8,2,8,128]{5,4,3,2,0,1:T(8,128)(2,1)S(1)} collective-permute-done((bf16[2,2,8,2,8,128]{5,4,3,2,0,1:T(8,128)(2,1)S(1)}, bf16[2,2,8,2,8,128]{5,4,3,2,0,1:T(8,128)(2,1)S(1)}, u32[]{:S(2)}, u32[]{:S(2)}) %collective-permute-start.4) | collective-permute-done | bytes 131104 | tf_op jit(solution)/shard_map/ppermute | solution.py:18
  54.2 1.9 collective-permute-start.5
  56.2 2.4 %collective-permute-start.10 = (bf16[128,3584]{1,0:T(8,128)(2,1)}, bf16[128,3584]{1,0:T(8,128)(2,1)}, u32[]{:S(2)}, u32[]{:S(2)}) collective-permute-start(bf16[128,3584]{1,0:T(8,128)(2,1)} %collective-permute-done.9.refs_6_), channel_id=1, source_target_pairs={{0,1},{1,0},{2,3},{3,2},{4,5},{5,4},{6,7},{7,6},{8,9},{9,8},{10,11... | collective-permute-start | bytes 2752520 | tf_op jit(solution)/shard_map/ppermute | solution.py:18
  58.7 4.5 %all-to-all-done = bf16[8,16,3712]{2,1,0:T(8,128)(2,1)} async-done(((bf16[8,16,3712]{2,1,0:T(8,128)(2,1)}), bf16[8,16,3712]{2,1,0:T(8,128)(2,1)}, u32[]{:S(2)}, u32[]{:S(2)}) %all-to-all-start) | async-done | bytes 950304 | tf_op jit(solution)/shard_map/all_to_all | solution.py:35
  64.4 4.9 %collective-permute-start.6 = (bf16[64,3712]{1,0:T(8,128)(2,1)S(1)}, bf16[64,3712]{1,0:T(8,128)(2,1)S(1)}, u32[]{:S(2)}, u32[]{:S(2)}) collective-permute-start(bf16[64,3712]{1,0:T(8,128)(2,1)S(1)} %get-tuple-element.30.own), channel_id=1, source_target_pairs={{0,4},{2,6},{4,0},{6,2},{1,5},{3,7},{5,1},{7,3},{8,12},{10,14},{12... | collective-permute-start | bytes 1425416 | tf_op jit(solution)/shard_map/ppermute | solution.py:18
  69.3 2.4 %collective-permute-start.13 = (bf16[64,3712]{1,0:T(8,128)(2,1)S(1)}, bf16[64,3712]{1,0:T(8,128)(2,1)S(1)}, u32[]{:S(2)}, u32[]{:S(2)}) collective-permute-start(bf16[64,3712]{1,0:T(8,128)(2,1)S(1)} %get-tuple-element.31.own), channel_id=1, source_target_pairs={{0,4},{2,6},{4,0},{6,2},{1,5},{3,7},{5,1},{7,3},{8,12},{10,14},{12... | collective-permute-start | bytes 1425416 | tf_op jit(solution)/shard_map/ppermute | solution.py:18
  71.8 9.8 %collective-permute-done.6.visiting = bf16[64,3712]{1,0:T(8,128)(2,1)S(1)} collective-permute-done((bf16[64,3712]{1,0:T(8,128)(2,1)S(1)}, bf16[64,3712]{1,0:T(8,128)(2,1)S(1)}, u32[]{:S(2)}, u32[]{:S(2)}) %collective-permute-start.6) | collective-permute-done | bytes 475168 | tf_op jit(solution)/shard_map/ppermute | solution.py:18
  81.6 5.3 %shard_map.114 = (f32[4,64,896]{2,1,0:T(8,128)S(1)}, bf16[4,64,896]{2,1,0:T(8,128)(2,1)S(1)}) custom-call(bf16[64,3712]{1,0:T(8,128)(2,1)S(1)} %get-tuple-element.30.own, bf16[64,3712]{1,0:T(8,128)(2,1)S(1)} %collective-permute-done.6.visiting, bf16[3584,256]{1,0:T(8,128)(2,1)S(1)} %constant_dynamic-update-slice_fusion.refs_0_, ...), custom_call_target="tpu_custom_call" | custom-call | flops 1409286144 | bytes 13303808 | tf_op jit(solution)/shard_map/pallas_call | solution.py:203
  86.9 4.9 %collective-permute-start.11 = (bf16[4,64,896]{2,1,0:T(8,128)(2,1)S(1)}, bf16[4,64,896]{2,1,0:T(8,128)(2,1)S(1)}, u32[]{:S(2)}, u32[]{:S(2)}) collective-permute-start(bf16[4,64,896]{2,1,0:T(8,128)(2,1)S(1)} %get-tuple-element.24), channel_id=1, source_target_pairs={{0,4},{2,6},{4,0},{6,2},{1,5},{3,7},{5,1},{7,3},{8,12},{10,14},{12... | collective-permute-start | bytes 1376264 | tf_op jit(solution)/shard_map/ppermute | solution.py:18
  91.9 6.2 %shard_map.115 = (f32[4,64,896]{2,1,0:T(8,128)S(1)}, bf16[4,64,896]{2,1,0:T(8,128)(2,1)S(1)}) custom-call(bf16[64,3712]{1,0:T(8,128)(2,1)S(1)} %get-tuple-element.31.own, bf16[64,3712]{1,0:T(8,128)(2,1)S(1)} %collective-permute-done.13.visiting, bf16[4,2,128,128]{3,2,1,0:T(8,128)(2,1)S(1)} %bitcast.60, ...), custom_call_target="tpu_custom_call" | custom-call | flops 1409286144 | bytes 13303808 | tf_op jit(solution)/shard_map/pallas_call | solution.py:203
  99.0 3.6 %collective-permute-start.14 = (bf16[4,64,896]{2,1,0:T(8,128)(2,1)S(1)}, bf16[4,64,896]{2,1,0:T(8,128)(2,1)S(1)}, u32[]{:S(2)}, u32[]{:S(2)}) collective-permute-start(bf16[4,64,896]{2,1,0:T(8,128)(2,1)S(1)} %get-tuple-element.27), channel_id=1, source_target_pairs={{0,4},{2,6},{4,0},{6,2},{1,5},{3,7},{5,1},{7,3},{8,12},{10,14},{12... | collective-permute-start | bytes 1376264 | tf_op jit(solution)/shard_map/ppermute | solution.py:18
  103.6 4.7 %all-to-all-start.1 = ((bf16[4,64,896]{2,1,0:T(8,128)(2,1)}), bf16[4,64,896]{2,1,0:T(8,128)(2,1)S(1)}, u32[]{:S(2)}, u32[]{:S(2)}) async-start(bf16[4,64,896]{2,1,0:T(8,128)(2,1)} %add_convert_fusion.1), calls=%async_computation.1 | async-start | bytes 917504 | tf_op jit(solution)/shard_map/all_to_all | solution.py:110
  108.2 2.8 %collective-permute-done.14 = bf16[4,64,896]{2,1,0:T(8,128)(2,1)S(1)} collective-permute-done((bf16[4,64,896]{2,1,0:T(8,128)(2,1)S(1)}, bf16[4,64,896]{2,1,0:T(8,128)(2,1)S(1)}, u32[]{:S(2)}, u32[]{:S(2)}) %collective-permute-start.14) | collective-permute-done | bytes 458784 | tf_op jit(solution)/shard_map/ppermute | solution.py:18
  111.9 2.0 all-to-all-done.1
  113.9 5.5 %all-to-all-start.2 = ((bf16[4,64,896]{2,1,0:T(8,128)(2,1)}), bf16[4,64,896]{2,1,0:T(8,128)(2,1)S(1)}, u32[]{:S(2)}, u32[]{:S(2)}) async-start(bf16[4,64,896]{2,1,0:T(8,128)(2,1)} %add_convert_fusion), calls=%async_computation.2 | async-start | bytes 917504 | tf_op jit(solution)/shard_map/all_to_all | solution.py:110
  119.5 8.2 %collective-permute-start.12 = (bf16[64,896]{1,0:T(8,128)(2,1)S(1)}, bf16[64,896]{1,0:T(8,128)(2,1)S(1)}, u32[]{:S(2)}, u32[]{:S(2)}) collective-permute-start(bf16[64,896]{1,0:T(8,128)(2,1)S(1)} %get-tuple-element.32), channel_id=1, source_target_pairs={{0,256},{256,0},{1,257},{257,1},{2,258},{258,2},{3,259},{259,3},{4... | collective-permute-start | bytes 344072 | tf_op jit(solution)/shard_map/ppermute | solution.py:18
  127.7 6.4 %collective-permute-start.15 = (bf16[64,896]{1,0:T(8,128)(2,1)S(1)}, bf16[64,896]{1,0:T(8,128)(2,1)S(1)}, u32[]{:S(2)}, u32[]{:S(2)}) collective-permute-start(bf16[64,896]{1,0:T(8,128)(2,1)S(1)} %get-tuple-element.37), channel_id=1, source_target_pairs={{0,256},{256,0},{1,257},{257,1},{2,258},{258,2},{3,259},{259,3},{4... | collective-permute-start | bytes 344072 | tf_op jit(solution)/shard_map/ppermute | solution.py:18
  134.1 10.6 %collective-permute-done.12 = bf16[64,896]{1,0:T(8,128)(2,1)S(1)} collective-permute-done((bf16[64,896]{1,0:T(8,128)(2,1)S(1)}, bf16[64,896]{1,0:T(8,128)(2,1)S(1)}, u32[]{:S(2)}, u32[]{:S(2)}) %collective-permute-start.12) | collective-permute-done | bytes 114720 | tf_op jit(solution)/shard_map/ppermute | solution.py:18
  144.7 6.3 %collective-permute-done.15 = bf16[64,896]{1,0:T(8,128)(2,1)S(1)} collective-permute-done((bf16[64,896]{1,0:T(8,128)(2,1)S(1)}, bf16[64,896]{1,0:T(8,128)(2,1)S(1)}, u32[]{:S(2)}, u32[]{:S(2)}) %collective-permute-start.15) | collective-permute-done | bytes 114720 | tf_op jit(solution)/shard_map/ppermute | solution.py:18
  152.0 5.0 %all-to-all-start.3 = ((bf16[32,16,896]{2,1,0:T(8,128)(2,1)}), bf16[32,16,896]{2,1,0:T(8,128)(2,1)S(1)}, u32[]{:S(2)}, u32[]{:S(2)}) async-start(bf16[32,16,896]{2,1,0:T(8,128)(2,1)} %maximum_maximum_fusion), calls=%async_computation.3 | async-start | bytes 1835008 | tf_op jit(solution)/shard_map/all_to_all | solution.py:118
  157.1 6.7 %collective-permute-start = (s32[1,64]{1,0:T(1,128)S(1)}, s32[1,64]{1,0:T(1,128)S(1)}, u32[]{:S(2)}, u32[]{:S(2)}) collective-permute-start(s32[1,64]{1,0:T(1,128)S(1)} %bitcast.77), channel_id=1, source_target_pairs={{0,64},{64,128},{128,192},{192,256},{256,320},{320,384},{384,448},... | collective-permute-start | bytes 776 | tf_op jit(solution)/shard_map/ppermute | solution.py:18
  165.7 8.2 %collective-permute-done.f_routes = s32[1,64]{1,0:T(1,128)S(1)} collective-permute-done((s32[1,64]{1,0:T(1,128)S(1)}, s32[1,64]{1,0:T(1,128)S(1)}, u32[]{:S(2)}, u32[]{:S(2)}) %collective-permute-start) | collective-permute-done | bytes 288 | tf_op jit(solution)/shard_map/ppermute | solution.py:18
  173.9 6.1 %collective-permute-done.1.b_routes = s32[1,64]{1,0:T(1,128)S(1)} collective-permute-done((s32[1,64]{1,0:T(1,128)S(1)}, s32[1,64]{1,0:T(1,128)S(1)}, u32[]{:S(2)}, u32[]{:S(2)}) %collective-permute-start.1) | collective-permute-done | bytes 288 | tf_op jit(solution)/shard_map/ppermute | solution.py:18
  180.0 20.5 %all-to-all-done.3 = bf16[32,16,896]{2,1,0:T(8,128)(2,1)S(1)} async-done(((bf16[32,16,896]{2,1,0:T(8,128)(2,1)}), bf16[32,16,896]{2,1,0:T(8,128)(2,1)S(1)}, u32[]{:S(2)}, u32[]{:S(2)}) %all-to-all-start.3) | async-done | bytes 917536 | tf_op jit(solution)/shard_map/all_to_all | solution.py:118
  201.5 2.6 %shard_map.116 = (bf16[64,3584]{1,0:T(8,128)(2,1)}, bf16[64,3584]{1,0:T(8,128)(2,1)}) custom-call(s32[1,64]{1,0:T(1,128)} %copy-done.8, s32[1,64]{1,0:T(1,128)} %copy-done.9, bf16[4,128,896]{2,1,0:T(8,128)(2,1)} %bitcast.62), custom_call_target="tpu_custom_call" | custom-call | flops 117440512 | bytes 1835008 | tf_op jit(solution)/shard_map/pallas_call | solution.py:96
  (48 shorter events, 14.0 us)
Async XLA Ops:
  3.5 59.6 %all-to-all-start = ((bf16[8,16,3712]{2,1,0:T(8,128)(2,1)}), bf16[8,16,3712]{2,1,0:T(8,128)(2,1)}, u32[]{:S(2)}, u32[]{:S(2)}) async-start(bf16[8,16,3712]{2,1,0:T(8,128)(2,1)} %bitcast.61), calls=%async_computation | async-start | bytes 1900544 | tf_op jit(solution)/shard_map/all_to_all | solution.py:35
  16.1 1.5 copy-start.4
  16.1 7.6 %copy-start = (bf16[1,128,3584]{2,1,0:T(8,128)(2,1)S(1)}, bf16[1,128,3584]{2,1,0:T(8,128)(2,1)}, u32[]{:S(2)}) copy-start(bf16[1,128,3584]{2,1,0:T(8,128)(2,1)} %param.19) | copy-start | bytes 2752516
  16.1 12.4 %copy-start.5 = (bf16[1,2,64,8,128]{4,3,2,1,0:T(8,128)(2,1)S(1)}, bf16[1,2,64,8,128]{4,3,2,1,0:T(8,128)(2,1)}, u32[]{:S(2)}) copy-start(bf16[1,2,64,8,128]{4,3,2,1,0:T(8,128)(2,1)} %param.16) | copy-start | bytes 786436
  17.8 25.2 %collective-permute-start.7 = (bf16[3584,256]{1,0:T(8,128)(2,1)S(1)}, bf16[3584,256]{1,0:T(8,128)(2,1)}, u32[]{:S(2)}, u32[]{:S(2)}) collective-permute-start(bf16[3584,256]{1,0:T(8,128)(2,1)S(1)} %constant_dynamic-update-slice_fusion.refs_0_), channel_id=1, source_target_pairs={{0,2},{1,7},{2,0},{3,5},{4,6},{5,3},{6,4},{7,1},{8,10},{9,15},{10,... | collective-permute-start | bytes 5505032 | tf_op jit(solution)/shard_map/ppermute | solution.py:18
  21.2 37.5 %collective-permute-start.2 = (bf16[3584,256]{1,0:T(8,128)(2,1)S(1)}, bf16[3584,256]{1,0:T(8,128)(2,1)}, u32[]{:S(2)}, u32[]{:S(2)}) collective-permute-start(bf16[3584,256]{1,0:T(8,128)(2,1)S(1)} %constant_dynamic-update-slice_fusion.refs_0_), channel_id=1, source_target_pairs={{0,1},{1,0},{2,3},{3,2},{4,5},{5,4},{6,7},{7,6},{8,9},{9,8},{10,11... | collective-permute-start | bytes 5505032 | tf_op jit(solution)/shard_map/ppermute | solution.py:18
  23.7 4.8 %collective-permute-start.3 = (bf16[128,3584]{1,0:T(8,128)(2,1)S(1)}, bf16[128,3584]{1,0:T(8,128)(2,1)}, u32[]{:S(2)}, u32[]{:S(2)}) collective-permute-start(bf16[128,3584]{1,0:T(8,128)(2,1)S(1)} %bitcast.56), channel_id=1, source_target_pairs={{0,1},{1,0},{2,3},{3,2},{4,5},{5,4},{6,7},{7,6},{8,9},{9,8},{10,11... | collective-permute-start | bytes 2752520 | tf_op jit(solution)/shard_map/ppermute | solution.py:18
  25.6 30.5 %collective-permute-start.9 = (bf16[128,3584]{1,0:T(8,128)(2,1)S(1)}, bf16[128,3584]{1,0:T(8,128)(2,1)}, u32[]{:S(2)}, u32[]{:S(2)}) collective-permute-start(bf16[128,3584]{1,0:T(8,128)(2,1)S(1)} %bitcast.57), channel_id=1, source_target_pairs={{0,2},{1,7},{2,0},{3,5},{4,6},{5,3},{6,4},{7,1},{8,10},{9,15},{10,... | collective-permute-start | bytes 2752520 | tf_op jit(solution)/shard_map/ppermute | solution.py:18
  28.6 25.6 %collective-permute-start.4 = (bf16[2,2,8,2,8,128]{5,4,3,2,0,1:T(8,128)(2,1)S(1)}, bf16[2,2,8,2,8,128]{5,4,3,2,0,1:T(8,128)(2,1)S(1)}, u32[]{:S(2)}, u32[]{:S(2)}) collective-permute-start(bf16[2,2,8,2,8,128]{5,4,3,2,0,1:T(8,128)(2,1)S(1)} %pad_maximum_fusion.1), channel_id=1, source_target_pairs={{0,2},{1,7},{2,0},{3,5},{4,6},{5,3},{6,4},{7,1},{8,10},{9,15},{10,... | collective-permute-start | bytes 393224 | tf_op jit(solution)/shard_map/ppermute | solution.py:18
  43.0 28.7 %collective-permute-start.8 = (bf16[3584,256]{1,0:T(8,128)(2,1)}, bf16[3584,256]{1,0:T(8,128)(2,1)}, u32[]{:S(2)}, u32[]{:S(2)}) collective-permute-start(bf16[3584,256]{1,0:T(8,128)(2,1)} %collective-permute-done.7.refs_2_), channel_id=1, source_target_pairs={{0,1},{1,0},{2,3},{3,2},{4,5},{5,4},{6,7},{7,6},{8,9},{9,8},{10,11... | collective-permute-start | bytes 5505032 | tf_op jit(solution)/shard_map/ppermute | solution.py:18
  54.2 4.4 %collective-permute-start.5 = (bf16[2,2,2,8,8,128]{5,4,3,2,1,0:T(8,128)(2,1)S(1)}, bf16[2,2,2,8,8,128]{5,4,3,2,1,0:T(8,128)(2,1)S(1)}, u32[]{:S(2)}, u32[]{:S(2)}) collective-permute-start(bf16[2,2,2,8,8,128]{5,4,3,2,1,0:T(8,128)(2,1)S(1)} %bitcast.69), channel_id=1, source_target_pairs={{0,1},{1,0},{2,3},{3,2},{4,5},{5,4},{6,7},{7,6},{8,9},{9,8},{10,11... | collective-permute-start | bytes 393224 | tf_op jit(solution)/shard_map/ppermute | solution.py:18
  56.2 15.6 %collective-permute-start.10 = (bf16[128,3584]{1,0:T(8,128)(2,1)}, bf16[128,3584]{1,0:T(8,128)(2,1)}, u32[]{:S(2)}, u32[]{:S(2)}) collective-permute-start(bf16[128,3584]{1,0:T(8,128)(2,1)} %collective-permute-done.9.refs_6_), channel_id=1, source_target_pairs={{0,1},{1,0},{2,3},{3,2},{4,5},{5,4},{6,7},{7,6},{8,9},{9,8},{10,11... | collective-permute-start | bytes 2752520 | tf_op jit(solution)/shard_map/ppermute | solution.py:18
  64.4 17.2 %collective-permute-start.6 = (bf16[64,3712]{1,0:T(8,128)(2,1)S(1)}, bf16[64,3712]{1,0:T(8,128)(2,1)S(1)}, u32[]{:S(2)}, u32[]{:S(2)}) collective-permute-start(bf16[64,3712]{1,0:T(8,128)(2,1)S(1)} %get-tuple-element.30.own), channel_id=1, source_target_pairs={{0,4},{2,6},{4,0},{6,2},{1,5},{3,7},{5,1},{7,3},{8,12},{10,14},{12... | collective-permute-start | bytes 1425416 | tf_op jit(solution)/shard_map/ppermute | solution.py:18
  69.3 22.5 %collective-permute-start.13 = (bf16[64,3712]{1,0:T(8,128)(2,1)S(1)}, bf16[64,3712]{1,0:T(8,128)(2,1)S(1)}, u32[]{:S(2)}, u32[]{:S(2)}) collective-permute-start(bf16[64,3712]{1,0:T(8,128)(2,1)S(1)} %get-tuple-element.31.own), channel_id=1, source_target_pairs={{0,4},{2,6},{4,0},{6,2},{1,5},{3,7},{5,1},{7,3},{8,12},{10,14},{12... | collective-permute-start | bytes 1425416 | tf_op jit(solution)/shard_map/ppermute | solution.py:18
  86.9 15.8 %collective-permute-start.11 = (bf16[4,64,896]{2,1,0:T(8,128)(2,1)S(1)}, bf16[4,64,896]{2,1,0:T(8,128)(2,1)S(1)}, u32[]{:S(2)}, u32[]{:S(2)}) collective-permute-start(bf16[4,64,896]{2,1,0:T(8,128)(2,1)S(1)} %get-tuple-element.24), channel_id=1, source_target_pairs={{0,4},{2,6},{4,0},{6,2},{1,5},{3,7},{5,1},{7,3},{8,12},{10,14},{12... | collective-permute-start | bytes 1376264 | tf_op jit(solution)/shard_map/ppermute | solution.py:18
  98.1 0.9 copy-start.1
  99.0 12.0 %copy-start.2 = (f32[4,64,896]{2,1,0:T(8,128)S(1)}, f32[4,64,896]{2,1,0:T(8,128)}, u32[]{:S(2)}) copy-start(f32[4,64,896]{2,1,0:T(8,128)} %copy-done.1) | copy-start | bytes 2752516
  99.0 12.0 %collective-permute-start.14 = (bf16[4,64,896]{2,1,0:T(8,128)(2,1)S(1)}, bf16[4,64,896]{2,1,0:T(8,128)(2,1)S(1)}, u32[]{:S(2)}, u32[]{:S(2)}) collective-permute-start(bf16[4,64,896]{2,1,0:T(8,128)(2,1)S(1)} %get-tuple-element.27), channel_id=1, source_target_pairs={{0,4},{2,6},{4,0},{6,2},{1,5},{3,7},{5,1},{7,3},{8,12},{10,14},{12... | collective-permute-start | bytes 1376264 | tf_op jit(solution)/shard_map/ppermute | solution.py:18
  103.6 10.3 %all-to-all-start.1 = ((bf16[4,64,896]{2,1,0:T(8,128)(2,1)}), bf16[4,64,896]{2,1,0:T(8,128)(2,1)S(1)}, u32[]{:S(2)}, u32[]{:S(2)}) async-start(bf16[4,64,896]{2,1,0:T(8,128)(2,1)} %add_convert_fusion.1), calls=%async_computation.1 | async-start | bytes 917504 | tf_op jit(solution)/shard_map/all_to_all | solution.py:110
  113.9 13.8 %all-to-all-start.2 = ((bf16[4,64,896]{2,1,0:T(8,128)(2,1)}), bf16[4,64,896]{2,1,0:T(8,128)(2,1)S(1)}, u32[]{:S(2)}, u32[]{:S(2)}) async-start(bf16[4,64,896]{2,1,0:T(8,128)(2,1)} %add_convert_fusion), calls=%async_computation.2 | async-start | bytes 917504 | tf_op jit(solution)/shard_map/all_to_all | solution.py:110
  119.5 25.2 %collective-permute-start.12 = (bf16[64,896]{1,0:T(8,128)(2,1)S(1)}, bf16[64,896]{1,0:T(8,128)(2,1)S(1)}, u32[]{:S(2)}, u32[]{:S(2)}) collective-permute-start(bf16[64,896]{1,0:T(8,128)(2,1)S(1)} %get-tuple-element.32), channel_id=1, source_target_pairs={{0,256},{256,0},{1,257},{257,1},{2,258},{258,2},{3,259},{259,3},{4... | collective-permute-start | bytes 344072 | tf_op jit(solution)/shard_map/ppermute | solution.py:18
  127.7 23.3 %collective-permute-start.15 = (bf16[64,896]{1,0:T(8,128)(2,1)S(1)}, bf16[64,896]{1,0:T(8,128)(2,1)S(1)}, u32[]{:S(2)}, u32[]{:S(2)}) collective-permute-start(bf16[64,896]{1,0:T(8,128)(2,1)S(1)} %get-tuple-element.37), channel_id=1, source_target_pairs={{0,256},{256,0},{1,257},{257,1},{2,258},{258,2},{3,259},{259,3},{4... | collective-permute-start | bytes 344072 | tf_op jit(solution)/shard_map/ppermute | solution.py:18
  151.0 6.1 %copy-start.6 = (s32[1,64,1]{1,2,0:T(1,128)S(1)}, s32[1,64,1]{1,2,0:T(1,128)}, u32[]{:S(2)}) copy-start(s32[1,64,1]{1,2,0:T(1,128)} %param.12) | copy-start | bytes 772
  151.0 12.7 %copy-start.7 = (s32[1,64,1]{1,2,0:T(1,128)S(1)}, s32[1,64,1]{1,2,0:T(1,128)}, u32[]{:S(2)}) copy-start(s32[1,64,1]{1,2,0:T(1,128)} %param.14) | copy-start | bytes 772
  152.0 48.5 %all-to-all-start.3 = ((bf16[32,16,896]{2,1,0:T(8,128)(2,1)}), bf16[32,16,896]{2,1,0:T(8,128)(2,1)S(1)}, u32[]{:S(2)}, u32[]{:S(2)}) async-start(bf16[32,16,896]{2,1,0:T(8,128)(2,1)} %maximum_maximum_fusion), calls=%async_computation.3 | async-start | bytes 1835008 | tf_op jit(solution)/shard_map/all_to_all | solution.py:118
  157.1 16.8 %collective-permute-start = (s32[1,64]{1,0:T(1,128)S(1)}, s32[1,64]{1,0:T(1,128)S(1)}, u32[]{:S(2)}, u32[]{:S(2)}) collective-permute-start(s32[1,64]{1,0:T(1,128)S(1)} %bitcast.77), channel_id=1, source_target_pairs={{0,64},{64,128},{128,192},{192,256},{256,320},{320,384},{384,448},... | collective-permute-start | bytes 776 | tf_op jit(solution)/shard_map/ppermute | solution.py:18
  163.7 16.3 %collective-permute-start.1 = (s32[1,64]{1,0:T(1,128)S(1)}, s32[1,64]{1,0:T(1,128)S(1)}, u32[]{:S(2)}, u32[]{:S(2)}) collective-permute-start(s32[1,64]{1,0:T(1,128)S(1)} %bitcast.79), channel_id=1, source_target_pairs={{0,448},{64,0},{128,64},{192,128},{256,192},{320,256},{384,320},{4... | collective-permute-start | bytes 776 | tf_op jit(solution)/shard_map/ppermute | solution.py:18
  173.9 26.7 %copy-start.8 = (s32[1,64]{1,0:T(1,128)}, s32[1,64]{1,0:T(1,128)S(1)}, u32[]{:S(2)}) copy-start(s32[1,64]{1,0:T(1,128)S(1)} %collective-permute-done.f_routes) | copy-start | bytes 772
  180.0 20.5 %copy-start.9 = (s32[1,64]{1,0:T(1,128)}, s32[1,64]{1,0:T(1,128)S(1)}, u32[]{:S(2)}) copy-start(s32[1,64]{1,0:T(1,128)S(1)} %collective-permute-done.1.b_routes) | copy-start | bytes 772
  200.5 0.9 copy-start.3

commit v7 on v6

--- a/solution.py
+++ b/solution.py
@@ -130,21 +130,22 @@
 
 
 def load_weights(refs, gate_up, down, sems):
+    units = down.shape[0] // 4
     for u in range(4):
         yield (
             pltpu.make_async_copy(refs[u], gate_up.at[u], sems.at[u]),
-            pltpu.make_async_copy(refs[4 + u], down.at[u], sems.at[4 + u]),
+            pltpu.make_async_copy(refs[4 + u], down.at[pl.ds(u * units, units), :], sems.at[4 + u]),
         )
 
 
 def forward_kernel(own, visiting, *refs):
     weights, (out_own, out_visiting, rows, gate_up, down, hidden, sems) = refs[:8], refs[8:]
     copies = list(load_weights(weights, gate_up, down, sems))
-    for pair in copies:
-        pair[0].start()
-        pair[1].start()
+    for kind in (0, 1):
+        for pair in copies:
+            pair[kind].start()
     half, width = own.shape[0], rows.shape[1]
-    units = down.shape[1]
+    units = down.shape[0] // 4
     gates = [ref[:, pl.ds(width, GATE_COLUMNS)].astype(F32)[:, :1] for ref in (own, visiting)]
     rows[pl.ds(0, half), :] = own[:, pl.ds(0, width)]
     rows[pl.ds(half, half), :] = visiting[:, pl.ds(0, width)]
@@ -152,13 +153,11 @@
         copies[u][0].wait()
         pre = jnp.dot(rows[...], gate_up[u], preferred_element_type=F32)
         gate, up = pre[:, :units], pre[:, units:]
-        hidden[u] = (gate * jax.nn.sigmoid(gate) * up).astype(BF)
+        hidden[:, pl.ds(u * units, units)] = (gate * jax.nn.sigmoid(gate) * up).astype(BF)
     for u in range(4):
         copies[u][1].wait()
     for q, within, at in column_chunks(width):
-        total = jnp.dot(hidden[0], down[0, :, at], preferred_element_type=F32)
-        for u in range(1, 4):
-            total = total + jnp.dot(hidden[u], down[u, :, at], preferred_element_type=F32)
+        total = jnp.dot(hidden[...], down[:, at], preferred_element_type=F32)
         out_own[q, :, within] = own[:, at].astype(F32) + gates[0] * total[:half]
         out_visiting[q, :, within] = (gates[1] * total[half:]).astype(BF)
 
@@ -166,11 +165,11 @@
 def backward_kernel(own, visiting, saved, *refs):
     weights, (out_own, out_visiting, rows, gate_up, down, grads, sems) = refs[:8], refs[8:]
     copies = list(load_weights(weights, gate_up, down, sems))
-    for pair in copies:
-        pair[1].start()
-        pair[0].start()
+    for kind in (1, 0):
+        for pair in copies:
+            pair[kind].start()
     half, width = own.shape[0], rows.shape[1]
-    units = down.shape[1]
+    units = down.shape[0] // 4
     for at_row, ref in ((0, own), (half, visiting)):
         gate = ref[:, pl.ds(width, GATE_COLUMNS)].astype(F32)[:, :1]
         for start in range(0, width, COLUMNS):
@@ -178,7 +177,9 @@
             rows[pl.ds(at_row, half), at] = (gate * ref[:, at].astype(F32)).astype(BF)
     for u in range(4):
         copies[u][1].wait()
-        grad = lax.dot_general(rows[...], down[u], ROWS_T, preferred_element_type=F32)
+    hidden_grad = lax.dot_general(rows[...], down[...], ROWS_T, preferred_element_type=F32)
+    for u in range(4):
+        grad = hidden_grad[:, u * units : (u + 1) * units]
         a, b = saved[u, 0].astype(F32), saved[u, 1].astype(F32)
         sig = jax.nn.sigmoid(a)
         grads[u, :, pl.ds(0, units)] = (grad * b * sig * (1.0 + a * (1.0 - sig))).astype(BF)
@@ -208,8 +209,8 @@
         scratch_shapes=[
             pltpu.VMEM((rows, width), BF),
             pltpu.VMEM((4, width, 2 * units), BF),
-            pltpu.VMEM((4, units, width), BF),
-            pltpu.VMEM((4, rows, middle), BF),
+            pltpu.VMEM((4 * units, width), BF),
+            pltpu.VMEM(middle, BF),
             pltpu.SemaphoreType.DMA((8,)),
         ],
         compiler_params=pltpu.CompilerParams(vmem_limit_bytes=40 * 1024 * 1024),
@@ -265,9 +266,12 @@
 
     f_rows = arrived[:, :capacity].reshape(nz * capacity, -1)
     b_rows = arrived[:, capacity:].reshape(nz * capacity, -1)
-    f_own, f_visited = expert_pass(forward_kernel, f_rows, swap_rows(f_rows), (), weights, units)
     b_own, b_visited = expert_pass(
-        backward_kernel, b_rows, swap_rows(b_rows), (kept,), weights, 2 * units
+        backward_kernel, b_rows, swap_rows(b_rows), (kept,), weights, (4, 2 * nz * capacity, 2 * units)
+    )
+    b_own, f_visiting = lax.optimization_barrier((b_own, swap_rows(f_rows)))
+    f_own, f_visited = expert_pass(
+        forward_kernel, f_rows, f_visiting, (), weights, (2 * nz * capacity, 4 * units)
     )
     f_out = (f_own + swap_rows(f_visited).astype(F32)).astype(BF)
     b_out = (b_own + swap_rows(b_visited).astype(F32)).astype(BF)

time: 207 us -> 206 us (level)
    all_to_all x1, starting transfers between devices: 5.03 us -> 7.42 us  [go_home(): lax.all_to_all(jnp.concatenate(blocks), ('y', 'z'), split_axis=0, concat_...]
  transfers between devices with their start and end apart: 20 -> 20, of which waited for: 12 -> 13; matrix products, arithmetic and copies ran while one was open for 2% -> 2% of each run, Pallas kernels for 6% -> 5%
where the time goes in v7:
time: 206 us; the launch traced here: 202 us
  waiting for transfers between devices  91 us (44%)
  starting transfers between devices  86.7 us (42%)
  Pallas kernels  15.9 us (8%)
  local copies, waits for them, and re-layouts  4.98 us (2%)
  other arithmetic  2.81 us (1%)
    ppermute x16, waiting for transfers between devices, permute(): return lax.ppermute(block, axis, list(enumerate(targets)))  66.3 us
    ppermute x16, starting transfers between devices, permute(): return lax.ppermute(block, axis, list(enumerate(targets)))  56.5 us
    all_to_all x1, waiting for transfers between devices, go_home(): lax.all_to_all(jnp.concatenate(blocks), ('y', 'z'), split_axis=0, concat_...  19.2 us
    all_to_all x1, starting transfers between devices, exchange(): return lax.all_to_all(block, 'z', split_axis=0, concat_axis=0, tiled=True)  12.5 us
    pallas_call x2, Pallas kernels, expert_pass(): pl.pallas_call(kernel, out_shape=(jax.ShapeDtypeStruct(quarters, F32), ja...  10.4 us
    all_to_all x2, starting transfers between devices, spread(): lax.all_to_all(quarters, 'y', split_axis=0, concat_axis=0, tiled=True)  10.2 us
    all_to_all x1, starting transfers between devices, go_home(): lax.all_to_all(jnp.concatenate(blocks), ('y', 'z'), split_axis=0, concat_...  7.42 us
    all_to_all x1, waiting for transfers between devices, exchange(): return lax.all_to_all(block, 'z', split_axis=0, concat_axis=0, tiled=True)  4.47 us
  transfers between devices with their start and end apart: 20, of which 13 were waited for; matrix products, arithmetic and copies ran while one was open for 2% of the time, Pallas kernels for 5%

profile of v7, /device:TPU:24, one launch (start us, length us, event | category | flops | bytes accessed | tf_op | source)
XLA Modules:
  0.0 202.3 jit_solution(15183141062036848260)
XLA Ops:
  0.6 2.9 %shard_map.113 = bf16[128,3712]{1,0:T(8,128)(2,1)} custom-call(s32[1,64]{1,0:T(1,128)} %bitcast.76, s32[1,64]{1,0:T(1,128)} %bitcast.78, bf16[1,64]{1,0:T(2,128)(2,1)} %bitcast.74, bf16[1,64]{1,0:T(2,128)(2,1)} %bitcast.75, bf16[64,3584]{1,0:T(8,128)(2,1)} %bitcast.66, bf16[64,3584]{1,0:T(8,128)(2,1)} %bitcast.67), custom_call_target="tpu_custom_call" | custom-call | flops 117440512 | bytes 1835008 | tf_op jit(solution)/shard_map/pallas_call | solution.py:72
  3.5 12.5 %all-to-all-start = ((bf16[8,16,3712]{2,1,0:T(8,128)(2,1)}), bf16[8,16,3712]{2,1,0:T(8,128)(2,1)}, u32[]{:S(2)}, u32[]{:S(2)}) async-start(bf16[8,16,3712]{2,1,0:T(8,128)(2,1)} %bitcast.61), calls=%async_computation | async-start | bytes 1900544 | tf_op jit(solution)/shard_map/all_to_all | solution.py:35
  17.8 3.4 %collective-permute-start.7 = (bf16[3584,256]{1,0:T(8,128)(2,1)S(1)}, bf16[3584,256]{1,0:T(8,128)(2,1)}, u32[]{:S(2)}, u32[]{:S(2)}) collective-permute-start(bf16[3584,256]{1,0:T(8,128)(2,1)S(1)} %constant_dynamic-update-slice_fusion.refs_0_), channel_id=1, source_target_pairs={{0,2},{1,7},{2,0},{3,5},{4,6},{5,3},{6,4},{7,1},{8,10},{9,15},{10,... | collective-permute-start | bytes 5505032 | tf_op jit(solution)/shard_map/ppermute | solution.py:18
  21.2 2.5 %collective-permute-start.2 = (bf16[3584,256]{1,0:T(8,128)(2,1)S(1)}, bf16[3584,256]{1,0:T(8,128)(2,1)}, u32[]{:S(2)}, u32[]{:S(2)}) collective-permute-start(bf16[3584,256]{1,0:T(8,128)(2,1)S(1)} %constant_dynamic-update-slice_fusion.refs_0_), channel_id=1, source_target_pairs={{0,1},{1,0},{2,3},{3,2},{4,5},{5,4},{6,7},{7,6},{8,9},{9,8},{10,11... | collective-permute-start | bytes 5505032 | tf_op jit(solution)/shard_map/ppermute | solution.py:18
  23.7 1.9 collective-permute-start.3
  25.6 2.4 %collective-permute-start.9 = (bf16[128,3584]{1,0:T(8,128)(2,1)S(1)}, bf16[128,3584]{1,0:T(8,128)(2,1)}, u32[]{:S(2)}, u32[]{:S(2)}) collective-permute-start(bf16[128,3584]{1,0:T(8,128)(2,1)S(1)} %bitcast.57), channel_id=1, source_target_pairs={{0,2},{1,7},{2,0},{3,5},{4,6},{5,3},{6,4},{7,1},{8,10},{9,15},{10,... | collective-permute-start | bytes 2752520 | tf_op jit(solution)/shard_map/ppermute | solution.py:18
  28.6 3.0 %collective-permute-start.4 = (bf16[2,2,8,2,8,128]{5,4,3,2,0,1:T(8,128)(2,1)S(1)}, bf16[2,2,8,2,8,128]{5,4,3,2,0,1:T(8,128)(2,1)S(1)}, u32[]{:S(2)}, u32[]{:S(2)}) collective-permute-start(bf16[2,2,8,2,8,128]{5,4,3,2,0,1:T(8,128)(2,1)S(1)} %pad_maximum_fusion.1), channel_id=1, source_target_pairs={{0,2},{1,7},{2,0},{3,5},{4,6},{5,3},{6,4},{7,1},{8,10},{9,15},{10,... | collective-permute-start | bytes 393224 | tf_op jit(solution)/shard_map/ppermute | solution.py:18
  31.6 11.4 %collective-permute-done.7.refs_2_ = bf16[3584,256]{1,0:T(8,128)(2,1)} collective-permute-done((bf16[3584,256]{1,0:T(8,128)(2,1)S(1)}, bf16[3584,256]{1,0:T(8,128)(2,1)}, u32[]{:S(2)}, u32[]{:S(2)}) %collective-permute-start.7) | collective-permute-done | bytes 1835040 | tf_op jit(solution)/shard_map/ppermute | solution.py:18
  45.0 9.2 %collective-permute-done.4 = bf16[2,2,8,2,8,128]{5,4,3,2,0,1:T(8,128)(2,1)S(1)} collective-permute-done((bf16[2,2,8,2,8,128]{5,4,3,2,0,1:T(8,128)(2,1)S(1)}, bf16[2,2,8,2,8,128]{5,4,3,2,0,1:T(8,128)(2,1)S(1)}, u32[]{:S(2)}, u32[]{:S(2)}) %collective-permute-start.4) | collective-permute-done | bytes 131104 | tf_op jit(solution)/shard_map/ppermute | solution.py:18
  54.2 1.9 collective-permute-start.5
  56.2 2.4 %collective-permute-start.10 = (bf16[128,3584]{1,0:T(8,128)(2,1)}, bf16[128,3584]{1,0:T(8,128)(2,1)}, u32[]{:S(2)}, u32[]{:S(2)}) collective-permute-start(bf16[128,3584]{1,0:T(8,128)(2,1)} %collective-permute-done.9.refs_6_), channel_id=1, source_target_pairs={{0,1},{1,0},{2,3},{3,2},{4,5},{5,4},{6,7},{7,6},{8,9},{9,8},{10,11... | collective-permute-start | bytes 2752520 | tf_op jit(solution)/shard_map/ppermute | solution.py:18
  58.7 4.5 %all-to-all-done = bf16[8,16,3712]{2,1,0:T(8,128)(2,1)} async-done(((bf16[8,16,3712]{2,1,0:T(8,128)(2,1)}), bf16[8,16,3712]{2,1,0:T(8,128)(2,1)}, u32[]{:S(2)}, u32[]{:S(2)}) %all-to-all-start) | async-done | bytes 950304 | tf_op jit(solution)/shard_map/all_to_all | solution.py:35
  64.4 4.9 %collective-permute-start.6 = (bf16[64,3712]{1,0:T(8,128)(2,1)S(1)}, bf16[64,3712]{1,0:T(8,128)(2,1)S(1)}, u32[]{:S(2)}, u32[]{:S(2)}) collective-permute-start(bf16[64,3712]{1,0:T(8,128)(2,1)S(1)} %get-tuple-element.35.own), channel_id=1, source_target_pairs={{0,4},{2,6},{4,0},{6,2},{1,5},{3,7},{5,1},{7,3},{8,12},{10,14},{12... | collective-permute-start | bytes 1425416 | tf_op jit(solution)/shard_map/ppermute | solution.py:18
  69.3 2.4 %collective-permute-start.11 = (bf16[64,3712]{1,0:T(8,128)(2,1)S(1)}, bf16[64,3712]{1,0:T(8,128)(2,1)S(1)}, u32[]{:S(2)}, u32[]{:S(2)}) collective-permute-start(bf16[64,3712]{1,0:T(8,128)(2,1)S(1)} %get-tuple-element.34.own), channel_id=1, source_target_pairs={{0,4},{2,6},{4,0},{6,2},{1,5},{3,7},{5,1},{7,3},{8,12},{10,14},{12... | collective-permute-start | bytes 1425416 | tf_op jit(solution)/shard_map/ppermute | solution.py:18
  71.8 9.8 %collective-permute-done.6.visiting = bf16[64,3712]{1,0:T(8,128)(2,1)S(1)} collective-permute-done((bf16[64,3712]{1,0:T(8,128)(2,1)S(1)}, bf16[64,3712]{1,0:T(8,128)(2,1)S(1)}, u32[]{:S(2)}, u32[]{:S(2)}) %collective-permute-start.6) | collective-permute-done | bytes 475168 | tf_op jit(solution)/shard_map/ppermute | solution.py:18
  81.6 6.1 %shard_map.114 = (f32[4,64,896]{2,1,0:T(8,128)S(1)}, bf16[4,64,896]{2,1,0:T(8,128)(2,1)S(1)}) custom-call(bf16[64,3712]{1,0:T(8,128)(2,1)S(1)} %get-tuple-element.35.own, bf16[64,3712]{1,0:T(8,128)(2,1)S(1)} %collective-permute-done.6.visiting, bf16[4,2,128,128]{3,2,1,0:T(8,128)(2,1)S(1)} %bitcast.60, ...), custom_call_target="tpu_custom_call" | custom-call | flops 1409286144 | bytes 13303808 | tf_op jit(solution)/shard_map/pallas_call | solution.py:204
  87.7 4.9 %collective-permute-start.14 = (bf16[4,64,896]{2,1,0:T(8,128)(2,1)S(1)}, bf16[4,64,896]{2,1,0:T(8,128)(2,1)S(1)}, u32[]{:S(2)}, u32[]{:S(2)}) collective-permute-start(bf16[4,64,896]{2,1,0:T(8,128)(2,1)S(1)} %get-tuple-element.31), channel_id=1, source_target_pairs={{0,4},{2,6},{4,0},{6,2},{1,5},{3,7},{5,1},{7,3},{8,12},{10,14},{12... | collective-permute-start | bytes 1376264 | tf_op jit(solution)/shard_map/ppermute | solution.py:18
  92.6 4.3 %shard_map.115 = (f32[4,64,896]{2,1,0:T(8,128)S(1)}, bf16[4,64,896]{2,1,0:T(8,128)(2,1)S(1)}) custom-call(bf16[64,3712]{1,0:T(8,128)(2,1)S(1)} %get-tuple-element.34.own, bf16[64,3712]{1,0:T(8,128)(2,1)S(1)} %collective-permute-done.11.visiting, bf16[3584,256]{1,0:T(8,128)(2,1)S(1)} %constant_dynamic-update-slice_fusion.refs_0_, ...), custom_call_target="tpu_custom_call" | custom-call | flops 1409286144 | bytes 13303808 | tf_op jit(solution)/shard_map/pallas_call | solution.py:204
  97.9 2.5 %collective-permute-start.12 = (bf16[4,64,896]{2,1,0:T(8,128)(2,1)S(1)}, bf16[4,64,896]{2,1,0:T(8,128)(2,1)S(1)}, u32[]{:S(2)}, u32[]{:S(2)}) collective-permute-start(bf16[4,64,896]{2,1,0:T(8,128)(2,1)S(1)} %get-tuple-element.29), channel_id=1, source_target_pairs={{0,4},{2,6},{4,0},{6,2},{1,5},{3,7},{5,1},{7,3},{8,12},{10,14},{12... | collective-permute-start | bytes 1376264 | tf_op jit(solution)/shard_map/ppermute | solution.py:18
  101.5 4.7 %all-to-all-start.2 = ((bf16[4,64,896]{2,1,0:T(8,128)(2,1)}), bf16[4,64,896]{2,1,0:T(8,128)(2,1)S(1)}, u32[]{:S(2)}, u32[]{:S(2)}) async-start(bf16[4,64,896]{2,1,0:T(8,128)(2,1)} %add_convert_fusion), calls=%async_computation.2 | async-start | bytes 917504 | tf_op jit(solution)/shard_map/all_to_all | solution.py:110
  106.1 3.8 %collective-permute-done.12 = bf16[4,64,896]{2,1,0:T(8,128)(2,1)S(1)} collective-permute-done((bf16[4,64,896]{2,1,0:T(8,128)(2,1)S(1)}, bf16[4,64,896]{2,1,0:T(8,128)(2,1)S(1)}, u32[]{:S(2)}, u32[]{:S(2)}) %collective-permute-start.12) | collective-permute-done | bytes 458784 | tf_op jit(solution)/shard_map/ppermute | solution.py:18
  111.8 5.5 %all-to-all-start.1 = ((bf16[4,64,896]{2,1,0:T(8,128)(2,1)}), bf16[4,64,896]{2,1,0:T(8,128)(2,1)S(1)}, u32[]{:S(2)}, u32[]{:S(2)}) async-start(bf16[4,64,896]{2,1,0:T(8,128)(2,1)} %add_convert_fusion.1), calls=%async_computation.1 | async-start | bytes 917504 | tf_op jit(solution)/shard_map/all_to_all | solution.py:110
  117.4 8.2 %collective-permute-start.15 = (bf16[64,896]{1,0:T(8,128)(2,1)S(1)}, bf16[64,896]{1,0:T(8,128)(2,1)S(1)}, u32[]{:S(2)}, u32[]{:S(2)}) collective-permute-start(bf16[64,896]{1,0:T(8,128)(2,1)S(1)} %get-tuple-element.41), channel_id=1, source_target_pairs={{0,256},{256,0},{1,257},{257,1},{2,258},{258,2},{3,259},{259,3},{4... | collective-permute-start | bytes 344072 | tf_op jit(solution)/shard_map/ppermute | solution.py:18
  125.6 6.3 %collective-permute-start.13 = (bf16[64,896]{1,0:T(8,128)(2,1)S(1)}, bf16[64,896]{1,0:T(8,128)(2,1)S(1)}, u32[]{:S(2)}, u32[]{:S(2)}) collective-permute-start(bf16[64,896]{1,0:T(8,128)(2,1)S(1)} %get-tuple-element.36), channel_id=1, source_target_pairs={{0,256},{256,0},{1,257},{257,1},{2,258},{258,2},{3,259},{259,3},{4... | collective-permute-start | bytes 344072 | tf_op jit(solution)/shard_map/ppermute | solution.py:18
  132.0 9.9 %collective-permute-done.15 = bf16[64,896]{1,0:T(8,128)(2,1)S(1)} collective-permute-done((bf16[64,896]{1,0:T(8,128)(2,1)S(1)}, bf16[64,896]{1,0:T(8,128)(2,1)S(1)}, u32[]{:S(2)}, u32[]{:S(2)}) %collective-permute-start.15) | collective-permute-done | bytes 114720 | tf_op jit(solution)/shard_map/ppermute | solution.py:18
  141.9 7.2 %collective-permute-done.13 = bf16[64,896]{1,0:T(8,128)(2,1)S(1)} collective-permute-done((bf16[64,896]{1,0:T(8,128)(2,1)S(1)}, bf16[64,896]{1,0:T(8,128)(2,1)S(1)}, u32[]{:S(2)}, u32[]{:S(2)}) %collective-permute-start.13) | collective-permute-done | bytes 114720 | tf_op jit(solution)/shard_map/ppermute | solution.py:18
  150.1 7.4 %all-to-all-start.3 = ((bf16[32,16,896]{2,1,0:T(8,128)(2,1)}), bf16[32,16,896]{2,1,0:T(8,128)(2,1)S(1)}, u32[]{:S(2)}, u32[]{:S(2)}) async-start(bf16[32,16,896]{2,1,0:T(8,128)(2,1)} %maximum_maximum_fusion), calls=%async_computation.3 | async-start | bytes 1835008 | tf_op jit(solution)/shard_map/all_to_all | solution.py:118
  157.6 5.8 %collective-permute-start = (s32[1,64]{1,0:T(1,128)S(1)}, s32[1,64]{1,0:T(1,128)S(1)}, u32[]{:S(2)}, u32[]{:S(2)}) collective-permute-start(s32[1,64]{1,0:T(1,128)S(1)} %bitcast.77), channel_id=1, source_target_pairs={{0,64},{64,128},{128,192},{192,256},{256,320},{320,384},{384,448},... | collective-permute-start | bytes 776 | tf_op jit(solution)/shard_map/ppermute | solution.py:18
  165.3 6.9 %collective-permute-done.f_routes = s32[1,64]{1,0:T(1,128)S(1)} collective-permute-done((s32[1,64]{1,0:T(1,128)S(1)}, s32[1,64]{1,0:T(1,128)S(1)}, u32[]{:S(2)}, u32[]{:S(2)}) %collective-permute-start) | collective-permute-done | bytes 288 | tf_op jit(solution)/shard_map/ppermute | solution.py:18
  172.2 7.4 %collective-permute-done.1.b_routes = s32[1,64]{1,0:T(1,128)S(1)} collective-permute-done((s32[1,64]{1,0:T(1,128)S(1)}, s32[1,64]{1,0:T(1,128)S(1)}, u32[]{:S(2)}, u32[]{:S(2)}) %collective-permute-start.1) | collective-permute-done | bytes 288 | tf_op jit(solution)/shard_map/ppermute | solution.py:18
  179.6 19.2 %all-to-all-done.3 = bf16[32,16,896]{2,1,0:T(8,128)(2,1)S(1)} async-done(((bf16[32,16,896]{2,1,0:T(8,128)(2,1)}), bf16[32,16,896]{2,1,0:T(8,128)(2,1)S(1)}, u32[]{:S(2)}, u32[]{:S(2)}) %all-to-all-start.3) | async-done | bytes 917536 | tf_op jit(solution)/shard_map/all_to_all | solution.py:118
  199.8 2.6 %shard_map.116 = (bf16[64,3584]{1,0:T(8,128)(2,1)}, bf16[64,3584]{1,0:T(8,128)(2,1)}) custom-call(s32[1,64]{1,0:T(1,128)} %copy-done.8, s32[1,64]{1,0:T(1,128)} %copy-done.9, bf16[4,128,896]{2,1,0:T(8,128)(2,1)} %bitcast.62), custom_call_target="tpu_custom_call" | custom-call | flops 117440512 | bytes 1835008 | tf_op jit(solution)/shard_map/pallas_call | solution.py:96
  (48 shorter events, 13.3 us)
Async XLA Ops:
  3.5 59.6 %all-to-all-start = ((bf16[8,16,3712]{2,1,0:T(8,128)(2,1)}), bf16[8,16,3712]{2,1,0:T(8,128)(2,1)}, u32[]{:S(2)}, u32[]{:S(2)}) async-start(bf16[8,16,3712]{2,1,0:T(8,128)(2,1)} %bitcast.61), calls=%async_computation | async-start | bytes 1900544 | tf_op jit(solution)/shard_map/all_to_all | solution.py:35
  16.1 1.5 copy-start.4
  16.1 7.6 %copy-start = (bf16[1,128,3584]{2,1,0:T(8,128)(2,1)S(1)}, bf16[1,128,3584]{2,1,0:T(8,128)(2,1)}, u32[]{:S(2)}) copy-start(bf16[1,128,3584]{2,1,0:T(8,128)(2,1)} %param.19) | copy-start | bytes 2752516
  16.1 12.4 %copy-start.5 = (bf16[1,2,64,8,128]{4,3,2,1,0:T(8,128)(2,1)S(1)}, bf16[1,2,64,8,128]{4,3,2,1,0:T(8,128)(2,1)}, u32[]{:S(2)}) copy-start(bf16[1,2,64,8,128]{4,3,2,1,0:T(8,128)(2,1)} %param.16) | copy-start | bytes 786436
  17.8 25.2 %collective-permute-start.7 = (bf16[3584,256]{1,0:T(8,128)(2,1)S(1)}, bf16[3584,256]{1,0:T(8,128)(2,1)}, u32[]{:S(2)}, u32[]{:S(2)}) collective-permute-start(bf16[3584,256]{1,0:T(8,128)(2,1)S(1)} %constant_dynamic-update-slice_fusion.refs_0_), channel_id=1, source_target_pairs={{0,2},{1,7},{2,0},{3,5},{4,6},{5,3},{6,4},{7,1},{8,10},{9,15},{10,... | collective-permute-start | bytes 5505032 | tf_op jit(solution)/shard_map/ppermute | solution.py:18
  21.2 37.5 %collective-permute-start.2 = (bf16[3584,256]{1,0:T(8,128)(2,1)S(1)}, bf16[3584,256]{1,0:T(8,128)(2,1)}, u32[]{:S(2)}, u32[]{:S(2)}) collective-permute-start(bf16[3584,256]{1,0:T(8,128)(2,1)S(1)} %constant_dynamic-update-slice_fusion.refs_0_), channel_id=1, source_target_pairs={{0,1},{1,0},{2,3},{3,2},{4,5},{5,4},{6,7},{7,6},{8,9},{9,8},{10,11... | collective-permute-start | bytes 5505032 | tf_op jit(solution)/shard_map/ppermute | solution.py:18
  23.7 4.8 %collective-permute-start.3 = (bf16[128,3584]{1,0:T(8,128)(2,1)S(1)}, bf16[128,3584]{1,0:T(8,128)(2,1)}, u32[]{:S(2)}, u32[]{:S(2)}) collective-permute-start(bf16[128,3584]{1,0:T(8,128)(2,1)S(1)} %bitcast.56), channel_id=1, source_target_pairs={{0,1},{1,0},{2,3},{3,2},{4,5},{5,4},{6,7},{7,6},{8,9},{9,8},{10,11... | collective-permute-start | bytes 2752520 | tf_op jit(solution)/shard_map/ppermute | solution.py:18
  25.6 30.5 %collective-permute-start.9 = (bf16[128,3584]{1,0:T(8,128)(2,1)S(1)}, bf16[128,3584]{1,0:T(8,128)(2,1)}, u32[]{:S(2)}, u32[]{:S(2)}) collective-permute-start(bf16[128,3584]{1,0:T(8,128)(2,1)S(1)} %bitcast.57), channel_id=1, source_target_pairs={{0,2},{1,7},{2,0},{3,5},{4,6},{5,3},{6,4},{7,1},{8,10},{9,15},{10,... | collective-permute-start | bytes 2752520 | tf_op jit(solution)/shard_map/ppermute | solution.py:18
  28.6 25.6 %collective-permute-start.4 = (bf16[2,2,8,2,8,128]{5,4,3,2,0,1:T(8,128)(2,1)S(1)}, bf16[2,2,8,2,8,128]{5,4,3,2,0,1:T(8,128)(2,1)S(1)}, u32[]{:S(2)}, u32[]{:S(2)}) collective-permute-start(bf16[2,2,8,2,8,128]{5,4,3,2,0,1:T(8,128)(2,1)S(1)} %pad_maximum_fusion.1), channel_id=1, source_target_pairs={{0,2},{1,7},{2,0},{3,5},{4,6},{5,3},{6,4},{7,1},{8,10},{9,15},{10,... | collective-permute-start | bytes 393224 | tf_op jit(solution)/shard_map/ppermute | solution.py:18
  43.0 28.7 %collective-permute-start.8 = (bf16[3584,256]{1,0:T(8,128)(2,1)}, bf16[3584,256]{1,0:T(8,128)(2,1)}, u32[]{:S(2)}, u32[]{:S(2)}) collective-permute-start(bf16[3584,256]{1,0:T(8,128)(2,1)} %collective-permute-done.7.refs_2_), channel_id=1, source_target_pairs={{0,1},{1,0},{2,3},{3,2},{4,5},{5,4},{6,7},{7,6},{8,9},{9,8},{10,11... | collective-permute-start | bytes 5505032 | tf_op jit(solution)/shard_map/ppermute | solution.py:18
  54.2 4.4 %collective-permute-start.5 = (bf16[2,2,2,8,8,128]{5,4,3,2,1,0:T(8,128)(2,1)S(1)}, bf16[2,2,2,8,8,128]{5,4,3,2,1,0:T(8,128)(2,1)S(1)}, u32[]{:S(2)}, u32[]{:S(2)}) collective-permute-start(bf16[2,2,2,8,8,128]{5,4,3,2,1,0:T(8,128)(2,1)S(1)} %bitcast.69), channel_id=1, source_target_pairs={{0,1},{1,0},{2,3},{3,2},{4,5},{5,4},{6,7},{7,6},{8,9},{9,8},{10,11... | collective-permute-start | bytes 393224 | tf_op jit(solution)/shard_map/ppermute | solution.py:18
  56.2 15.6 %collective-permute-start.10 = (bf16[128,3584]{1,0:T(8,128)(2,1)}, bf16[128,3584]{1,0:T(8,128)(2,1)}, u32[]{:S(2)}, u32[]{:S(2)}) collective-permute-start(bf16[128,3584]{1,0:T(8,128)(2,1)} %collective-permute-done.9.refs_6_), channel_id=1, source_target_pairs={{0,1},{1,0},{2,3},{3,2},{4,5},{5,4},{6,7},{7,6},{8,9},{9,8},{10,11... | collective-permute-start | bytes 2752520 | tf_op jit(solution)/shard_map/ppermute | solution.py:18
  64.4 17.2 %collective-permute-start.6 = (bf16[64,3712]{1,0:T(8,128)(2,1)S(1)}, bf16[64,3712]{1,0:T(8,128)(2,1)S(1)}, u32[]{:S(2)}, u32[]{:S(2)}) collective-permute-start(bf16[64,3712]{1,0:T(8,128)(2,1)S(1)} %get-tuple-element.35.own), channel_id=1, source_target_pairs={{0,4},{2,6},{4,0},{6,2},{1,5},{3,7},{5,1},{7,3},{8,12},{10,14},{12... | collective-permute-start | bytes 1425416 | tf_op jit(solution)/shard_map/ppermute | solution.py:18
  69.3 23.3 %collective-permute-start.11 = (bf16[64,3712]{1,0:T(8,128)(2,1)S(1)}, bf16[64,3712]{1,0:T(8,128)(2,1)S(1)}, u32[]{:S(2)}, u32[]{:S(2)}) collective-permute-start(bf16[64,3712]{1,0:T(8,128)(2,1)S(1)} %get-tuple-element.34.own), channel_id=1, source_target_pairs={{0,4},{2,6},{4,0},{6,2},{1,5},{3,7},{5,1},{7,3},{8,12},{10,14},{12... | collective-permute-start | bytes 1425416 | tf_op jit(solution)/shard_map/ppermute | solution.py:18
  87.7 12.9 %collective-permute-start.14 = (bf16[4,64,896]{2,1,0:T(8,128)(2,1)S(1)}, bf16[4,64,896]{2,1,0:T(8,128)(2,1)S(1)}, u32[]{:S(2)}, u32[]{:S(2)}) collective-permute-start(bf16[4,64,896]{2,1,0:T(8,128)(2,1)S(1)} %get-tuple-element.31), channel_id=1, source_target_pairs={{0,4},{2,6},{4,0},{6,2},{1,5},{3,7},{5,1},{7,3},{8,12},{10,14},{12... | collective-permute-start | bytes 1376264 | tf_op jit(solution)/shard_map/ppermute | solution.py:18
  97.0 0.9 copy-start.1
  97.9 12.0 %copy-start.2 = (f32[4,64,896]{2,1,0:T(8,128)S(1)}, f32[4,64,896]{2,1,0:T(8,128)}, u32[]{:S(2)}) copy-start(f32[4,64,896]{2,1,0:T(8,128)} %copy-done.1) | copy-start | bytes 2752516
  97.9 12.0 %collective-permute-start.12 = (bf16[4,64,896]{2,1,0:T(8,128)(2,1)S(1)}, bf16[4,64,896]{2,1,0:T(8,128)(2,1)S(1)}, u32[]{:S(2)}, u32[]{:S(2)}) collective-permute-start(bf16[4,64,896]{2,1,0:T(8,128)(2,1)S(1)} %get-tuple-element.29), channel_id=1, source_target_pairs={{0,4},{2,6},{4,0},{6,2},{1,5},{3,7},{5,1},{7,3},{8,12},{10,14},{12... | collective-permute-start | bytes 1376264 | tf_op jit(solution)/shard_map/ppermute | solution.py:18
  101.5 10.3 %all-to-all-start.2 = ((bf16[4,64,896]{2,1,0:T(8,128)(2,1)}), bf16[4,64,896]{2,1,0:T(8,128)(2,1)S(1)}, u32[]{:S(2)}, u32[]{:S(2)}) async-start(bf16[4,64,896]{2,1,0:T(8,128)(2,1)} %add_convert_fusion), calls=%async_computation.2 | async-start | bytes 917504 | tf_op jit(solution)/shard_map/all_to_all | solution.py:110
  111.8 13.8 %all-to-all-start.1 = ((bf16[4,64,896]{2,1,0:T(8,128)(2,1)}), bf16[4,64,896]{2,1,0:T(8,128)(2,1)S(1)}, u32[]{:S(2)}, u32[]{:S(2)}) async-start(bf16[4,64,896]{2,1,0:T(8,128)(2,1)} %add_convert_fusion.1), calls=%async_computation.1 | async-start | bytes 917504 | tf_op jit(solution)/shard_map/all_to_all | solution.py:110
  117.4 24.5 %collective-permute-start.15 = (bf16[64,896]{1,0:T(8,128)(2,1)S(1)}, bf16[64,896]{1,0:T(8,128)(2,1)S(1)}, u32[]{:S(2)}, u32[]{:S(2)}) collective-permute-start(bf16[64,896]{1,0:T(8,128)(2,1)S(1)} %get-tuple-element.41), channel_id=1, source_target_pairs={{0,256},{256,0},{1,257},{257,1},{2,258},{258,2},{3,259},{259,3},{4... | collective-permute-start | bytes 344072 | tf_op jit(solution)/shard_map/ppermute | solution.py:18
  125.6 23.5 %collective-permute-start.13 = (bf16[64,896]{1,0:T(8,128)(2,1)S(1)}, bf16[64,896]{1,0:T(8,128)(2,1)S(1)}, u32[]{:S(2)}, u32[]{:S(2)}) collective-permute-start(bf16[64,896]{1,0:T(8,128)(2,1)S(1)} %get-tuple-element.36), channel_id=1, source_target_pairs={{0,256},{256,0},{1,257},{257,1},{2,258},{258,2},{3,259},{259,3},{4... | collective-permute-start | bytes 344072 | tf_op jit(solution)/shard_map/ppermute | solution.py:18
  149.1 8.4 %copy-start.6 = (s32[1,64,1]{1,2,0:T(1,128)S(1)}, s32[1,64,1]{1,2,0:T(1,128)}, u32[]{:S(2)}) copy-start(s32[1,64,1]{1,2,0:T(1,128)} %param.12) | copy-start | bytes 772
  149.1 14.3 %copy-start.7 = (s32[1,64,1]{1,2,0:T(1,128)S(1)}, s32[1,64,1]{1,2,0:T(1,128)}, u32[]{:S(2)}) copy-start(s32[1,64,1]{1,2,0:T(1,128)} %param.14) | copy-start | bytes 772
  150.1 48.7 %all-to-all-start.3 = ((bf16[32,16,896]{2,1,0:T(8,128)(2,1)}), bf16[32,16,896]{2,1,0:T(8,128)(2,1)S(1)}, u32[]{:S(2)}, u32[]{:S(2)}) async-start(bf16[32,16,896]{2,1,0:T(8,128)(2,1)} %maximum_maximum_fusion), calls=%async_computation.3 | async-start | bytes 1835008 | tf_op jit(solution)/shard_map/all_to_all | solution.py:118
  157.6 14.6 %collective-permute-start = (s32[1,64]{1,0:T(1,128)S(1)}, s32[1,64]{1,0:T(1,128)S(1)}, u32[]{:S(2)}, u32[]{:S(2)}) collective-permute-start(s32[1,64]{1,0:T(1,128)S(1)} %bitcast.77), channel_id=1, source_target_pairs={{0,64},{64,128},{128,192},{192,256},{256,320},{320,384},{384,448},... | collective-permute-start | bytes 776 | tf_op jit(solution)/shard_map/ppermute | solution.py:18
  163.4 16.3 %collective-permute-start.1 = (s32[1,64]{1,0:T(1,128)S(1)}, s32[1,64]{1,0:T(1,128)S(1)}, u32[]{:S(2)}, u32[]{:S(2)}) collective-permute-start(s32[1,64]{1,0:T(1,128)S(1)} %bitcast.79), channel_id=1, source_target_pairs={{0,448},{64,0},{128,64},{192,128},{256,192},{320,256},{384,320},{4... | collective-permute-start | bytes 776 | tf_op jit(solution)/shard_map/ppermute | solution.py:18
  172.2 26.7 %copy-start.8 = (s32[1,64]{1,0:T(1,128)}, s32[1,64]{1,0:T(1,128)S(1)}, u32[]{:S(2)}) copy-start(s32[1,64]{1,0:T(1,128)S(1)} %collective-permute-done.f_routes) | copy-start | bytes 772
  179.6 19.2 %copy-start.9 = (s32[1,64]{1,0:T(1,128)}, s32[1,64]{1,0:T(1,128)S(1)}, u32[]{:S(2)}) copy-start(s32[1,64]{1,0:T(1,128)S(1)} %collective-permute-done.1.b_routes) | copy-start | bytes 772
  198.8 0.9 copy-start.3
